TPU v7x, 32 devices: a whole 2x2x4 slice. The times are simulated.
32 devices in a mesh: seq: 4 (over y, core), fsdp: 8 (over z, x).
Axes of the slice: x: 2, y: 2, z: 4, core: 2. Of those that a mesh axis runs over, the one named last changes fastest.
Arguments:
- tokens: bfloat16 [8, 2, 1024, 2048], P('fsdp', None, 'seq'), may hold values from -6 to 6
- cotangent: bfloat16 [8, 2, 1024, 2048], P('fsdp', None, 'seq'), may hold values from -6 to 6
- w_qkv: bfloat16 [2048, 6144], P('fsdp'), may hold values from -0.125 to 0.125
- w_out: bfloat16 [2048, 2048], P('fsdp'), may hold values from -0.5 to 0.5
- w_gate_up: bfloat16 [2048, 16384], P('fsdp'), may hold values from -0.125 to 0.125
- w_down: bfloat16 [8192, 2048], P('fsdp'), may hold values from -0.0625 to 0.0625
- gain_attn: float32 [2048], replicated, may hold values from 0.5 to 1.5
- gain_ffn: float32 [2048], replicated, may hold values from 0.5 to 1.5
- gate_bias: float32 [16], replicated, may hold values from -1 to 3
- memory_in: float32 [8, 16, 128, 128], P('fsdp'), may hold values from -12300 to 12300
- norms_in: float32 [8, 16, 128], P('fsdp'), may hold values from 1 to 1025
- resets: int32 [8, 1], P('fsdp'), may hold values 0 or 1
- depth: int32 [8], P('fsdp'), may hold values from 1 to 2
Outputs:
- output: bfloat16 [8, 2, 1024, 2048], P('fsdp', None, 'seq')
- input_grad: bfloat16 [8, 2, 1024, 2048], P('fsdp', None, 'seq')
- grad_qkv: float32 [2048, 6144], P('fsdp')
- grad_out: float32 [2048, 2048], P('fsdp')
- grad_gate_up: float32 [2048, 16384], P('fsdp')
- grad_down: float32 [8192, 2048], P('fsdp')
- grad_gain_attn: float32 [2048], replicated
- grad_gain_ffn: float32 [2048], replicated
- grad_gate_bias: float32 [16], replicated
All inputs are finite; a program needn't handle non-finite values. No bound on the sum of `resets` on one device may be relied on, other than what follows from the above.
Results may differ from a plain program's by a relative error of at most 0.022.
Values may be sent and summed in bfloat16 or wider, within the bound.
A program may use at most 576 MiB of HBM per device.

v0:
```python
import jax
import jax.numpy as jnp
from jax import lax
from jax.sharding import PartitionSpec as P

norm_eps = 1e-05


def rms(value_rows_segment):
    return value_rows_segment * lax.rsqrt(
        jnp.mean(value_rows_segment * value_rows_segment, axis=-1, keepdims=True) + norm_eps
    )


def feature(value_rows_segment):
    return jnp.where(
        value_rows_segment > 0,
        value_rows_segment + 1.0,
        jnp.exp(jnp.minimum(value_rows_segment, 0.0)),
    )


def swiglu(gate_part, up_part):
    return jax.nn.silu(gate_part) * up_part


def local_memory(query, key, value_rows_segment, memory_matrix_entry, normalizer_entry):
    hidden_previous = lax.Precision.HIGHEST
    feature_queries = feature(query)
    feature_keys = feature(key)
    attention_memory_mix = (
        jnp.einsum("zqi,qis->zqs", feature_queries, memory_matrix_entry, precision=hidden_previous)
        / jnp.einsum("rzo,zo->rz", feature_queries, normalizer_entry, precision=hidden_previous)[
            ..., None
        ]
    )
    memory_recall_read = (
        jnp.einsum("zqi,qis->zqs", feature_keys, memory_matrix_entry, precision=hidden_previous)
        / jnp.einsum("rzo,zo->rz", feature_keys, normalizer_entry, precision=hidden_previous)[
            ..., None
        ]
    )
    memory_delta_write = jnp.einsum(
        "ubf,ubc->bfc",
        feature_keys,
        value_rows_segment - memory_recall_read,
        precision=hidden_previous,
    )
    return (attention_memory_mix, memory_delta_write, jnp.sum(feature_keys, axis=0))


def fold_rows(left, weight):
    return jnp.dot(
        left, lax.all_gather(weight, "fsdp", axis=0, tiled=True), preferred_element_type=jnp.float32
    )


def spread_rows(grad, weight):
    return lax.dot_general(
        grad,
        lax.all_gather(weight, "fsdp", axis=0, tiled=True),
        (((1,), (1,)), ((), ())),
        preferred_element_type=jnp.float32,
    )


def reduce_rows(left, grad):
    return lax.psum_scatter(
        lax.dot_general(
            left, grad, (((0,), (0,)), ((), ())), preferred_element_type=jnp.float32
        ).astype(jnp.bfloat16),
        "fsdp",
        scatter_dimension=0,
        tiled=True,
    ).astype(jnp.float32)


def body(
    tokens,
    cotangent,
    w_qkv,
    w_out,
    w_gate_up,
    w_down,
    gain_attn,
    gain_ffn,
    gate_bias,
    memory_in,
    norms_in,
    resets,
    depth,
):
    seq_dev, segs, local, width = tokens.shape
    heads = gate_bias.shape[0]
    hdim = width // heads
    hidden_w = w_gate_up.shape[1] // 2
    rows = seq_dev * segs * local
    scale = 1.0 / hdim**0.5
    held = (w_qkv, w_out, w_gate_up, w_down)

    def project(left, which):
        return fold_rows(left, held[which])

    def project_back(grad, which):
        return spread_rows(grad, held[which])

    x_flat = tokens.reshape(rows, width).astype(jnp.float32)
    r_one = rms(x_flat)
    h_one = (r_one * gain_attn).astype(jnp.bfloat16)
    qkv = project(h_one, 0).astype(jnp.bfloat16).reshape(seq_dev, segs, local, 3, heads, hdim)
    q_places = lax.axis_index("seq") * local + jnp.arange(local, dtype=jnp.int32)
    k_places = jnp.arange(local * lax.axis_size("seq"), dtype=jnp.int32)
    allowed = (k_places[None, :] <= q_places[:, None])[None]
    gate = jax.nn.sigmoid(gate_bias)[None, :, None]
    saved = []
    mixes = []
    b = 0
    memory = memory_in[b]
    norms = norms_in[b]
    for s in range(segs):
        query = qkv[b, s, :, 0]
        keys_all, values_all = (
            lax.all_gather(qkv[b, s, :, 1], "seq", axis=0, tiled=True),
            lax.all_gather(qkv[b, s, :, 2], "seq", axis=0, tiled=True),
        )
        scores = (
            jnp.einsum("qhd,khd->hqk", query, keys_all, preferred_element_type=jnp.float32) * scale
        )
        scores = jnp.where(allowed, scores, -1e30)
        top = jnp.max(scores, axis=-1, keepdims=True)
        weights = jnp.exp(scores - top)
        total = jnp.sum(weights, axis=-1, keepdims=True)
        probs = (weights / total).astype(jnp.bfloat16)
        lse = top + jnp.log(total)
        adot = jnp.einsum("hqk,khd->qhd", probs, values_all, preferred_element_type=jnp.float32)
        if s == 0:
            memory_matrix_entry = memory_in[b]
            normalizer_entry = norms_in[b]
        else:
            fresh = resets[b, s - 1] > 0
            memory_matrix_entry = jnp.where(fresh, jnp.zeros_like(memory), memory)
            normalizer_entry = jnp.where(fresh, jnp.ones_like(norms), norms)
        qf = query.astype(jnp.float32)
        kf = qkv[b, s, :, 1].astype(jnp.float32)
        vf = qkv[b, s, :, 2].astype(jnp.float32)
        attention_memory_mix, memory_delta_write, key_sum = local_memory(
            qf, kf, vf, memory_matrix_entry, normalizer_entry
        )
        if s + 1 < segs:
            memory_delta_write, key_sum = (
                lax.psum(memory_delta_write.astype(jnp.bfloat16), "seq").astype(jnp.float32),
                lax.psum(key_sum.astype(jnp.bfloat16), "seq").astype(jnp.float32),
            )
            memory = memory_matrix_entry + memory_delta_write
            norms = normalizer_entry + key_sum
        mixes.append((gate * attention_memory_mix + (1.0 - gate) * adot).reshape(local, width))
        saved.append(
            (
                query,
                keys_all,
                values_all,
                lse,
                adot,
                attention_memory_mix,
                qf,
                kf,
                vf,
                memory_matrix_entry,
                normalizer_entry,
            )
        )
    attn = jnp.concatenate(mixes, axis=0).astype(jnp.bfloat16)
    x_one = x_flat + project(attn, 1)
    r_two = rms(x_one)
    h_two = (r_two * gain_ffn).astype(jnp.bfloat16)
    gate_up = project(h_two, 2).astype(jnp.bfloat16).astype(jnp.float32)
    gate_part = gate_up[:, :hidden_w]
    up_part = gate_up[:, hidden_w:]
    hidden = swiglu(gate_part, up_part).astype(jnp.bfloat16)
    output = (x_one + project(hidden, 3)).astype(jnp.bfloat16).reshape(tokens.shape)
    grad_y = cotangent.reshape(rows, width)
    part_down = reduce_rows(hidden, grad_y)
    grad_hidden = project_back(grad_y, 3)
    _, swiglu_back = jax.vjp(swiglu, gate_part, up_part)
    grad_gate, grad_up = swiglu_back(grad_hidden)
    grad_gu = jnp.concatenate([grad_gate, grad_up], axis=1).astype(jnp.bfloat16)
    part_gate_up = reduce_rows(h_two, grad_gu)
    grad_h_two = project_back(grad_gu, 2)
    gain_ffn_term = jnp.sum(grad_h_two * r_two, axis=0)
    _, norm_two_back = jax.vjp(rms, x_one)
    grad_x_one = grad_y.astype(jnp.float32) + norm_two_back(grad_h_two * gain_ffn)[0]
    grad_o = grad_x_one.astype(jnp.bfloat16)
    part_out = reduce_rows(attn, grad_o)
    grad_attn = project_back(grad_o, 1).astype(jnp.bfloat16).astype(jnp.float32)
    bias_term = jnp.zeros((heads,), jnp.float32)
    grads_q = [None] * len(saved)
    grads_k = [None] * len(saved)
    grads_v = [None] * len(saved)
    b = 0
    grad_m = jnp.zeros((heads, hdim, hdim), jnp.float32)
    grad_z = jnp.zeros((heads, hdim), jnp.float32)
    for s in reversed(range(segs)):
        index = b * segs + s
        (
            query,
            keys_all,
            values_all,
            lse,
            adot,
            attention_memory_mix,
            qf,
            kf,
            vf,
            memory_matrix_entry,
            normalizer_entry,
        ) = saved[index]
        grad_mix = grad_attn[index * local : (index + 1) * local].reshape(local, heads, hdim)
        bias_term = (
            bias_term
            + jnp.sum(grad_mix * (attention_memory_mix - adot), axis=(0, 2))
            * (gate * (1.0 - gate))[0, :, 0]
        )
        grad_amem = gate * grad_mix
        grad_adot = ((1.0 - gate) * grad_mix).astype(jnp.bfloat16)
        scores = (
            jnp.einsum("qhd,khd->hqk", query, keys_all, preferred_element_type=jnp.float32) * scale
        )
        scores = jnp.where(allowed, scores, -1e30)
        probs = jnp.exp(scores - lse)
        grad_p = jnp.einsum(
            "qhd,khd->hqk", grad_adot, values_all, preferred_element_type=jnp.float32
        )
        grad_s = (probs * (grad_p - jnp.sum(probs * grad_p, axis=-1, keepdims=True))).astype(
            jnp.bfloat16
        )
        q_att = (
            jnp.einsum("hqk,khd->qhd", grad_s, keys_all, preferred_element_type=jnp.float32) * scale
        )
        k_all = (
            jnp.einsum("hqk,qhd->khd", grad_s, query, preferred_element_type=jnp.float32) * scale
        )
        v_all = jnp.einsum(
            "hqk,qhd->khd",
            probs.astype(jnp.bfloat16),
            grad_adot,
            preferred_element_type=jnp.float32,
        )
        k_att, v_att = (
            lax.psum_scatter(
                k_all.astype(jnp.bfloat16), "seq", scatter_dimension=0, tiled=True
            ).astype(jnp.float32),
            lax.psum_scatter(
                v_all.astype(jnp.bfloat16), "seq", scatter_dimension=0, tiled=True
            ).astype(jnp.float32),
        )
        _, memory_back = jax.vjp(local_memory, qf, kf, vf, memory_matrix_entry, normalizer_entry)
        q_mem, k_mem, v_mem, m_local, z_local = memory_back((grad_amem, grad_m, grad_z))
        if s > 0:
            m_local, z_local = (
                lax.psum(m_local.astype(jnp.bfloat16), "seq").astype(jnp.float32),
                lax.psum(z_local.astype(jnp.bfloat16), "seq").astype(jnp.float32),
            )
            cut = (resets[b, s - 1] > 0) | (s % depth[b] == 0)
            grad_m = jnp.where(cut, jnp.zeros_like(grad_m), m_local)
            grad_z = jnp.where(cut, jnp.zeros_like(grad_z), z_local)
        grads_q[index] = (q_att + q_mem).reshape(local, width)
        grads_k[index] = (k_att + k_mem).reshape(local, width)
        grads_v[index] = (v_att + v_mem).reshape(local, width)
    grad_qkv_rows = jnp.concatenate(
        [
            jnp.concatenate(grads_q, axis=0),
            jnp.concatenate(grads_k, axis=0),
            jnp.concatenate(grads_v, axis=0),
        ],
        axis=1,
    ).astype(jnp.bfloat16)
    part_qkv = reduce_rows(h_one, grad_qkv_rows)
    grad_h_one = project_back(grad_qkv_rows, 0)
    gain_attn_term = jnp.sum(grad_h_one * r_one, axis=0)
    _, norm_one_back = jax.vjp(rms, x_flat)
    grad_x = grad_x_one + norm_one_back(grad_h_one * gain_attn)[0]
    input_grad = grad_x.astype(jnp.bfloat16).reshape(tokens.shape)
    grad_qkv, grad_out, grad_gate_up, grad_down = (
        lax.psum(part_qkv.astype(jnp.bfloat16), "seq").astype(jnp.float32),
        lax.psum(part_out.astype(jnp.bfloat16), "seq").astype(jnp.float32),
        lax.psum(part_gate_up.astype(jnp.bfloat16), "seq").astype(jnp.float32),
        lax.psum(part_down.astype(jnp.bfloat16), "seq").astype(jnp.float32),
    )
    grad_gain_attn, grad_gain_ffn, grad_gate_bias = lax.psum(
        (gain_attn_term, gain_ffn_term, bias_term), ("seq", "fsdp")
    )
    return (
        output,
        input_grad,
        grad_qkv,
        grad_out,
        grad_gate_up,
        grad_down,
        grad_gain_attn,
        grad_gain_ffn,
        grad_gate_bias,
    )


def solution(mesh):
    in_specs = (
        P("fsdp", None, "seq", None),
        P("fsdp", None, "seq", None),
        P("fsdp", None),
        P("fsdp", None),
        P("fsdp", None),
        P("fsdp", None),
        P(),
        P(),
        P(),
        P("fsdp", None, None, None),
        P("fsdp", None, None),
        P("fsdp", None),
        P("fsdp"),
    )
    out_specs = (
        P("fsdp", None, "seq", None),
        P("fsdp", None, "seq", None),
        P("fsdp", None),
        P("fsdp", None),
        P("fsdp", None),
        P("fsdp", None),
        P(),
        P(),
        P(),
    )
    return jax.shard_map(body, mesh=mesh, in_specs=in_specs, out_specs=out_specs, check_vma=False)
```

profile of v0, /device:TPU:0, one launch (start us, length us, event | category | flops | bytes accessed | tf_op | source)
XLA Modules:
  0.0 5563.6 jit_solution(6473872001343915223)
XLA Ops:
  12.3 480.4 %all-gather.13.cloned.1.call-done = bf16[2048,6144]{1,0:T(8,128)(2,1)} async-done(((bf16[256,6144]{1,0:T(8,128)(2,1)}), bf16[2048,6144]{1,0:T(8,128)(2,1)}) %all-gather.13.cloned.1.call-update) | async-done | bytes 25165840 | tf_op jit(solution)/shard_map/all_gather | solution.py:54
  492.7 18.5 fusion.46
  571.2 31.4 all-gather.27.cloned.1.call-done
  613.1 26.1 all-gather.23.cloned.1.call-done
  639.1 13.0 fusion.256
  661.9 13.7 all-gather.25.cloned.1.call-done
  685.5 26.6 all-gather.21.cloned.1.call-done
  712.1 12.8 fusion.99
  724.9 114.2 %all-gather.15.cloned.1.call-done = bf16[2048,2048]{1,0:T(8,128)(2,1)} async-done(((bf16[256,2048]{1,0:T(8,128)(2,1)}), bf16[2048,2048]{1,0:T(8,128)(2,1)}) %all-gather.15.cloned.1.call-update) | async-done | bytes 8388624 | tf_op jit(solution)/shard_map/all_gather | solution.py:54
  850.3 1255.5 %all-gather.17.cloned.1.call-done = bf16[2048,16384]{1,0:T(8,128)(2,1)} async-done(((bf16[256,16384]{1,0:T(8,128)(2,1)}), bf16[2048,16384]{1,0:T(8,128)(2,1)}) %all-gather.17.cloned.1.call-update) | async-done | bytes 67108880 | tf_op jit(solution)/shard_map/all_gather | solution.py:54
  2105.8 45.9 fusion
  2151.7 593.4 %all-gather.19.cloned.1.call-done = bf16[8192,2048]{1,0:T(8,128)(2,1)} async-done(((bf16[1024,2048]{1,0:T(8,128)(2,1)}), bf16[8192,2048]{1,0:T(8,128)(2,1)}) %all-gather.19.cloned.1.call-update) | async-done | bytes 33554448 | tf_op jit(solution)/shard_map/all_gather | solution.py:54
  2745.1 38.5 fusion.3
  2783.6 49.1 multiply_reduce_fusion.2
  2877.4 11.5 convert_bitcast_fusion.1
  2889.0 13.9 multiply_reduce_fusion.1
  2902.9 12.0 multiply_convert_fusion.1
  2923.1 13.2 multiply_reduce_fusion
  2936.3 13.4 multiply_convert_fusion
  3055.2 22.6 reduce-scatter.11.cloned.1.call-done
  3088.5 24.0 convolution_convert_fusion.3
  3114.1 25.0 convolution_convert_fusion.1
  3139.8 44.2 convolution_convert_fusion
  3184.7 45.5 reduce-scatter.19.cloned.1.call-done
  3230.2 406.9 %reduce-scatter.17.cloned.1.call-done = bf16[256,6144]{1,0:T(8,128)(2,1)} async-done(((bf16[2048,6144]{1,0:T(8,128)(2,1)}), bf16[256,6144]{1,0:T(8,128)(2,1)}) %reduce-scatter.17.cloned.1.call-update) | async-done | bytes 3145744 | tf_op jit(solution)/shard_map/reduce_scatter | solution.py:68
  3637.2 546.3 %reduce-scatter.23.cloned.1.call-done = bf16[1024,2048]{1,0:T(8,128)(2,1)} async-done(((bf16[8192,2048]{1,0:T(8,128)(2,1)}), bf16[1024,2048]{1,0:T(8,128)(2,1)}) %reduce-scatter.23.cloned.1.call-update) | async-done | bytes 4194320 | tf_op jit(solution)/shard_map/reduce_scatter | solution.py:68
  4183.5 1058.7 %reduce-scatter.21.cloned.1.call-done = bf16[256,16384]{1,0:T(8,128)(2,1)} async-done(((bf16[2048,16384]{1,0:T(8,128)(2,1)}), bf16[256,16384]{1,0:T(8,128)(2,1)}) %reduce-scatter.21.cloned.1.call-update) | async-done | bytes 8388624 | tf_op jit(solution)/shard_map/reduce_scatter | solution.py:68
  5242.2 25.1 add_convert_fusion
  5267.3 28.2 fusion.38
  5295.6 40.9 all-reduce
  5342.7 193.0 %all-reduce.10.cloned.1.call-done = (bf16[256,6144]{1,0:T(8,128)(2,1)}, bf16[256,2048]{1,0:T(8,128)(2,1)}, bf16[256,16384]{1,0:T(8,128)(2,1)}, bf16[1024,2048]{1,0:T(8,128)(2,1)}) async-done(((bf16[256,6144]{1,0:T(8,128)(2,1)}, bf16[256,2048]{1,0:T(8,128)(2,1)}, bf16[256,16384]{1,0:T(8,128)(2,1)}, bf16[1024,2048]{1,0:T(8,128)(2,1)}), (bf16[256,6144]{1,0:T(8,128)(2,1)}, bf16[256,2048]{1,0:T(8,128)(2,1)}, ...) | async-done | bytes 16777232 | tf_op jit(solution)/shard_map/psum | solution.py:284
  5535.7 11.7 convert_element_type.236
  (296 shorter events, 292.0 us)
Async XLA Ops:
  7.2 485.5 %all-gather.13.cloned.1.call-start = ((), (), s32[]{:S(2)}) async-start(), calls=%async_computation.8 | async-start | bytes 28311552 | tf_op jit(solution)/shard_map/all_gather | solution.py:54
  7.9 558.0 %all-reduce.6.cloned.1.call-start = ((), (), s32[]{:S(2)}) async-start(), calls=%async_computation.9 | async-start | bytes 1048576 | tf_op jit(solution)/shard_map/psum | solution.py:151
  532.7 70.0 %all-gather.27.cloned.1.call-start = ((), (), s32[]{:S(2)}) async-start(), calls=%async_computation.25 | async-start | bytes 5242880 | tf_op jit(solution)/shard_map/all_gather | solution.py:123
  534.0 105.1 %all-gather.23.cloned.1.call-start = ((), (), s32[]{:S(2)}) async-start(), calls=%async_computation.23 | async-start | bytes 5242880 | tf_op jit(solution)/shard_map/all_gather | solution.py:123
  536.6 139.0 %all-gather.25.cloned.1.call-start = ((), (), s32[]{:S(2)}) async-start(), calls=%async_computation.24 | async-start | bytes 5242880 | tf_op jit(solution)/shard_map/all_gather | solution.py:124
  538.3 173.8 %all-gather.21.cloned.1.call-start = ((), (), s32[]{:S(2)}) async-start(), calls=%async_computation.22 | async-start | bytes 5242880 | tf_op jit(solution)/shard_map/all_gather | solution.py:124
  538.8 300.3 %all-gather.15.cloned.1.call-start = ((), (), s32[]{:S(2)}) async-start(), calls=%async_computation.10 | async-start | bytes 9437184 | tf_op jit(solution)/shard_map/all_gather | solution.py:54
  539.6 1566.2 %all-gather.17.cloned.1.call-start = ((), (), s32[]{:S(2)}) async-start(), calls=%async_computation.11 | async-start | bytes 75497472 | tf_op jit(solution)/shard_map/all_gather | solution.py:54
  540.4 2204.7 %all-gather.19.cloned.1.call-start = ((), (), s32[]{:S(2)}) async-start(), calls=%async_computation.12 | async-start | bytes 37748736 | tf_op jit(solution)/shard_map/all_gather | solution.py:54
  541.1 2468.6 %reduce-scatter.15.cloned.1.call-start = ((), (), s32[]{:S(2)}) async-start(), calls=%async_computation.17 | async-start | bytes 5242880 | tf_op jit(solution)/shard_map/reduce_scatter | solution.py:252
  541.8 170.2 %copy-start.66 = (f32[16]{0:T(128)}, f32[16]{0:T(128)S(1)}, u32[]{:S(2)}) copy-start(f32[16]{0:T(128)S(1)} %get-tuple-element.24) | copy-start | bytes 196
  541.8 170.2 %copy-start.77 = (f32[16]{0:T(128)}, f32[16]{0:T(128)S(1)}, u32[]{:S(2)}) copy-start(f32[16]{0:T(128)S(1)} %get-tuple-element.25) | copy-start | bytes 196
  553.5 158.5 %copy-start.44 = (f32[16,1,256]{2,0,1:T(8,128)}, f32[16,1,256]{2,0,1:T(8,128)S(1)}, u32[]{:S(2)}) copy-start(f32[16,1,256]{2,0,1:T(8,128)S(1)} %copy.243) | copy-start | bytes 49156
  556.6 155.5 %copy-start.46 = (f32[16,1,256]{2,0,1:T(8,128)}, f32[16,1,256]{2,0,1:T(8,128)S(1)}, u32[]{:S(2)}) copy-start(f32[16,1,256]{2,0,1:T(8,128)S(1)} %copy.244) | copy-start | bytes 49156
  652.2 59.9 %copy-start.42 = (f32[16,256]{1,0:T(8,128)}, f32[16,256]{1,0:T(8,128)S(1)}, u32[]{:S(2)}) copy-start(f32[16,256]{1,0:T(8,128)S(1)} %get-tuple-element.53) | copy-start | bytes 49156
  661.9 50.2 copy-start.54
  724.9 124.8 %copy-start.84 = (bf16[256,16,128]{0,2,1:T(8,128)(2,1)}, bf16[256,16,128]{0,2,1:T(8,128)(2,1)S(1)}, u32[]{:S(2)}) copy-start(bf16[256,16,128]{0,2,1:T(8,128)(2,1)S(1)} %get-tuple-element.49) | copy-start | bytes 3145732
  839.1 1266.7 %copy-start.64 = (f32[2048]{0:T(1024)S(1)}, f32[2048]{0:T(1024)}, u32[]{:S(2)}) copy-start(f32[2048]{0:T(1024)} %param.20) | copy-start | bytes 24580
  849.7 1302.1 %copy-start.68 = (f32[512]{0:T(512)}, f32[512]{0:T(512)S(1)}, u32[]{:S(2)}) copy-start(f32[512]{0:T(512)S(1)} %get-tuple-element.58) | copy-start | bytes 6148
  849.7 1983.1 %copy-start.75 = (f32[512]{0:T(512)}, f32[512]{0:T(512)S(1)}, u32[]{:S(2)}) copy-start(f32[512]{0:T(512)S(1)} %fusion.203) | copy-start | bytes 6148
  2105.8 639.3 %copy-start.29 = (bf16[1,2,256,2048]{3,2,1,0:T(8,128)(2,1)S(1)}, bf16[1,2,256,2048]{3,2,1,0:T(8,128)(2,1)}, u32[]{:S(2)}) copy-start(bf16[1,2,256,2048]{3,2,1,0:T(8,128)(2,1)} %param.14) | copy-start | bytes 6291460
  2783.6 49.1 copy-start.69
  2856.1 169.2 %all-reduce.8.cloned.1.call-start = ((), (), s32[]{:S(2)}) async-start(), calls=%async_computation.14 | async-start | bytes 1048576 | tf_op jit(solution)/shard_map/psum | solution.py:260
  2877.4 147.9 %reduce-scatter.13.cloned.1.call-start = ((), (), s32[]{:S(2)}) async-start(), calls=%async_computation.16 | async-start | bytes 5242880 | tf_op jit(solution)/shard_map/reduce_scatter | solution.py:252
  2888.9 148.9 %reduce-scatter.9.cloned.1.call-start = ((), (), s32[]{:S(2)}) async-start(), calls=%async_computation.13 | async-start | bytes 5242880 | tf_op jit(solution)/shard_map/reduce_scatter | solution.py:249
  2923.0 154.8 %reduce-scatter.11.cloned.1.call-start = ((), (), s32[]{:S(2)}) async-start(), calls=%async_computation.15 | async-start | bytes 5242880 | tf_op jit(solution)/shard_map/reduce_scatter | solution.py:249
  2957.9 272.3 %reduce-scatter.19.cloned.1.call-start = ((), (), s32[]{:S(2)}) async-start(), calls=%async_computation.19 | async-start | bytes 9437184 | tf_op jit(solution)/shard_map/reduce_scatter | solution.py:68
  2968.7 668.4 %reduce-scatter.17.cloned.1.call-start = ((), (), s32[]{:S(2)}) async-start(), calls=%async_computation.18 | async-start | bytes 28311552 | tf_op jit(solution)/shard_map/reduce_scatter | solution.py:68
  3112.5 1071.0 %reduce-scatter.23.cloned.1.call-start = ((), (), s32[]{:S(2)}) async-start(), calls=%async_computation.21 | async-start | bytes 37748736 | tf_op jit(solution)/shard_map/reduce_scatter | solution.py:68
  3139.1 2103.0 %reduce-scatter.21.cloned.1.call-start = ((), (), s32[]{:S(2)}) async-start(), calls=%async_computation.20 | async-start | bytes 75497472 | tf_op jit(solution)/shard_map/reduce_scatter | solution.py:68
  3184.0 2351.7 %all-reduce.10.cloned.1.call-start = ((), (), s32[]{:S(2)}) async-start(), calls=%async_computation.26 | async-start | bytes 33554432 | tf_op jit(solution)/shard_map/psum | solution.py:284
  5267.3 69.1 %copy-start.61 = (f32[1,2,2,128]{3,1,2,0:T(2,128)S(1)}, f32[1,2,2,128]{3,1,2,0:T(2,128)}, u32[]{:S(2)}) copy-start(f32[1,2,2,128]{3,1,2,0:T(2,128)} %copy-done.60) | copy-start | bytes 6148
  (72 other events, 464.6 us)
Sparse Core Ops, SparseCore 0:
  9.6 483.1 all-gather.12
  532.8 33.1 all-reduce.5
  568.1 34.4 all-gather.26
  604.6 34.4 all-gather.22
  640.5 35.0 all-gather.24
  677.0 35.0 all-gather.20
  714.2 124.9 all-gather.14
  840.7 1265.0 all-gather.16
  2107.3 637.6 all-gather.18
  2856.2 44.4 reduce-scatter.14
  2903.2 33.1 all-reduce.7
  2938.9 44.5 reduce-scatter.12
  2986.0 44.6 reduce-scatter.8
  3033.3 44.5 reduce-scatter.10
  3081.3 148.8 reduce-scatter.18
  3234.4 402.6 reduce-scatter.16
  3641.3 542.1 reduce-scatter.22
  4187.6 1054.5 reduce-scatter.20
  5245.2 290.4 all-reduce.9
where the time goes:
time: 5570 us; the launch traced here: 5560 us
  waiting for transfers between devices  4820 us (87%)
  matrix products  544 us (10%)
  other arithmetic  76.1 us (1%)
  blocking collectives  55.7 us (1%)
    all_gather x4, waiting for transfers between devices, fold_rows(): lax.all_gather(weight, 'fsdp', axis=0, tiled=True)  2440 us
    reduce_scatter x4, waiting for transfers between devices, reduce_rows(): lax.psum_scatter(lax.dot_general(left, grad, (((0,), (0,)), ((), ())), pr...  2060 us
    psum x1, waiting for transfers between devices, body(): lax.psum(part_qkv.astype(jnp.bfloat16), 'seq').astype(jnp.float32)  193 us
    dot_general x4, matrix products, spread_rows(): lax.dot_general(grad, lax.all_gather(weight, 'fsdp', axis=0, tiled=True),...  120 us
  transfers between devices with their start and end apart: 19, of which 15 were waited for; matrix products, arithmetic and copies ran while one was open for 9% of the time, Pallas kernels for 0%

commit v1 on v0

v1 whole, which is shorter than its diff:
```python
import jax
import jax.numpy as jnp
from jax import lax
from jax.sharding import PartitionSpec as P

norm_eps = 1e-05
bf16 = jnp.bfloat16
f32 = jnp.float32


def rms(value_rows_segment):
    return value_rows_segment * lax.rsqrt(
        jnp.mean(value_rows_segment * value_rows_segment, axis=-1, keepdims=True) + norm_eps
    )


def feature(value_rows_segment):
    return jnp.where(
        value_rows_segment > 0,
        value_rows_segment + 1.0,
        jnp.exp(jnp.minimum(value_rows_segment, 0.0)),
    )


def swiglu(gate_part, up_part):
    return jax.nn.silu(gate_part) * up_part


def local_memory(query, key, value_rows_segment, memory_matrix_entry, normalizer_entry):
    high = lax.Precision.HIGHEST
    feature_queries = feature(query)
    feature_keys = feature(key)
    attention_memory_mix = (
        jnp.einsum("zqi,qis->zqs", feature_queries, memory_matrix_entry, precision=high)
        / jnp.einsum("rzo,zo->rz", feature_queries, normalizer_entry, precision=high)[..., None]
    )
    memory_recall_read = (
        jnp.einsum("zqi,qis->zqs", feature_keys, memory_matrix_entry, precision=high)
        / jnp.einsum("rzo,zo->rz", feature_keys, normalizer_entry, precision=high)[..., None]
    )
    memory_delta_write = jnp.einsum(
        "ubf,ubc->bfc", feature_keys, value_rows_segment - memory_recall_read, precision=high
    )
    return (attention_memory_mix, memory_delta_write, jnp.sum(feature_keys, axis=0))


def ring_order(n):
    if n % 4 or n < 8:
        return list(range(n))
    wide = n // 4
    walk = []
    for r in range(4):
        cols = range(1, wide) if r % 2 == 0 else range(wide - 1, 0, -1)
        walk += [r * wide + c for c in cols]
    return walk + [r * wide for r in reversed(range(4))]


def tie(value, other):
    return lax.optimization_barrier((value, other))[0]


class Ring:
    def __init__(self, n):
        self.n = n
        self.order = ring_order(n)
        self.where = [self.order.index(i) for i in range(n)]
        self.me = lax.axis_index("fsdp")
        self.order_array = jnp.array(self.order, dtype=jnp.int32)
        self.at = jnp.array(self.where, dtype=jnp.int32)[self.me]

    def owner(self, step, way):
        return self.order_array[(self.at - way * step) % self.n]

    def send(self, value, way):
        n, order = self.n, self.order
        return lax.ppermute(
            value, "fsdp", [(order[p], order[(p + way) % n]) for p in range(n)]
        )

    def gather(self, block, way):
        out = jnp.zeros((self.n,) + block.shape, block.dtype)
        out = lax.dynamic_update_slice(out, block[None], (self.me,) + (0,) * block.ndim)
        travelling = block
        marks = []
        for step in range(1, self.n):
            travelling = self.send(travelling, way)
            marks.append(travelling)
            out = lax.dynamic_update_slice(
                out, travelling[None], (self.owner(step, way),) + (0,) * block.ndim
            )
        return out, marks

    def scatter(self, parts, way):
        def part(step):
            return lax.dynamic_index_in_dim(parts, self.owner(step, way), 0, keepdims=False)

        travelling = part(1 - self.n)
        for step in range(2 - self.n, 1):
            arrived = self.send(travelling, way)
            travelling = (arrived.astype(f32) + part(step).astype(f32)).astype(bf16)
        return travelling


class Team:
    def __init__(self, n):
        self.n = n
        self.me = lax.axis_index("seq")

    def send(self, value, other):
        return lax.ppermute(value, "seq", [(i, other(i)) for i in range(self.n)])

    def gather(self, block):
        n = self.n
        held = [(self.me, block)]
        travelling = block
        for step in range(1, n // 2):
            travelling = self.send(travelling, lambda i: (i + 2) % n)
            held.append(((self.me - 2 * step) % n, travelling))
        held += [(i ^ 1, self.send(value, lambda i: i ^ 1)) for i, value in list(held)]
        return held

    def scatter(self, part):
        n, pairs = self.n, self.n // 2
        other = self.me ^ 1

        def at(base, k):
            return (base + 2 * k) % n

        sums = [None] * pairs
        for k in reversed(range(pairs)):
            arrived = self.send(part(at(other, k)), lambda i: i ^ 1)
            sums[k] = arrived.astype(f32) + part(at(self.me, k)).astype(f32)
        total = sums[pairs - 1]
        for step in range(pairs - 1):
            arrived = self.send(total.astype(bf16), lambda i: (i + 2) % n)
            total = arrived.astype(f32) + sums[(-2 - step) % pairs]
        return total

    def exchange(self, part):
        held = [(self.me, part(self.me))]
        for k in range(1, self.n):
            held.append((self.me ^ k, self.send(part(self.me ^ k), lambda i: i ^ k)))
        return held


def place(held, axis, count):
    out = jnp.zeros((count,) + held[0][1].shape, held[0][1].dtype)
    for i, value in held:
        out = lax.dynamic_update_slice(out, value[None], (i,) + (0,) * value.ndim)
    return jnp.squeeze(jnp.moveaxis(out, 0, axis), axis + 1)


def mm(left, right):
    return jnp.dot(left, right, preferred_element_type=f32)


def mm_nt(left, right):
    return lax.dot_general(left, right, (((1,), (1,)), ((), ())), preferred_element_type=f32)


def mm_tn(left, right):
    return lax.dot_general(left, right, (((0,), (0,)), ((), ())), preferred_element_type=f32)


def make_body(n_seq, n_fsdp):
    def body(
        tokens,
        cotangent,
        w_qkv,
        w_out,
        w_gate_up,
        w_down,
        gain_attn,
        gain_ffn,
        gate_bias,
        memory_in,
        norms_in,
        resets,
        depth,
    ):
        _, segs, local, width = tokens.shape
        heads = gate_bias.shape[0]
        hdim = width // heads
        my_heads = heads // n_seq
        my_width = width // n_seq
        seg = local * n_seq
        rows = segs * local
        total_rows = segs * seg
        shard = w_qkv.shape[0]
        hidden_shard = w_down.shape[0]
        my_hidden = hidden_shard // n_seq
        scale = 1.0 / hdim**0.5
        ring = Ring(n_fsdp)
        team = Team(n_seq)
        me = team.me

        def mine(array, axis):
            return lax.dynamic_index_in_dim(array, me, axis, keepdims=False)

        qkv_own = mine(w_qkv.reshape(shard, 3, n_seq, my_width), 2)
        gate_up_own = mine(w_gate_up.reshape(shard, 2, n_fsdp, n_seq, my_hidden), 3)
        down_own = mine(w_down.reshape(n_seq, my_hidden, width), 0)
        out_rows = shard // n_seq
        out_own = mine(w_out.reshape(n_seq, out_rows, width), 0)

        def gather_rows(block, after):
            half = block.shape[0] // 2
            top, bottom = block[:half], block[half:]
            if after is not None:
                top, bottom = tie(top, after[0]), tie(bottom, after[1])
            a, marks_a = ring.gather(top, 1)
            b, marks_b = ring.gather(bottom, -1)
            return jnp.stack([a, b], axis=1), (marks_a[-2], marks_b[-2])

        def gather_pair(one, two, after):
            a, marks_a = ring.gather(tie(one, after[0]), 1)
            b, marks_b = ring.gather(tie(two, after[1]), -1)
            return a, b, (marks_a[-2], marks_b[-2])

        w_q, after = gather_rows(qkv_own.reshape(shard, 3 * my_width), None)
        w_q = w_q.reshape(width, 3 * my_width)
        w_o, after = gather_rows(out_own, after)
        w_o = w_o.reshape(n_fsdp, 1, out_rows, width)
        w_o = place(team.gather(w_o), 1, n_seq).reshape(width, width)
        w_g, w_u, after = gather_pair(
            gate_up_own[:, 0].reshape(shard, -1), gate_up_own[:, 1].reshape(shard, -1), after
        )
        w_g = w_g.reshape(width, -1)
        w_u = w_u.reshape(width, -1)
        w_d, after = gather_rows(down_own, after)
        w_d = w_d.reshape(n_fsdp * my_hidden, width)

        def gather_tokens(value):
            held = team.gather(value.reshape(segs, 1, local, width))
            return place(held, 1, n_seq).reshape(total_rows, width)

        def scatter_tokens(value):
            parts = value.reshape(segs, n_seq, local, width)
            return team.scatter(
                lambda i: lax.dynamic_index_in_dim(parts, i, 1, keepdims=False)
            ).reshape(rows, width)

        x_flat = tokens.reshape(rows, width).astype(f32)
        r_one = rms(x_flat)
        h_one = gather_tokens((r_one * gain_attn).astype(bf16))
        grad_y = cotangent.reshape(rows, width)
        grad_y_all = gather_tokens(grad_y)

        qkv = mm(h_one, w_q).astype(bf16).reshape(segs, seg, 3, my_heads, hdim)
        places = jnp.arange(seg, dtype=jnp.int32)
        allowed = (places[None, :] <= places[:, None])[None]
        bias = lax.dynamic_slice(gate_bias, (me * my_heads,), (my_heads,))
        gate = jax.nn.sigmoid(bias)[None, :, None]
        memory = lax.dynamic_slice(
            memory_in[0], (me * my_heads, 0, 0), (my_heads, hdim, hdim)
        )
        norms = lax.dynamic_slice(norms_in[0], (me * my_heads, 0), (my_heads, hdim))
        saved = []
        mixes = []
        for s in range(segs):
            query, key, value = qkv[s, :, 0], qkv[s, :, 1], qkv[s, :, 2]
            scores = jnp.einsum("qhd,khd->hqk", query, key, preferred_element_type=f32) * scale
            scores = jnp.where(allowed, scores, -1e30)
            top = jnp.max(scores, axis=-1, keepdims=True)
            weights = jnp.exp(scores - top)
            total = jnp.sum(weights, axis=-1, keepdims=True)
            probs = (weights / total).astype(bf16)
            lse = top + jnp.log(total)
            adot = jnp.einsum("hqk,khd->qhd", probs, value, preferred_element_type=f32)
            if s > 0:
                fresh = resets[0, s - 1] > 0
                memory = jnp.where(fresh, jnp.zeros_like(memory), memory)
                norms = jnp.where(fresh, jnp.ones_like(norms), norms)
            qf, kf, vf = query.astype(f32), key.astype(f32), value.astype(f32)
            amem, delta, key_sum = local_memory(qf, kf, vf, memory, norms)
            mixes.append((gate * amem + (1.0 - gate) * adot).reshape(seg, my_width))
            saved.append((query, key, value, lse, adot, amem, qf, kf, vf, memory, norms))
            memory = memory + delta
            norms = norms + key_sum
        attn_heads = jnp.stack(mixes).astype(bf16).reshape(segs, n_seq, local, my_width)
        attn = place(
            team.exchange(
                lambda i: lax.dynamic_index_in_dim(attn_heads, i, 1, keepdims=False).reshape(
                    rows, 1, my_width
                )
            ),
            1,
            n_seq,
        ).reshape(rows, width)
        x_one = x_flat + mm(attn, w_o)
        r_two = rms(x_one)
        h_two = gather_tokens((r_two * gain_ffn).astype(bf16))
        gate_part = mm(h_two, w_g).astype(bf16)
        up_part = mm(h_two, w_u).astype(bf16)
        hidden = swiglu(gate_part.astype(f32), up_part.astype(f32)).astype(bf16)
        output = x_one + scatter_tokens(mm(hidden, w_d).astype(bf16))
        output = output.astype(bf16).reshape(tokens.shape)

        def scatter_ring(left, grad, shape, way):
            parts = mm_tn(left, grad).astype(bf16)
            return ring.scatter(parts.reshape((n_fsdp, -1) + parts.shape[1:]), way)

        half = width // 2
        down_terms = (
            scatter_ring(hidden, grad_y_all[:, :half], None, 1),
            scatter_ring(hidden, grad_y_all[:, half:], None, -1),
        )
        grad_hidden = mm_nt(grad_y_all, w_d)
        _, swiglu_back = jax.vjp(swiglu, gate_part.astype(f32), up_part.astype(f32))
        grad_gate, grad_up = swiglu_back(grad_hidden)
        grad_gate, grad_up = grad_gate.astype(bf16), grad_up.astype(bf16)
        gate_up_terms = (
            scatter_ring(h_two, grad_gate, None, 1),
            scatter_ring(h_two, grad_up, None, -1),
        )
        grad_h_two = scatter_tokens((mm_nt(grad_gate, w_g) + mm_nt(grad_up, w_u)).astype(bf16))
        gain_ffn_term = jnp.sum(grad_h_two * r_two, axis=0)
        _, norm_two_back = jax.vjp(rms, x_one)
        grad_x_one = grad_y.astype(f32) + norm_two_back(grad_h_two * gain_ffn)[0]
        grad_o = grad_x_one.astype(bf16)

        out_parts = mm_tn(attn, grad_o).astype(bf16).reshape(n_fsdp, n_seq, out_rows, width)
        out_sum = team.scatter(
            lambda i: lax.dynamic_index_in_dim(out_parts, i, 1, keepdims=False)
        ).astype(bf16)
        out_terms = (
            ring.scatter(out_sum[:, : out_rows // 2], 1),
            ring.scatter(out_sum[:, out_rows // 2 :], -1),
        )

        grad_attn = mm_nt(grad_o, w_o).astype(bf16).reshape(rows, n_seq, my_width)
        grad_attn = place(
            team.exchange(
                lambda i: lax.dynamic_index_in_dim(grad_attn, i, 1, keepdims=False).reshape(
                    segs, 1, local, my_width
                )
            ),
            1,
            n_seq,
        )
        grad_attn = grad_attn.astype(f32).reshape(segs, seg, my_heads, hdim)
        bias_term = jnp.zeros((my_heads,), f32)
        grads = [None] * segs
        grad_m = jnp.zeros((my_heads, hdim, hdim), f32)
        grad_z = jnp.zeros((my_heads, hdim), f32)
        for s in reversed(range(segs)):
            query, key, value, lse, adot, amem, qf, kf, vf, memory, norms = saved[s]
            grad_mix = grad_attn[s]
            bias_term = (
                bias_term
                + jnp.sum(grad_mix * (amem - adot), axis=(0, 2)) * (gate * (1.0 - gate))[0, :, 0]
            )
            grad_amem = gate * grad_mix
            grad_adot = ((1.0 - gate) * grad_mix).astype(bf16)
            scores = jnp.einsum("qhd,khd->hqk", query, key, preferred_element_type=f32) * scale
            scores = jnp.where(allowed, scores, -1e30)
            probs = jnp.exp(scores - lse)
            grad_p = jnp.einsum("qhd,khd->hqk", grad_adot, value, preferred_element_type=f32)
            grad_s = (
                probs * (grad_p - jnp.sum(probs * grad_p, axis=-1, keepdims=True))
            ).astype(bf16)
            q_att = jnp.einsum("hqk,khd->qhd", grad_s, key, preferred_element_type=f32) * scale
            k_att = jnp.einsum("hqk,qhd->khd", grad_s, query, preferred_element_type=f32) * scale
            v_att = jnp.einsum(
                "hqk,qhd->khd", probs.astype(bf16), grad_adot, preferred_element_type=f32
            )
            _, memory_back = jax.vjp(local_memory, qf, kf, vf, memory, norms)
            q_mem, k_mem, v_mem, m_back, z_back = memory_back((grad_amem, grad_m, grad_z))
            if s > 0:
                cut = (resets[0, s - 1] > 0) | (s % depth[0] == 0)
                grad_m = jnp.where(cut, jnp.zeros_like(grad_m), m_back + grad_m)
                grad_z = jnp.where(cut, jnp.zeros_like(grad_z), z_back + grad_z)
            grads[s] = jnp.stack(
                [q_att + q_mem, k_att + k_mem, v_att + v_mem], axis=1
            ).astype(bf16)
        grad_qkv_rows = jnp.stack(grads).reshape(total_rows, 3 * my_width)
        half = 3 * my_width // 2
        qkv_terms = (
            scatter_ring(h_one, grad_qkv_rows[:, :half], None, 1),
            scatter_ring(h_one, grad_qkv_rows[:, half:], None, -1),
        )
        grad_h_one = scatter_tokens(mm_nt(grad_qkv_rows, w_q).astype(bf16))
        gain_attn_term = jnp.sum(grad_h_one * r_one, axis=0)
        _, norm_one_back = jax.vjp(rms, x_flat)
        grad_x = grad_x_one + norm_one_back(grad_h_one * gain_attn)[0]
        input_grad = grad_x.astype(bf16).reshape(tokens.shape)

        down_all = place(
            team.gather(jnp.concatenate(down_terms, axis=-1)[None]), 0, n_seq
        ).reshape(hidden_shard, width)
        gate_up_all = place(
            team.gather(jnp.stack(gate_up_terms, axis=1).reshape(shard, 2, n_fsdp, 1, my_hidden)),
            3,
            n_seq,
        ).reshape(shard, -1)
        out_all = place(team.gather(jnp.concatenate(out_terms, axis=0)[None]), 0, n_seq).reshape(
            shard, width
        )
        qkv_all = place(
            team.gather(jnp.concatenate(qkv_terms, axis=-1).reshape(shard, 3, 1, my_width)),
            2,
            n_seq,
        ).reshape(shard, -1)
        bias_all = lax.dynamic_update_slice(
            jnp.zeros((heads,), f32), bias_term, (me * my_heads,)
        )
        grad_gain_attn, grad_gain_ffn, grad_gate_bias = lax.psum(
            (gain_attn_term, gain_ffn_term, bias_all), ("seq", "fsdp")
        )
        return (
            output,
            input_grad,
            qkv_all.astype(f32),
            out_all.astype(f32),
            gate_up_all.astype(f32),
            down_all.astype(f32),
            grad_gain_attn,
            grad_gain_ffn,
            grad_gate_bias,
        )

    return body


def solution(mesh):
    in_specs = (
        P("fsdp", None, "seq", None),
        P("fsdp", None, "seq", None),
        P("fsdp", None),
        P("fsdp", None),
        P("fsdp", None),
        P("fsdp", None),
        P(),
        P(),
        P(),
        P("fsdp", None, None, None),
        P("fsdp", None, None),
        P("fsdp", None),
        P("fsdp"),
    )
    out_specs = (
        P("fsdp", None, "seq", None),
        P("fsdp", None, "seq", None),
        P("fsdp", None),
        P("fsdp", None),
        P("fsdp", None),
        P("fsdp", None),
        P(),
        P(),
        P(),
    )
    body = make_body(mesh.shape["seq"], mesh.shape["fsdp"])
    return jax.shard_map(body, mesh=mesh, in_specs=in_specs, out_specs=out_specs, check_vma=False)
```

time: 5570 us -> 2040 us (0.37)
  waiting for transfers between devices: 4820 us -> 499 us
  local copies, waits for them, and re-layouts: 46.9 us -> 632 us
  starting transfers between devices: 0.98 us -> 144 us
  other arithmetic: 76.1 us -> 176 us
  matrix products: 544 us -> 476 us
    all_gather x8 -> x0, waiting for transfers between devices: 2540 us -> none  [the longest x4 2440 us: fold_rows(): lax.all_gather(weight, 'fsdp', axis=0, tiled=True)]
    reduce_scatter x8 -> x0, waiting for transfers between devices: 2080 us -> none  [the longest x4 2060 us: reduce_rows(): lax.psum_scatter(lax.dot_general(left, grad, (((0,), (0,)), ((), ())), pr...]
    ppermute x0 -> x154, waiting for transfers between devices: none -> 499 us  [the longest x112 455 us: send(): lax.ppermute(value, 'fsdp', [(order[p], order[(p + way) % n]) for p in ra...]
    dynamic_update_slice x0 -> x100, local copies, waits for them, and re-layouts: none -> 360 us  [the longest x37 324 us: place(): out = lax.dynamic_update_slice(out, value[None], (i,) + (0,) * value.ndim)]
    psum x3 -> x0, waiting for transfers between devices: 198 us -> none  [the longest x1 193 us: body(): lax.psum(part_qkv.astype(jnp.bfloat16), 'seq').astype(jnp.float32)]
    ppermute x0 -> x154, starting transfers between devices: none -> 144 us  [the longest x112 124 us: send(): lax.ppermute(value, 'fsdp', [(order[p], order[(p + way) % n]) for p in ra...]
    dot_general x30 -> x35, matrix products: 457 us -> 413 us  [the longest x5 101 us: mm(): return jnp.dot(left, right, preferred_element_type=f32)]
  transfers between devices with their start and end apart: 19 -> 154, of which waited for: 15 -> 65; matrix products, arithmetic and copies ran while one was open for 9% -> 49% of each run, Pallas kernels for 0% -> 0%
where the time goes in v1:
time: 2040 us; the launch traced here: 2010 us
  local copies, waits for them, and re-layouts  632 us (31%)
  waiting for transfers between devices  499 us (24%)
  matrix products  476 us (23%)
  other arithmetic  176 us (9%)
  starting transfers between devices  144 us (7%)
  between operations  44.7 us (2%)
  blocking collectives  38.8 us (2%)
    ppermute x112, waiting for transfers between devices, send(): lax.ppermute(value, 'fsdp', [(order[p], order[(p + way) % n]) for p in ra...  455 us
    dynamic_update_slice x37, local copies, waits for them, and re-layouts, place(): out = lax.dynamic_update_slice(out, value[None], (i,) + (0,) * value.ndim)  324 us
    ppermute x112, starting transfers between devices, send(): lax.ppermute(value, 'fsdp', [(order[p], order[(p + way) % n]) for p in ra...  124 us
    dot_general x5, matrix products, mm(): return jnp.dot(left, right, preferred_element_type=f32)  101 us
    dot_general x7, matrix products, mm_tn(): lax.dot_general(left, right, (((0,), (0,)), ((), ())), preferred_element_...  99.9 us
    dot_general x5, matrix products, mm_nt(): lax.dot_general(left, right, (((1,), (1,)), ((), ())), preferred_element_...  98.4 us
    unnamed x327, local copies, waits for them, and re-layouts  53.5 us
    ppermute x42, waiting for transfers between devices, send(): return lax.ppermute(value, 'seq', [(i, other(i)) for i in range(self.n)])  43.6 us
  transfers between devices with their start and end apart: 154, of which 65 were waited for; matrix products, arithmetic and copies ran while one was open for 49% of the time, Pallas kernels for 0%

profile of v1, /device:TPU:0, one launch (start us, length us, event | category | flops | bytes accessed | tf_op | source)
XLA Modules:
  0.0 2010.1 jit_solution(8947298731218376383)
XLA Ops:
  273.5 18.6 convolution_convert_fusion.7
  461.0 14.7 collective-permute-done.49
  482.0 17.3 collective-permute-done.50
  531.5 14.9 collective-permute-done.45
  566.6 19.3 collective-permute-done.53
  619.2 19.6 convolution_convert_fusion.5
  668.2 24.7 %fusion.332 = f32[2048,2048]{1,0:T(8,128)} fusion(bf16[2048,2048]{1,0:T(8,128)(2,1)} %bitcast.175, bf16[2048,2048]{1,0:T(8,128)(2,1)} %bitcast.1063), kind=kOutput, calls=%fused_computation.640 | convolution fusion | flops 17179869184 | bytes 33554432 | tf_op jit(solution)/shard_map/dot_general | solution.py:158
  692.9 35.4 %fusion.6 = (bf16[2048,2048]{1,0:T(8,128)(2,1)}, bf16[2048,2048]{1,0:T(8,128)(2,1)}, bf16[2048,2048]{1,0:T(8,128)(2,1)}) fusion(f32[2048,2048]{1,0:T(8,128)} %fusion.332, bf16[2048,2048]{1,0:T(8,128)(2,1)} %convolution_convert_fusion.5, bf16[2048,2048]{1,0:T(8,128)(2,1)} %bitcast.1076, bf16[2048,2048]{1,0:T(8,128)(2,1)} %bitcast.1069), kind=kOutput, calls=%fused_computation.12 | convolution fusion | flops 17259560960 | bytes 67108864 | tf_op jit(solution)/shard_map/dot_general | solution.py:154
  728.3 22.8 %convolution_convert_fusion.4 = bf16[2048,2048]{1,0:T(8,128)(2,1)S(1)} fusion(bf16[2048,2048]{1,0:T(8,128)(2,1)} %get-tuple-element.38, bf16[2048,2048]{1,0:T(8,128)(2,1)} %bitcast.1064), kind=kOutput, calls=%fused_computation.43 | convolution fusion | flops 17184063488 | bytes 25165824 | tf_op jit(solution)/shard_map/dot_general | solution.py:154
  779.8 22.0 %fusion.333 = f32[2048,2048]{1,0:T(8,128)} fusion(bf16[2048,2048]{1,0:T(8,128)(2,1)} %get-tuple-element.37, bf16[2048,2048]{1,0:T(8,128)(2,1)S(1)} %bitcast.1068), kind=kOutput, calls=%fused_computation.641 | convolution fusion | flops 17179869184 | bytes 33554432 | tf_op jit(solution)/shard_map/dot_general | solution.py:158
  801.8 22.5 %convolution_convert_fusion = bf16[2048,2048]{1,0:T(8,128)(2,1)} fusion(bf16[2048,2048]{1,0:T(8,128)(2,1)S(1)} %bitcast.1079, bf16[2048,2048]{1,0:T(8,128)(2,1)} %get-tuple-element.37), kind=kOutput, calls=%fused_computation.39 | convolution fusion | flops 17184063488 | bytes 25165824 | tf_op jit(solution)/shard_map/dot_general | solution.py:162
  826.1 22.2 %convolution_convert_fusion.1 = bf16[2048,2048]{1,0:T(8,128)(2,1)} fusion(bf16[2048,2048]{1,0:T(8,128)(2,1)S(1)} %bitcast.1080, bf16[2048,2048]{1,0:T(8,128)(2,1)} %get-tuple-element.36), kind=kOutput, calls=%fused_computation.40 | convolution fusion | flops 17184063488 | bytes 25165824 | tf_op jit(solution)/shard_map/dot_general | solution.py:162
  848.2 25.8 %add_convert_fusion = bf16[2048,2048]{1,0:T(8,128)(2,1)} fusion(f32[2048,2048]{1,0:T(8,128)} %fusion.333, bf16[2048,2048]{1,0:T(8,128)(2,1)} %get-tuple-element.36, bf16[2048,2048]{1,0:T(8,128)(2,1)} %bitcast.1070), kind=kOutput, calls=%fused_computation.20 | convolution fusion | flops 17188257792 | bytes 41943040 | tf_op jit(solution)/shard_map/dot_general | solution.py:158
  893.7 18.7 collective-permute-done.120
  946.6 25.4 %collective-permute-done.140 = bf16[256,1024]{1,0:T(8,128)(2,1)} collective-permute-done((bf16[256,1024]{1,0:T(8,128)(2,1)}, bf16[256,1024]{1,0:T(8,128)(2,1)}, u32[]{:S(2)}, u32[]{:S(2)}) %collective-permute-start.140) | collective-permute-done | bytes 524320 | tf_op jit(solution)/shard_map/ppermute | solution.py:76
  1048.7 35.0 %collective-permute-done.69 = bf16[2,256,2048]{2,1,0:T(8,128)(2,1)} collective-permute-done((bf16[2,256,2048]{2,1,0:T(8,128)(2,1)S(1)}, bf16[2,256,2048]{2,1,0:T(8,128)(2,1)}, u32[]{:S(2)}, u32[]{:S(2)}) %collective-permute-start.69) | collective-permute-done | bytes 2097184 | tf_op jit(solution)/shard_map/ppermute | solution.py:110
  1121.2 19.3 dynamic_update_slice.447
  1178.1 19.3 dynamic_update_slice.449
  1197.3 19.3 dynamic_update_slice.450
  1384.7 20.0 convolution_convert_fusion.3
  1481.2 22.5 %collective-permute-done.85 = bf16[256,768]{0,1:T(8,128)(2,1)S(1)} collective-permute-done((bf16[256,768]{0,1:T(8,128)(2,1)S(1)}, bf16[256,768]{0,1:T(8,128)(2,1)S(1)}, u32[]{:S(2)}, u32[]{:S(2)}) %collective-permute-start.85) | collective-permute-done | bytes 393248 | tf_op jit(solution)/shard_map/ppermute | solution.py:76
  1513.9 22.1 %collective-permute-done.93 = bf16[256,768]{0,1:T(8,128)(2,1)S(1)} collective-permute-done((bf16[256,768]{0,1:T(8,128)(2,1)S(1)}, bf16[256,768]{0,1:T(8,128)(2,1)S(1)}, u32[]{:S(2)}, u32[]{:S(2)}) %collective-permute-start.93) | collective-permute-done | bytes 393248 | tf_op jit(solution)/shard_map/ppermute | solution.py:76
  1555.1 23.2 %collective-permute-done.88 = bf16[256,768]{0,1:T(8,128)(2,1)S(1)} collective-permute-done((bf16[256,768]{0,1:T(8,128)(2,1)S(1)}, bf16[256,768]{0,1:T(8,128)(2,1)S(1)}, u32[]{:S(2)}, u32[]{:S(2)}) %collective-permute-start.88) | collective-permute-done | bytes 393248 | tf_op jit(solution)/shard_map/ppermute | solution.py:76
  1586.7 20.1 collective-permute-done.96
  1621.1 26.7 %dynamic_update_slice.451 = bf16[4,256,3,1,512]{4,0,2,1,3:T(4,128)(2,1)} dynamic-update-slice(bf16[4,256,3,1,512]{4,0,2,1,3:T(4,128)(2,1)} %broadcast_in_dim.328, bf16[1,256,3,1,512]{4,0,2,1,3:T(2,128)(2,1)S(1)} %copy.335, s32[]{:T(128)S(6)} %select_n.861, s32[]{:T(128)} %constant.688.clone.1, s32[]{:T(128)} %constant.688.clone.1, s32[]{:T(128)} %constant.688.clone.1, s32[]{:T(128)} %constant.688.clone.1) | dynamic-update-slice | bytes 1572868 | tf_op jit(solution)/shard_map/dynamic_update_slice | solution.py:149
  1658.4 26.7 %dynamic_update_slice.452 = bf16[4,256,3,1,512]{4,0,2,1,3:T(4,128)(2,1)} dynamic-update-slice(bf16[4,256,3,1,512]{4,0,2,1,3:T(4,128)(2,1)} %dynamic_update_slice.451, bf16[1,256,3,1,512]{4,0,2,1,3:T(2,128)(2,1)S(1)} %copy.336, s32[]{:T(128)S(6)} %select_n.863, s32[]{:T(128)} %constant.688.clone.1, s32[]{:T(128)} %constant.688.clone.1, s32[]{:T(128)} %constant.688.clone.1, s32[]{:T(128)} %constant.688.clone.1) | dynamic-update-slice | bytes 1572868 | tf_op jit(solution)/shard_map/dynamic_update_slice | solution.py:149
  1685.0 26.8 %dynamic_update_slice.453 = bf16[4,256,3,1,512]{4,0,2,1,3:T(4,128)(2,1)} dynamic-update-slice(bf16[4,256,3,1,512]{4,0,2,1,3:T(4,128)(2,1)} %dynamic_update_slice.452, bf16[1,256,3,1,512]{4,0,2,1,3:T(2,128)(2,1)} %copy.337, s32[]{:T(128)S(6)} %select_n.864, s32[]{:T(128)} %constant.688.clone.1, s32[]{:T(128)} %constant.688.clone.1, s32[]{:T(128)} %constant.688.clone.1, s32[]{:T(128)} %constant.688.clone.1) | dynamic-update-slice | bytes 1572868 | tf_op jit(solution)/shard_map/dynamic_update_slice | solution.py:149
  1769.3 38.8 %all-reduce = (f32[2048]{0:T(1024)}, f32[2048]{0:T(1024)}, f32[16]{0:T(128)}) all-reduce(f32[2048]{0:T(1024)S(1)} %get-tuple-element.30, f32[2048]{0:T(1024)S(1)} %copy-done.102, f32[16]{0:T(128)S(1)} %multiply_dynamic-update-slice_fusion), channel_id=1, replica_groups=mesh['seq'=4,'fsdp'=8] {'seq','fsdp'}, use_global_device_ids=true, to_apply=%region_16.17 | all-reduce | flops 4112 | bytes 32896 | tf_op jit(solution)/shard_map/psum | solution.py:407
  1813.2 26.7 %dynamic_update_slice.454 = bf16[4,256,3,1,512]{4,0,2,1,3:T(4,128)(2,1)} dynamic-update-slice(bf16[4,256,3,1,512]{4,0,2,1,3:T(4,128)(2,1)} %dynamic_update_slice.453, bf16[1,256,3,1,512]{4,0,2,1,3:T(2,128)(2,1)S(1)} %copy.339, s32[]{:T(128)S(6)} %select_n.865, s32[]{:T(128)} %constant.688.clone.1, s32[]{:T(128)} %constant.688.clone.1, s32[]{:T(128)} %constant.688.clone.1, s32[]{:T(128)} %constant.688.clone.1) | dynamic-update-slice | bytes 1572868 | tf_op jit(solution)/shard_map/dynamic_update_slice | solution.py:149
  1871.8 18.0 copy.347
  1899.6 80.0 %dynamic_update_slice.462 = bf16[4,256,2,8,1,256]{5,0,3,2,1,4:T(4,128)(2,1)} dynamic-update-slice(bf16[4,256,2,8,1,256]{5,0,3,2,1,4:T(4,128)(2,1)} %copy.347, bf16[1,256,2,8,1,256]{5,0,3,2,1,4:T(2,128)(2,1)} %copy.348, s32[]{:T(128)S(6)} %select_n.865, s32[]{:T(128)} %constant.688.clone.1, s32[]{:T(128)} %constant.688.clone.1, s32[]{:T(128)} %constant.688.clone.1, s32[]{:T(128)} %constant.688.clone.1, ...) | dynamic-update-slice | bytes 4194308 | tf_op jit(solution)/shard_map/dynamic_update_slice | solution.py:149
  1989.1 20.7 %reshape.838 = f32[256,16384]{1,0:T(8,128)} reshape(f32[256,2,8,4,1,256]{5,3,2,1,0,4:T(4,128)} %convert_bitcast_fusion) | data formatting | bytes 33554432 | tf_op jit(solution)/shard_map/convert_element_type | solution.py:415
  (968 shorter events, 1176.5 us)
Async XLA Ops:
  5.5 160.1 %collective-permute-start = (bf16[2,1,256,2048]{3,2,0,1:T(8,128)(2,1)}, bf16[2,1,256,2048]{3,2,0,1:T(8,128)(2,1)}, u32[]{:S(2)}, u32[]{:S(2)}) collective-permute-start(bf16[2,1,256,2048]{3,2,0,1:T(8,128)(2,1)} %fusion.26), channel_id=1, source_target_pairs={{0,16},{8,24},{16,0},{24,8},{1,17},{9,25},{17,1},{25,9},{2,18},{10... | collective-permute-start | bytes 6291464 | tf_op jit(solution)/shard_map/ppermute | solution.py:110
  8.5 165.0 %collective-permute-start.1 = (bf16[2,1,256,2048]{3,2,0,1:T(8,128)(2,1)}, bf16[2,1,256,2048]{3,2,0,1:T(8,128)(2,1)}, u32[]{:S(2)}, u32[]{:S(2)}) collective-permute-start(bf16[2,1,256,2048]{3,2,0,1:T(8,128)(2,1)} %fusion.26), channel_id=1, source_target_pairs={{0,8},{8,0},{16,24},{24,16},{1,9},{9,1},{17,25},{25,17},{2,10},{10... | collective-permute-start | bytes 6291464 | tf_op jit(solution)/shard_map/ppermute | solution.py:110
  15.1 96.7 %collective-permute-start.3 = (bf16[128,1536]{0,1:T(8,128)(2,1)}, bf16[128,1536]{0,1:T(8,128)(2,1)}, u32[]{:S(2)}, u32[]{:S(2)}) collective-permute-start(bf16[128,1536]{0,1:T(8,128)(2,1)} %bitcast.14), channel_id=1, source_target_pairs={{1,3},{3,5},{5,7},{7,6},{6,4},{4,2},{2,0},{0,1},{9,11},{11,13},{13... | collective-permute-start | bytes 1179656 | tf_op jit(solution)/shard_map/ppermute | solution.py:76
  16.6 96.4 %collective-permute-start.10 = (bf16[128,1536]{0,1:T(8,128)(2,1)S(1)}, bf16[128,1536]{0,1:T(8,128)(2,1)}, u32[]{:S(2)}, u32[]{:S(2)}) collective-permute-start(bf16[128,1536]{0,1:T(8,128)(2,1)S(1)} %bitcast.1119), channel_id=1, source_target_pairs={{1,0},{3,1},{5,3},{7,5},{6,7},{4,6},{2,4},{0,2},{9,8},{11,9},{13,1... | collective-permute-start | bytes 1179656 | tf_op jit(solution)/shard_map/ppermute | solution.py:76
  17.1 153.3 %collective-permute-start.71 = (bf16[2,1,256,2048]{3,2,0,1:T(8,128)(2,1)}, bf16[2,1,256,2048]{3,2,0,1:T(8,128)(2,1)}, u32[]{:S(2)}, u32[]{:S(2)}) collective-permute-start(bf16[2,1,256,2048]{3,2,0,1:T(8,128)(2,1)} %bitcast.1082), channel_id=1, source_target_pairs={{0,16},{8,24},{16,0},{24,8},{1,17},{9,25},{17,1},{25,9},{2,18},{10... | collective-permute-start | bytes 6291464 | tf_op jit(solution)/shard_map/ppermute | solution.py:110
  170.4 98.3 %collective-permute-start.2 = (bf16[2,1,256,2048]{3,2,0,1:T(8,128)(2,1)}, bf16[2,1,256,2048]{3,2,0,1:T(8,128)(2,1)}, u32[]{:S(2)}, u32[]{:S(2)}) collective-permute-start(bf16[2,1,256,2048]{3,2,0,1:T(8,128)(2,1)} %collective-permute-done), channel_id=1, source_target_pairs={{0,8},{8,0},{16,24},{24,16},{1,9},{9,1},{17,25},{25,17},{2,10},{10... | collective-permute-start | bytes 6291464 | tf_op jit(solution)/shard_map/ppermute | solution.py:110
  173.5 238.7 %collective-permute-start.73 = (bf16[2,1,256,2048]{3,2,0,1:T(8,128)(2,1)}, bf16[2,1,256,2048]{3,2,0,1:T(8,128)(2,1)}, u32[]{:S(2)}, u32[]{:S(2)}) collective-permute-start(bf16[2,1,256,2048]{3,2,0,1:T(8,128)(2,1)} %collective-permute-done.71), channel_id=1, source_target_pairs={{0,8},{8,0},{16,24},{24,16},{1,9},{9,1},{17,25},{25,17},{2,10},{10... | collective-permute-start | bytes 6291464 | tf_op jit(solution)/shard_map/ppermute | solution.py:110
  234.5 189.2 %collective-permute-start.47 = (bf16[256,2048]{1,0:T(8,128)(2,1)}, bf16[256,2048]{1,0:T(8,128)(2,1)}, u32[]{:S(2)}, u32[]{:S(2)}) collective-permute-start(bf16[256,2048]{1,0:T(8,128)(2,1)} %bitcast.467), channel_id=1, source_target_pairs={{1,0},{3,1},{5,3},{7,5},{6,7},{4,6},{2,4},{0,2},{9,8},{11,9},{13,1... | collective-permute-start | bytes 3145736 | tf_op jit(solution)/shard_map/ppermute | solution.py:76
  237.5 187.8 %collective-permute-start.40 = (bf16[256,2048]{1,0:T(8,128)(2,1)}, bf16[256,2048]{1,0:T(8,128)(2,1)}, u32[]{:S(2)}, u32[]{:S(2)}) collective-permute-start(bf16[256,2048]{1,0:T(8,128)(2,1)} %bitcast.464), channel_id=1, source_target_pairs={{1,3},{3,5},{5,7},{7,6},{6,4},{4,2},{2,0},{0,1},{9,11},{11,13},{13... | collective-permute-start | bytes 3145736 | tf_op jit(solution)/shard_map/ppermute | solution.py:76
  263.9 193.7 %collective-permute-start.34 = (bf16[8,1,64,2048]{3,2,0,1:T(8,128)(2,1)}, bf16[8,1,64,2048]{3,2,0,1:T(8,128)(2,1)}, u32[]{:S(2)}, u32[]{:S(2)}) collective-permute-start(bf16[8,1,64,2048]{3,2,0,1:T(8,128)(2,1)} %bitcast.100), channel_id=1, source_target_pairs={{0,16},{8,24},{16,0},{24,8},{1,17},{9,25},{17,1},{25,9},{2,18},{10... | collective-permute-start | bytes 6291464 | tf_op jit(solution)/shard_map/ppermute | solution.py:110
  561.2 57.7 %collective-permute-start.39 = (bf16[2,1,256,2048]{3,2,0,1:T(8,128)(2,1)}, bf16[2,1,256,2048]{3,2,0,1:T(8,128)(2,1)S(1)}, u32[]{:S(2)}, u32[]{:S(2)}) collective-permute-start(bf16[2,1,256,2048]{3,2,0,1:T(8,128)(2,1)} %collective-permute-done.37), channel_id=1, source_target_pairs={{0,8},{8,0},{16,24},{24,16},{1,9},{9,1},{17,25},{25,17},{2,10},{10... | collective-permute-start | bytes 6291464 | tf_op jit(solution)/shard_map/ppermute | solution.py:110
  826.1 115.2 %collective-permute-start.68 = (bf16[2,256,2048]{2,1,0:T(8,128)(2,1)}, bf16[2,256,2048]{2,1,0:T(8,128)(2,1)}, u32[]{:S(2)}, u32[]{:S(2)}) collective-permute-start(bf16[2,256,2048]{2,1,0:T(8,128)(2,1)} %get-tuple-element.45), channel_id=1, source_target_pairs={{0,8},{8,0},{16,24},{24,16},{1,9},{9,1},{17,25},{25,17},{2,10},{10... | collective-permute-start | bytes 6291464 | tf_op jit(solution)/shard_map/ppermute | solution.py:110
  884.2 60.9 %collective-permute-start.74 = (bf16[2,256,2048]{2,1,0:T(8,128)(2,1)S(1)}, bf16[2,256,2048]{2,1,0:T(8,128)(2,1)S(1)}, u32[]{:S(2)}, u32[]{:S(2)}) collective-permute-start(bf16[2,256,2048]{2,1,0:T(8,128)(2,1)S(1)} %get-tuple-element.43), channel_id=1, source_target_pairs={{0,8},{8,0},{16,24},{24,16},{1,9},{9,1},{17,25},{25,17},{2,10},{10... | collective-permute-start | bytes 6291464 | tf_op jit(solution)/shard_map/ppermute | solution.py:110
  923.2 117.7 %collective-permute-start.76 = (bf16[2,256,2048]{2,1,0:T(8,128)(2,1)S(1)}, bf16[2,256,2048]{2,1,0:T(8,128)(2,1)}, u32[]{:S(2)}, u32[]{:S(2)}) collective-permute-start(bf16[2,256,2048]{2,1,0:T(8,128)(2,1)S(1)} %get-tuple-element.44), channel_id=1, source_target_pairs={{0,8},{8,0},{16,24},{24,16},{1,9},{9,1},{17,25},{25,17},{2,10},{10... | collective-permute-start | bytes 6291464 | tf_op jit(solution)/shard_map/ppermute | solution.py:110
  972.1 68.8 %collective-permute-start.75 = (bf16[2,256,2048]{2,1,0:T(8,128)(2,1)S(1)}, bf16[2,256,2048]{2,1,0:T(8,128)(2,1)}, u32[]{:S(2)}, u32[]{:S(2)}) collective-permute-start(bf16[2,256,2048]{2,1,0:T(8,128)(2,1)S(1)} %fusion.43), channel_id=1, source_target_pairs={{0,16},{8,24},{16,0},{24,8},{1,17},{9,25},{17,1},{25,9},{2,18},{10... | collective-permute-start | bytes 6291464 | tf_op jit(solution)/shard_map/ppermute | solution.py:110
  1036.7 108.6 %collective-permute-start.123 = (bf16[256,2048]{1,0:T(8,128)(2,1)}, bf16[256,2048]{1,0:T(8,128)(2,1)}, u32[]{:S(2)}, u32[]{:S(2)}) collective-permute-start(bf16[256,2048]{1,0:T(8,128)(2,1)} %fusion.98), channel_id=1, source_target_pairs={{1,3},{3,5},{5,7},{7,6},{6,4},{4,2},{2,0},{0,1},{9,11},{11,13},{13... | collective-permute-start | bytes 3145736 | tf_op jit(solution)/shard_map/ppermute | solution.py:76
  1040.8 107.8 %collective-permute-start.130 = (bf16[256,2048]{1,0:T(8,128)(2,1)}, bf16[256,2048]{1,0:T(8,128)(2,1)}, u32[]{:S(2)}, u32[]{:S(2)}) collective-permute-start(bf16[256,2048]{1,0:T(8,128)(2,1)} %fusion.91), channel_id=1, source_target_pairs={{1,0},{3,1},{5,3},{7,5},{6,7},{4,6},{2,4},{0,2},{9,8},{11,9},{13,1... | collective-permute-start | bytes 3145736 | tf_op jit(solution)/shard_map/ppermute | solution.py:76
  1042.9 401.9 %collective-permute-start.151 = (bf16[1,256,2048]{2,1,0:T(8,128)(2,1)}, bf16[1,256,2048]{2,1,0:T(8,128)(2,1)}, u32[]{:S(2)}, u32[]{:S(2)}) collective-permute-start(bf16[1,256,2048]{2,1,0:T(8,128)(2,1)} %fusion.258), channel_id=1, source_target_pairs={{0,16},{8,24},{16,0},{24,8},{1,17},{9,25},{17,1},{25,9},{2,18},{10... | collective-permute-start | bytes 3145736 | tf_op jit(solution)/shard_map/ppermute | solution.py:110
  1148.7 299.5 %collective-permute-start.152 = (bf16[1,256,2048]{2,1,0:T(8,128)(2,1)}, bf16[1,256,2048]{2,1,0:T(8,128)(2,1)}, u32[]{:S(2)}, u32[]{:S(2)}) collective-permute-start(bf16[1,256,2048]{2,1,0:T(8,128)(2,1)} %fusion.258), channel_id=1, source_target_pairs={{0,8},{8,0},{16,24},{24,16},{1,9},{9,1},{17,25},{25,17},{2,10},{10... | collective-permute-start | bytes 3145736 | tf_op jit(solution)/shard_map/ppermute | solution.py:110
  1152.0 354.0 %collective-permute-start.100 = (bf16[8,64,2048]{2,1,0:T(8,128)(2,1)}, bf16[8,64,2048]{2,1,0:T(8,128)(2,1)}, u32[]{:S(2)}, u32[]{:S(2)}) collective-permute-start(bf16[8,64,2048]{2,1,0:T(8,128)(2,1)} %get-tuple-element.39), channel_id=1, source_target_pairs={{0,8},{8,0},{16,24},{24,16},{1,9},{9,1},{17,25},{25,17},{2,10},{10... | collective-permute-start | bytes 6291464 | tf_op jit(solution)/shard_map/ppermute | solution.py:110
  1154.7 304.3 %collective-permute-start.124 = (bf16[256,2048]{1,0:T(8,128)(2,1)}, bf16[256,2048]{1,0:T(8,128)(2,1)}, u32[]{:S(2)}, u32[]{:S(2)}) collective-permute-start(bf16[256,2048]{1,0:T(8,128)(2,1)} %fusion.97), channel_id=1, source_target_pairs={{1,3},{3,5},{5,7},{7,6},{6,4},{4,2},{2,0},{0,1},{9,11},{11,13},{13... | collective-permute-start | bytes 3145736 | tf_op jit(solution)/shard_map/ppermute | solution.py:76
  1160.4 302.2 %collective-permute-start.131 = (bf16[256,2048]{1,0:T(8,128)(2,1)}, bf16[256,2048]{1,0:T(8,128)(2,1)}, u32[]{:S(2)}, u32[]{:S(2)}) collective-permute-start(bf16[256,2048]{1,0:T(8,128)(2,1)} %fusion.90), channel_id=1, source_target_pairs={{1,0},{3,1},{5,3},{7,5},{6,7},{4,6},{2,4},{0,2},{9,8},{11,9},{13,1... | collective-permute-start | bytes 3145736 | tf_op jit(solution)/shard_map/ppermute | solution.py:76
  1456.0 93.7 %collective-permute-start.80 = (bf16[2,256,2048]{2,1,0:T(8,128)(2,1)S(1)}, bf16[2,256,2048]{2,1,0:T(8,128)(2,1)S(1)}, u32[]{:S(2)}, u32[]{:S(2)}) collective-permute-start(bf16[2,256,2048]{2,1,0:T(8,128)(2,1)S(1)} %get-tuple-element.41), channel_id=1, source_target_pairs={{0,8},{8,0},{16,24},{24,16},{1,9},{9,1},{17,25},{25,17},{2,10},{10... | collective-permute-start | bytes 6291464 | tf_op jit(solution)/shard_map/ppermute | solution.py:110
  1470.5 67.1 %collective-permute-start.125 = (bf16[256,2048]{1,0:T(8,128)(2,1)S(1)}, bf16[256,2048]{1,0:T(8,128)(2,1)S(1)}, u32[]{:S(2)}, u32[]{:S(2)}) collective-permute-start(bf16[256,2048]{1,0:T(8,128)(2,1)S(1)} %fusion.96), channel_id=1, source_target_pairs={{1,3},{3,5},{5,7},{7,6},{6,4},{4,2},{2,0},{0,1},{9,11},{11,13},{13... | collective-permute-start | bytes 3145736 | tf_op jit(solution)/shard_map/ppermute | solution.py:76
  1513.8 198.0 %collective-permute-start.102 = (bf16[8,64,2048]{2,1,0:T(8,128)(2,1)}, bf16[8,64,2048]{2,1,0:T(8,128)(2,1)}, u32[]{:S(2)}, u32[]{:S(2)}) collective-permute-start(bf16[8,64,2048]{2,1,0:T(8,128)(2,1)} %get-tuple-element.40), channel_id=1, source_target_pairs={{0,8},{8,0},{16,24},{24,16},{1,9},{9,1},{17,25},{25,17},{2,10},{10... | collective-permute-start | bytes 6291464 | tf_op jit(solution)/shard_map/ppermute | solution.py:110
  1536.1 175.8 %collective-permute-start.101 = (bf16[8,64,2048]{2,1,0:T(8,128)(2,1)}, bf16[8,64,2048]{2,1,0:T(8,128)(2,1)}, u32[]{:S(2)}, u32[]{:S(2)}) collective-permute-start(bf16[8,64,2048]{2,1,0:T(8,128)(2,1)} %fusion.39), channel_id=1, source_target_pairs={{0,16},{8,24},{16,0},{24,8},{1,17},{9,25},{17,1},{25,9},{2,18},{10... | collective-permute-start | bytes 6291464 | tf_op jit(solution)/shard_map/ppermute | solution.py:110
  1586.5 170.7 %collective-permute-start.82 = (bf16[2,256,2048]{2,1,0:T(8,128)(2,1)}, bf16[2,256,2048]{2,1,0:T(8,128)(2,1)}, u32[]{:S(2)}, u32[]{:S(2)}) collective-permute-start(bf16[2,256,2048]{2,1,0:T(8,128)(2,1)} %get-tuple-element.42), channel_id=1, source_target_pairs={{0,8},{8,0},{16,24},{24,16},{1,9},{9,1},{17,25},{25,17},{2,10},{10... | collective-permute-start | bytes 6291464 | tf_op jit(solution)/shard_map/ppermute | solution.py:110
  1647.8 111.2 %collective-permute-start.81 = (bf16[2,256,2048]{2,1,0:T(8,128)(2,1)}, bf16[2,256,2048]{2,1,0:T(8,128)(2,1)}, u32[]{:S(2)}, u32[]{:S(2)}) collective-permute-start(bf16[2,256,2048]{2,1,0:T(8,128)(2,1)} %fusion.41), channel_id=1, source_target_pairs={{0,16},{8,24},{16,0},{24,8},{1,17},{9,25},{17,1},{25,9},{2,18},{10... | collective-permute-start | bytes 6291464 | tf_op jit(solution)/shard_map/ppermute | solution.py:110
  1652.9 212.1 %collective-permute-start.134 = (bf16[256,2,8,1,256]{4,2,1,0,3:T(8,128)(2,1)}, bf16[256,2,8,1,256]{4,2,1,0,3:T(8,128)(2,1)}, u32[]{:S(2)}, u32[]{:S(2)}) collective-permute-start(bf16[256,2,8,1,256]{4,2,1,0,3:T(8,128)(2,1)} %constant_dynamic-update-slice_fusion.22), channel_id=1, source_target_pairs={{0,16},{8,24},{16,0},{24,8},{1,17},{9,25},{17,1},{25,9},{2,18},{10... | collective-permute-start | bytes 6291464 | tf_op jit(solution)/shard_map/ppermute | solution.py:110
  1711.8 156.9 %collective-permute-start.135 = (bf16[256,2,8,1,256]{4,2,1,0,3:T(8,128)(2,1)}, bf16[256,2,8,1,256]{4,2,1,0,3:T(8,128)(2,1)}, u32[]{:S(2)}, u32[]{:S(2)}) collective-permute-start(bf16[256,2,8,1,256]{4,2,1,0,3:T(8,128)(2,1)} %constant_dynamic-update-slice_fusion.22), channel_id=1, source_target_pairs={{0,8},{8,0},{16,24},{24,16},{1,9},{9,1},{17,25},{25,17},{2,10},{10... | collective-permute-start | bytes 6291464 | tf_op jit(solution)/shard_map/ppermute | solution.py:110
  1757.2 54.5 %collective-permute-start.99 = (bf16[256,3,1,512]{0,3,1,2:T(8,128)(2,1)}, bf16[256,3,1,512]{0,3,1,2:T(8,128)(2,1)S(1)}, u32[]{:S(2)}, u32[]{:S(2)}) collective-permute-start(bf16[256,3,1,512]{0,3,1,2:T(8,128)(2,1)} %collective-permute-done.97), channel_id=1, source_target_pairs={{0,8},{8,0},{16,24},{24,16},{1,9},{9,1},{17,25},{25,17},{2,10},{10... | collective-permute-start | bytes 2359304 | tf_op jit(solution)/shard_map/ppermute | solution.py:110
  1759.0 52.0 %collective-permute-start.114 = (bf16[32,2048]{1,0:T(8,128)(2,1)S(1)}, bf16[32,2048]{1,0:T(8,128)(2,1)S(1)}, u32[]{:S(2)}, u32[]{:S(2)}) collective-permute-start(bf16[32,2048]{1,0:T(8,128)(2,1)S(1)} %fusion.270), channel_id=1, source_target_pairs={{1,0},{3,1},{5,3},{7,5},{6,7},{4,6},{2,4},{0,2},{9,8},{11,9},{13,1... | collective-permute-start | bytes 393224 | tf_op jit(solution)/shard_map/ppermute | solution.py:76
  (271 other events, 5166.9 us)

commit v2 on v1

v2 whole, which is shorter than its diff:
```python
import functools

import jax
import jax.numpy as jnp
from jax import lax
from jax.experimental import pallas as pl
from jax.experimental.pallas import tpu as pltpu
from jax.sharding import PartitionSpec as P

norm_eps = 1e-05
bf16 = jnp.bfloat16
f32 = jnp.float32


def rms(value_rows_segment):
    return value_rows_segment * lax.rsqrt(
        jnp.mean(value_rows_segment * value_rows_segment, axis=-1, keepdims=True) + norm_eps
    )


def swiglu(gate_part, up_part):
    return jax.nn.silu(gate_part) * up_part


def feature(value_rows_segment):
    return jnp.where(
        value_rows_segment > 0,
        value_rows_segment + 1.0,
        jnp.exp(jnp.minimum(value_rows_segment, 0.0)),
    )


def contract(left, right, left_dim, right_dim):
    return lax.dot_general(
        left, right, (((left_dim,), (right_dim,)), ((), ())), preferred_element_type=f32
    )


def split(value):
    high = value.astype(bf16)
    return high, (value - high.astype(f32)).astype(bf16)


def fine(left, right, left_dim, right_dim):
    lh, ll = left
    rh, rl = right
    return (
        contract(lh, rl, left_dim, right_dim)
        + contract(ll, rh, left_dim, right_dim)
        + contract(lh, rh, left_dim, right_dim)
    )


LOG2E = 1.4426950408889634


def scores_of(key, query, block, i):
    n = (i + 1) * block
    sc = contract(key[:n], query, 1, 1)
    rows = lax.broadcasted_iota(jnp.int32, (block, block), 0)
    cols = lax.broadcasted_iota(jnp.int32, (block, block), 1)
    last = jnp.where(rows <= cols, sc[n - block :], -1e30)
    if i == 0:
        return last
    return jnp.concatenate([sc[: n - block], last], axis=0)


def forward_kernel(
    block, segs, gate, resets, q_ref, k_ref, v_ref, m_ref, z_ref, a_ref, lse_ref, mem_ref, nrm_ref, mem, nrm
):
    h, s = pl.program_id(0), pl.program_id(1)
    seg, hdim = q_ref.shape
    scale = LOG2E / hdim**0.5

    @pl.when(s == 0)
    def _():
        mem[...] = m_ref[0]
        nrm[...] = z_ref[0]

    @pl.when(s > 0)
    def _():
        @pl.when(resets[jnp.maximum(s - 1, 0)] > 0)
        def _():
            mem[...] = jnp.zeros_like(mem)
            nrm[...] = jnp.ones_like(nrm)

    mem_ref[0, 0] = mem[...]
    nrm_ref[0, 0] = nrm[...]
    g = gate[h]
    mem_parts = split(mem[...])
    key, value = k_ref[...], v_ref[...]
    value_t = value.T
    for i in range(seg // block):
        rows = slice(i * block, (i + 1) * block)
        query = q_ref[rows, :]
        sc = scores_of(key, query, block, i)
        top = jnp.max(sc, axis=0, keepdims=True)
        weights = jnp.exp2((sc - top) * scale)
        total = jnp.sum(weights, axis=0, keepdims=True)
        lse_ref[0, 0, :, rows] = top * scale + jnp.log2(total)
        adot_t = contract(value_t[:, : (i + 1) * block], weights.astype(bf16), 1, 0)
        adot_t = adot_t * ((1.0 - g) / total)
        sq = feature(query.astype(f32))
        amem = fine(split(sq), mem_parts, 1, 0) * (
            g / jnp.sum(sq * nrm[...], axis=1, keepdims=True)
        )
        a_ref[rows, :] = (amem + adot_t.T).astype(bf16)

    @pl.when(s + 1 < segs)
    def _():
        sk = feature(key.astype(f32))
        sk_parts = split(sk)
        recall = fine(sk_parts, mem_parts, 1, 0) / jnp.sum(sk * nrm[...], axis=1, keepdims=True)
        delta = split(value.astype(f32) - recall)
        mem[...] = mem[...] + fine(sk_parts, delta, 0, 0)
        nrm[...] = nrm[...] + jnp.sum(sk, axis=0, keepdims=True)


def specs(seg, hdim, heads, back, segs):
    def at(part):
        return pl.BlockSpec(
            (seg, hdim), lambda h, t: ((segs - 1 - t) if back else t, part * heads + h)
        )

    return at


def attention_forward(qkv, gate, resets, memory, norms, segs):
    total_rows, cols = qkv.shape
    heads, hdim, _ = memory.shape
    seg = total_rows // segs
    at = specs(seg, hdim, heads, False, segs)
    return pl.pallas_call(
        functools.partial(forward_kernel, min(256, seg), segs),
        grid=(heads, segs),
        in_specs=[
            pl.BlockSpec(memory_space=pltpu.SMEM),
            pl.BlockSpec(memory_space=pltpu.SMEM),
            at(0),
            at(1),
            at(2),
            pl.BlockSpec((1, hdim, hdim), lambda h, t: (h, 0, 0)),
            pl.BlockSpec((1, 1, hdim), lambda h, t: (h, 0, 0)),
        ],
        out_specs=[
            at(0),
            pl.BlockSpec((1, 1, 1, seg), lambda h, t: (h, t, 0, 0)),
            pl.BlockSpec((1, 1, hdim, hdim), lambda h, t: (h, t, 0, 0)),
            pl.BlockSpec((1, 1, 1, hdim), lambda h, t: (h, t, 0, 0)),
        ],
        out_shape=[
            jax.ShapeDtypeStruct((total_rows, heads * hdim), bf16),
            jax.ShapeDtypeStruct((heads, segs, 1, seg), f32),
            jax.ShapeDtypeStruct((heads, segs, hdim, hdim), f32),
            jax.ShapeDtypeStruct((heads, segs, 1, hdim), f32),
        ],
        scratch_shapes=[pltpu.VMEM((hdim, hdim), f32), pltpu.VMEM((1, hdim), f32)],
        compiler_params=pltpu.CompilerParams(vmem_limit_bytes=48 << 20),
        cost_estimate=pl.CostEstimate(
            flops=30 * total_rows * seg * heads * hdim // 8,
            bytes_accessed=4 * total_rows * cols,
            transcendentals=total_rows * seg * heads // 2,
        ),
        name="attention_forward",
    )(gate, resets, qkv, qkv, qkv, memory, norms.reshape(heads, 1, hdim))


def backward_kernel(
    block, segs, gate, resets, depth, q_ref, k_ref, v_ref, da_ref, lse_ref, mem_ref, nrm_ref,
    dq_ref, dk_ref, dv_ref, bias_ref, dm, dz, dk_att, dv_att,
):
    h, t = pl.program_id(0), pl.program_id(1)
    s = segs - 1 - t
    seg, hdim = q_ref.shape
    scale = 1.0 / hdim**0.5
    g = gate[h]

    @pl.when(t == 0)
    def _():
        dm[...] = jnp.zeros_like(dm)
        dz[...] = jnp.zeros_like(dz)
        bias_ref[...] = jnp.zeros_like(bias_ref)

    dk_att[...] = jnp.zeros_like(dk_att)
    dv_att[...] = jnp.zeros_like(dv_att)
    mem, nrm = mem_ref[0, 0], nrm_ref[0, 0]
    mem_parts = split(mem)
    key, value = k_ref[...], v_ref[...]
    key_t = key.T
    term = jnp.zeros((1, 1), f32)
    m_next = jnp.zeros((hdim, hdim), f32)
    z_next = jnp.zeros((1, hdim), f32)
    for i in range(seg // block):
        n = (i + 1) * block
        rows = slice(i * block, n)
        query = q_ref[rows, :]
        sc = scores_of(key, query, block, i)
        probs = jnp.exp2(sc * (scale * LOG2E) - lse_ref[0, 0, :, rows])
        grad_mix = da_ref[rows, :].astype(f32)
        grad_adot = ((1.0 - g) * grad_mix).astype(bf16)
        grad_p = contract(value[:n], grad_adot, 1, 1)
        row = jnp.sum(probs * grad_p, axis=0, keepdims=True)
        grad_s = (probs * (grad_p - row)).astype(bf16)
        dk_att[:n, :] += contract(grad_s, query, 1, 0)
        dv_att[:n, :] += contract(probs.astype(bf16), grad_adot, 1, 0)
        dq = contract(key_t[:, :n], grad_s, 1, 0).T * scale

        qf = query.astype(f32)
        sq = feature(qf)
        slope = jnp.where(qf > 0, 1.0, sq)
        sq_parts = split(sq)
        inverse = 1.0 / jnp.sum(sq * nrm, axis=1, keepdims=True)
        amem = fine(sq_parts, mem_parts, 1, 0) * inverse
        mixed = jnp.sum(grad_mix * amem, axis=1, keepdims=True)
        term = term + (g * (1.0 - g)) * jnp.sum(mixed, axis=0, keepdims=True)
        term = term - g * jnp.sum(row, axis=1, keepdims=True)
        d_top = split(grad_mix * (g * inverse))
        d_low = -(g * mixed) * inverse
        d_sq = fine(d_top, mem_parts, 1, 1) + d_low * nrm
        dq_ref[rows, :] = (dq + d_sq * slope).astype(bf16)
        m_next = m_next + fine(sq_parts, d_top, 0, 0)
        z_next = z_next + jnp.sum(sq * d_low, axis=0, keepdims=True)
    bias_ref[...] += jnp.broadcast_to(term[None], bias_ref.shape)
    dk_ref[...] = (dk_att[...] * scale).astype(bf16)
    dv_ref[...] = dv_att[...].astype(bf16)

    @pl.when(s + 1 < segs)
    def _():
        dm_now, dz_now = dm[...], dz[...]
        dm_parts = split(dm_now)
        kf = key.astype(f32)
        sk = feature(kf)
        slope = jnp.where(kf > 0, 1.0, sk)
        sk_parts = split(sk)
        inverse = 1.0 / jnp.sum(sk * nrm, axis=1, keepdims=True)
        recall = fine(sk_parts, mem_parts, 1, 0) * inverse
        delta = value.astype(f32) - recall
        d_delta = fine(sk_parts, dm_parts, 1, 0)
        d_top = split(-d_delta * inverse)
        d_low = jnp.sum(d_delta * recall, axis=1, keepdims=True) * inverse
        d_sk = (
            fine(split(delta), dm_parts, 1, 1)
            + dz_now
            + fine(d_top, mem_parts, 1, 1)
            + d_low * nrm
        )
        dk_ref[...] = (dk_att[...] * scale + d_sk * slope).astype(bf16)
        dv_ref[...] = (dv_att[...] + d_delta).astype(bf16)
        dm[...] = dm_now + fine(sk_parts, d_top, 0, 0)
        dz[...] = dz_now + jnp.sum(sk * d_low, axis=0, keepdims=True)

    @pl.when(s > 0)
    def _():
        cut = (resets[jnp.maximum(s - 1, 0)] > 0) | (lax.rem(s, depth[0]) == 0)
        dm[...] = jnp.where(cut, 0.0, dm[...] + m_next)
        dz[...] = jnp.where(cut, 0.0, dz[...] + z_next)


def attention_backward(qkv, grad_attn, gate, resets, depth, lse, mems, nrms, segs):
    total_rows, cols = qkv.shape
    heads, _, hdim, _ = mems.shape
    seg = total_rows // segs
    at = specs(seg, hdim, heads, True, segs)
    smem = pl.BlockSpec(memory_space=pltpu.SMEM)
    grad = jax.ShapeDtypeStruct((total_rows, heads * hdim), bf16)
    return pl.pallas_call(
        functools.partial(backward_kernel, min(256, seg), segs),
        grid=(heads, segs),
        in_specs=[
            smem,
            smem,
            smem,
            at(0),
            at(1),
            at(2),
            at(0),
            pl.BlockSpec((1, 1, 1, seg), lambda h, t: (h, segs - 1 - t, 0, 0)),
            pl.BlockSpec((1, 1, hdim, hdim), lambda h, t: (h, segs - 1 - t, 0, 0)),
            pl.BlockSpec((1, 1, 1, hdim), lambda h, t: (h, segs - 1 - t, 0, 0)),
        ],
        out_specs=[at(0), at(0), at(0), pl.BlockSpec((1, 8, hdim), lambda h, t: (h, 0, 0))],
        out_shape=[grad, grad, grad, jax.ShapeDtypeStruct((heads, 8, hdim), f32)],
        scratch_shapes=[
            pltpu.VMEM((hdim, hdim), f32),
            pltpu.VMEM((1, hdim), f32),
            pltpu.VMEM((seg, hdim), f32),
            pltpu.VMEM((seg, hdim), f32),
        ],
        compiler_params=pltpu.CompilerParams(vmem_limit_bytes=48 << 20),
        cost_estimate=pl.CostEstimate(
            flops=60 * total_rows * seg * heads * hdim // 8,
            bytes_accessed=4 * total_rows * cols,
            transcendentals=total_rows * seg * heads // 2,
        ),
        name="attention_backward",
    )(gate, resets, depth, qkv, qkv, qkv, grad_attn, lse, mems, nrms)


def tie(value, *others):
    return lax.optimization_barrier((value,) + others)[0]


MESH = pl.DeviceIdType.MESH


class Team:
    def __init__(self, n):
        self.n = n
        self.pairs = n // 2
        self.me = lax.axis_index("seq")
        self.calls = 0

    def call(self, kernel, inputs, out_shapes, scratch, name, cost):
        self.calls += 1
        anywhere = pl.BlockSpec(memory_space=pl.ANY)
        return pl.pallas_call(
            kernel,
            in_specs=[anywhere] * len(inputs),
            out_specs=[anywhere] * len(out_shapes),
            out_shape=out_shapes,
            scratch_shapes=scratch,
            compiler_params=pltpu.CompilerParams(
                collective_id=self.calls, has_side_effects=True, vmem_limit_bytes=48 << 20
            ),
            cost_estimate=pl.CostEstimate(flops=0, bytes_accessed=cost, transcendentals=0),
            name=name,
        )(*inputs)

    @staticmethod
    def greet(peers):
        barrier = pltpu.get_barrier_semaphore()
        for peer in peers:
            pl.semaphore_signal(barrier, inc=1, device_id={"seq": peer}, device_id_type=MESH)
        pl.semaphore_wait(barrier, len(peers))

    def gather(self, blocks, outer):
        n, pairs, count = self.n, self.pairs, len(blocks)
        shapes = [
            jax.ShapeDtypeStruct(
                ((n, b.shape[0]) if outer else (b.shape[0], n)) + b.shape[1:], b.dtype
            )
            for b in blocks
        ]
        steps = [(a, c) for a, b in enumerate(blocks) for c in range(b.shape[0])]
        total = len(steps)

        def kernel(*refs):
            ins, outs = refs[:count], refs[count : 2 * count]
            keep, y_out, y_in, c_out, c_in = refs[2 * count :]
            me = lax.axis_index("seq")
            core = lax.rem(me, 2)
            partner = me + 1 - 2 * core
            ahead = [lax.rem(me + 2 * k, n) for k in range(pairs)]
            behind = [lax.rem(me + n - 2 * k, n) for k in range(pairs)]
            self.greet([partner] + ahead[1:])

            def at(a, dev, c):
                return outs[a].at[dev, c] if outer else outs[a].at[c, dev]

            def remote(src, a, dev, c, out_sem, in_sem, to):
                return pltpu.make_async_remote_copy(
                    src_ref=src,
                    dst_ref=at(a, dev, c),
                    send_sem=out_sem,
                    recv_sem=in_sem,
                    device_id={"seq": to},
                    device_id_type=MESH,
                )

            started = []
            for i, (a, c) in enumerate(steps):
                for k in range(1, pairs):
                    copy = remote(
                        ins[a].at[c], a, me, c, y_out.at[k - 1, i], y_in.at[k - 1, i], ahead[k]
                    )
                    copy.start()
                    started.append(copy)
            crossed = []
            for i, (a, c) in enumerate(steps):
                copy = remote(ins[a].at[c], a, me, c, c_out.at[0, i], c_in.at[0, i], partner)
                copy.start()
                crossed.append(copy)
                copy = pltpu.make_async_copy(ins[a].at[c], at(a, me, c), keep.at[i])
                copy.start()
            for i, (a, c) in enumerate(steps):
                for k in range(1, pairs):
                    remote(
                        ins[a].at[c], a, behind[k], c, y_out.at[k - 1, i], y_in.at[k - 1, i], ahead[k]
                    ).wait_recv()
                    copy = remote(
                        at(a, behind[k], c),
                        a,
                        behind[k],
                        c,
                        c_out.at[k, i],
                        c_in.at[k, i],
                        partner,
                    )
                    copy.start()
                    crossed.append(copy)
            for copy in started:
                copy.wait_send()
            for copy in crossed:
                copy.wait()
            for i, (a, c) in enumerate(steps):
                pltpu.make_async_copy(ins[a].at[c], at(a, me, c), keep.at[i]).wait()

        dma = pltpu.SemaphoreType.DMA
        held = max(pairs - 1, 1)
        return self.call(
            kernel,
            blocks,
            shapes,
            [
                dma((total,)),
                dma((held, total)),
                dma((held, total)),
                dma((pairs, total)),
                dma((pairs, total)),
            ],
            "gather_team",
            sum(60 * b.size * 2 for b in blocks),
        )

    def exchange(self, array, out_shape, source, target):
        n = self.n

        def kernel(in_ref, out_ref, keep, out_sem, in_sem):
            me = lax.axis_index("seq")
            core = lax.rem(me, 2)
            peers = [
                lax.rem(me - core + 2 * k, n) + (1 - core if flip else core)
                for k in range(self.pairs)
                for flip in (False, True)
            ]
            self.greet(peers[1:])
            own = pltpu.make_async_copy(source(in_ref, me), target(out_ref, me), keep)
            own.start()
            copies = []
            for k in reversed(range(1, n)):
                copy = pltpu.make_async_remote_copy(
                    src_ref=source(in_ref, peers[k]),
                    dst_ref=target(out_ref, me),
                    send_sem=out_sem.at[k - 1],
                    recv_sem=in_sem.at[k - 1],
                    device_id={"seq": peers[k]},
                    device_id_type=MESH,
                )
                copy.start()
                copies.append(copy)
            for copy in copies:
                copy.wait()
            own.wait()

        dma = pltpu.SemaphoreType.DMA
        return self.call(
            kernel,
            [array],
            [jax.ShapeDtypeStruct(out_shape, array.dtype)],
            [dma, dma((n - 1,)), dma((n - 1,))],
            "exchange_team",
            40 * array.size * 2,
        )[0]

    def scatter(self, parts, dtype):
        chunks, n, rows, columns = parts.shape
        pairs = self.pairs
        held = max(pairs - 1, 1)

        def kernel(in_ref, out_ref, mine, met, sent, come, result, load, c_out, c_in, y_out, y_in, store):
            me = lax.axis_index("seq")
            core = lax.rem(me, 2)
            partner = me + 1 - 2 * core
            ahead = [lax.rem(me + 2 * k, n) for k in range(pairs)]
            self.greet([partner] + ahead[1:])
            order = [(k, c) for k in list(range(1, pairs)) + [0] for c in range(chunks)]

            def read(k, c):
                return pltpu.make_async_copy(in_ref.at[c, ahead[k]], mine.at[k, c], load.at[k, c])

            def cross(k, c):
                return pltpu.make_async_remote_copy(
                    src_ref=in_ref.at[c, lax.rem(partner + 2 * k, n)],
                    dst_ref=met.at[k, c],
                    send_sem=c_out.at[k, c],
                    recv_sem=c_in.at[k, c],
                    device_id={"seq": partner},
                    device_id_type=MESH,
                )

            def pass_on(k, c):
                return pltpu.make_async_remote_copy(
                    src_ref=sent.at[k - 1, c],
                    dst_ref=come.at[k - 1, c],
                    send_sem=y_out.at[k - 1, c],
                    recv_sem=y_in.at[k - 1, c],
                    device_id={"seq": ahead[k]},
                    device_id_type=MESH,
                )

            for k, c in order:
                cross(k, c).start()
                read(k, c).start()
            for k, c in order:
                cross(k, c).wait_recv()
                read(k, c).wait()
                if k:
                    sent[k - 1, c] = (mine[k, c].astype(f32) + met[k, c].astype(f32)).astype(bf16)
                    pass_on(k, c).start()
            for c in range(chunks):
                total = mine[0, c].astype(f32) + met[0, c].astype(f32)
                for k in range(1, pairs):
                    pass_on(k, c).wait_recv()
                    total = total + come[k - 1, c].astype(f32)
                result[c] = total.astype(dtype)
                pltpu.make_async_copy(result.at[c], out_ref.at[c], store.at[c]).start()
            for k, c in order:
                cross(k, c).wait_send()
                if k:
                    pass_on(k, c).wait_send()
            for c in range(chunks):
                pltpu.make_async_copy(result.at[c], out_ref.at[c], store.at[c]).wait()

        dma = pltpu.SemaphoreType.DMA
        block = (chunks, rows, columns)
        return self.call(
            kernel,
            [parts],
            [jax.ShapeDtypeStruct(block, dtype)],
            [
                pltpu.VMEM((pairs,) + block, bf16),
                pltpu.VMEM((pairs,) + block, bf16),
                pltpu.VMEM((held,) + block, bf16),
                pltpu.VMEM((held,) + block, bf16),
                pltpu.VMEM(block, dtype),
                dma((pairs, chunks)),
                dma((pairs, chunks)),
                dma((pairs, chunks)),
                dma((held, chunks)),
                dma((held, chunks)),
                dma((chunks,)),
            ],
            "scatter_team",
            60 * parts.size // n * 2,
        )[0]


def own_columns(weight, me, groups, count, each):
    shard = weight.shape[0]
    per = weight.shape[1] // (groups * count * each)
    if each % 128:
        cut = weight.reshape(shard, groups, count, per, each)
        cut = lax.dynamic_index_in_dim(cut, me, 3, keepdims=False)
        return [cut[:, g].reshape(shard, count * each) for g in range(groups)]

    def kernel(me_ref, *refs):
        for g in range(groups):
            refs[groups + g][...] = refs[g][...]

    def source(g):
        return pl.BlockSpec((shard, each), lambda i, me_ref: (0, (g * count + i) * per + me_ref[0]))

    return pl.pallas_call(
        kernel,
        grid_spec=pltpu.PrefetchScalarGridSpec(
            num_scalar_prefetch=1,
            grid=(count,),
            in_specs=[source(g) for g in range(groups)],
            out_specs=[pl.BlockSpec((shard, each), lambda i, me_ref: (0, i))] * groups,
        ),
        out_shape=[jax.ShapeDtypeStruct((shard, count * each), weight.dtype)] * groups,
        name="own_columns",
    )(me.reshape(1), *([weight] * groups))


def spread_columns(pieces, count, each, block_rows):
    devices, rows, _ = pieces[0].shape
    groups = len(pieces)
    if each % 128:
        cut = jnp.stack(pieces).reshape(groups, devices, rows, count, each)
        return jnp.transpose(cut, (2, 0, 3, 1, 4)).reshape(rows, -1).astype(f32)
    wide = devices * each

    def kernel(in_ref, *refs):
        for j in range(devices):
            refs[-1][:, j * each : (j + 1) * each] = in_ref[j].astype(f32)

    out = None
    for g, piece in enumerate(pieces):
        out = pl.pallas_call(
            kernel,
            grid=(count, rows // block_rows),
            in_specs=[pl.BlockSpec((devices, block_rows, each), lambda i, r: (0, r, i))]
            + ([] if out is None else [pl.BlockSpec(memory_space=pl.ANY)]),
            out_specs=pl.BlockSpec((block_rows, wide), lambda i, r, g=g: (r, g * count + i)),
            out_shape=jax.ShapeDtypeStruct((rows, groups * count * wide), f32),
            input_output_aliases={} if out is None else {1: 0},
            name="spread_columns",
        )(*([piece] if out is None else [piece, out]))
    return out


def mm(left, right):
    return jnp.dot(left, right, preferred_element_type=f32)


def mm_nt(left, right):
    return lax.dot_general(left, right, (((1,), (1,)), ((), ())), preferred_element_type=f32)


def mm_tn(left, right):
    return lax.dot_general(left, right, (((0,), (0,)), ((), ())), preferred_element_type=f32)


def make_body(n_seq, n_fsdp):
    def body(
        tokens,
        cotangent,
        w_qkv,
        w_out,
        w_gate_up,
        w_down,
        gain_attn,
        gain_ffn,
        gate_bias,
        memory_in,
        norms_in,
        resets,
        depth,
    ):
        _, segs, local, width = tokens.shape
        heads = gate_bias.shape[0]
        hdim = width // heads
        my_heads = heads // n_seq
        my_width = width // n_seq
        seg = local * n_seq
        rows = segs * local
        total_rows = segs * seg
        shard = w_qkv.shape[0]
        hidden_shard = w_down.shape[0]
        my_hidden = hidden_shard // n_seq
        out_rows = shard // n_seq
        team = Team(n_seq)
        me = team.me

        (qkv_own,) = own_columns(w_qkv, me, 1, 3, my_width)
        gate_own, up_own = own_columns(w_gate_up, me, 2, n_fsdp, my_hidden)
        down_own = lax.dynamic_slice(w_down, (me * my_hidden, 0), (my_hidden, width))
        out_own = lax.dynamic_slice(w_out, (me * out_rows, 0), (out_rows, width))

        x_flat = tokens.reshape(rows, width).astype(f32)
        r_one = rms(x_flat)
        h_one_own = (r_one * gain_attn).astype(bf16)
        grad_y = cotangent.reshape(rows, width)

        def gather_rows(block):
            return lax.all_gather(block, "fsdp", axis=0, tiled=True)

        def gather_tokens(value):
            (out,) = team.gather([value.reshape(segs, local, width)], False)
            return out.reshape(total_rows, width)

        def scatter_tokens(value):
            return team.scatter(value.reshape(segs, n_seq, local, width), f32).reshape(rows, width)

        w_o = gather_rows(tie(out_own, h_one_own))
        w_q = gather_rows(tie(qkv_own, h_one_own))
        h_one = gather_tokens(h_one_own)
        w_g = gather_rows(tie(gate_own, h_one))
        (whole_o,) = team.gather([tie(w_o, h_one).reshape(n_fsdp, out_rows, width)], False)
        whole_o = whole_o.reshape(width, width)
        w_u = gather_rows(tie(up_own, whole_o))

        qkv = mm(h_one, w_q).astype(bf16)
        gate = jax.nn.sigmoid(lax.dynamic_slice(gate_bias, (me * my_heads,), (my_heads,)))
        memory = lax.dynamic_slice(memory_in[0], (me * my_heads, 0, 0), (my_heads, hdim, hdim))
        norms = lax.dynamic_slice(norms_in[0], (me * my_heads, 0), (my_heads, hdim))
        attn_heads, lse, mems, nrms = attention_forward(qkv, gate, resets[0], memory, norms, segs)

        w_d = gather_rows(tie(down_own, attn_heads))

        def columns_of(ref, i):
            return ref.at[:, :, pl.ds(pl.multiple_of(i * my_width, my_width), my_width)]

        def tokens_of(ref, i):
            return ref.at[:, i]

        attn = team.exchange(
            attn_heads.reshape(segs, n_seq, local, my_width),
            (segs, local, width),
            tokens_of,
            columns_of,
        ).reshape(rows, width)
        x_one = x_flat + mm(attn, whole_o)
        r_two = rms(x_one)
        h_two = gather_tokens((r_two * gain_ffn).astype(bf16))
        grad_y_all = gather_tokens(tie(grad_y, h_two))
        gate_part = mm(h_two, w_g).astype(bf16)
        up_part = mm(h_two, w_u).astype(bf16)
        hidden = swiglu(gate_part.astype(f32), up_part.astype(f32)).astype(bf16)

        def scatter_rows(parts):
            return lax.psum_scatter(parts, "fsdp", scatter_dimension=0, tiled=True)

        down_parts = mm_tn(hidden, grad_y_all).astype(bf16)
        down_term = scatter_rows(down_parts)
        grad_hidden = mm_nt(tie(grad_y_all, down_parts), w_d)
        _, swiglu_back = jax.vjp(swiglu, gate_part.astype(f32), up_part.astype(f32))
        grad_gate, grad_up = swiglu_back(grad_hidden)
        grad_gate, grad_up = grad_gate.astype(bf16), grad_up.astype(bf16)
        gate_parts = mm_tn(h_two, grad_gate).astype(bf16)
        gate_term = scatter_rows(gate_parts)
        up_parts = mm_tn(h_two, tie(grad_up, gate_parts)).astype(bf16)
        up_term = scatter_rows(up_parts)
        grad_gate, grad_up, _ = lax.optimization_barrier((grad_gate, grad_up, up_parts))
        grad_h_two = scatter_tokens((mm_nt(grad_gate, w_g) + mm_nt(grad_up, w_u)).astype(bf16))

        gain_ffn_term = jnp.sum(grad_h_two * r_two, axis=0)
        _, norm_two_back = jax.vjp(rms, x_one)
        grad_x_one = grad_y.astype(f32) + norm_two_back(grad_h_two * gain_ffn)[0]
        grad_o = grad_x_one.astype(bf16)

        grad_attn_parts = mm_nt(grad_o, whole_o).astype(bf16)
        grad_attn = team.exchange(
            grad_attn_parts.reshape(segs, local, width),
            (segs, n_seq, local, my_width),
            columns_of,
            tokens_of,
        ).reshape(total_rows, my_width)
        grads_q, grads_k, grads_v, bias_terms = attention_backward(
            qkv, grad_attn, gate, resets[0], depth, lse, mems, nrms, segs
        )
        grad_qkv_rows = jnp.concatenate([grads_q, grads_k, grads_v], axis=1)
        qkv_parts = mm_tn(h_one, grad_qkv_rows).astype(bf16)
        qkv_term = scatter_rows(tie(qkv_parts, gate_term))

        out_parts = mm_tn(attn, tie(grad_o, qkv_parts)).astype(bf16)
        out_sum = team.scatter(out_parts.reshape(n_fsdp, n_seq, out_rows, width), bf16)
        out_term = scatter_rows(tie(out_sum, up_term).reshape(-1, width))
        grad_qkv_rows = tie(grad_qkv_rows, qkv_parts)
        grad_h_one = scatter_tokens(mm_nt(grad_qkv_rows, w_q).astype(bf16))
        output = x_one + scatter_tokens(mm(tie(hidden, grad_h_one), w_d).astype(bf16))
        output = output.astype(bf16).reshape(tokens.shape)
        gain_attn_term = jnp.sum(grad_h_one * r_one, axis=0)
        _, norm_one_back = jax.vjp(rms, x_flat)
        grad_x = grad_x_one + norm_one_back(grad_h_one * gain_attn)[0]
        input_grad = grad_x.astype(bf16).reshape(tokens.shape)

        (down_all,) = team.gather([down_term[None]], True)
        (gate_all,) = team.gather([gate_term[None]], True)
        (up_all,) = team.gather([up_term[None]], True)
        qkv_all, out_all = team.gather([qkv_term[None], out_term[None]], True)
        down_all = down_all.reshape(hidden_shard, width).astype(f32)
        out_all = out_all.reshape(shard, width).astype(f32)
        gate_up_all = spread_columns([gate_all[:, 0], up_all[:, 0]], n_fsdp, my_hidden, shard)
        qkv_all = spread_columns([qkv_all[:, 0]], 3, my_width, shard // 2)

        bias_all = lax.dynamic_update_slice(
            jnp.zeros((heads,), f32), bias_terms[:, 0, 0], (me * my_heads,)
        )
        small = jnp.concatenate([gain_attn_term, gain_ffn_term, bias_all])
        for axis, n in (("seq", n_seq), ("fsdp", n_fsdp)):
            k = 1
            while k < n:
                small = small + lax.ppermute(small, axis, [(i, i ^ k) for i in range(n)])
                k *= 2
        return (
            output,
            input_grad,
            qkv_all,
            out_all,
            gate_up_all,
            down_all,
            small[:width],
            small[width : 2 * width],
            small[2 * width :],
        )

    return body


def solution(mesh):
    rows = P("fsdp", None)
    tokens = P("fsdp", None, "seq", None)
    body = make_body(mesh.shape["seq"], mesh.shape["fsdp"])
    return jax.shard_map(
        body,
        mesh=mesh,
        in_specs=(
            tokens,
            tokens,
            rows,
            rows,
            rows,
            rows,
            P(),
            P(),
            P(),
            P("fsdp", None, None, None),
            P("fsdp", None, None),
            rows,
            P("fsdp"),
        ),
        out_specs=(tokens, tokens, rows, rows, rows, rows, P(), P(), P()),
        check_vma=False,
    )
```

time: 2040 us -> 1320 us (0.65)
  Pallas kernels: 0 us -> 652 us
  local copies, waits for them, and re-layouts: 632 us -> 34.4 us
  waiting for transfers between devices: 499 us -> 269 us
  matrix products: 476 us -> 309 us
  other arithmetic: 176 us -> 22.3 us
  starting transfers between devices: 144 us -> 5.05 us
  blocking collectives: 38.8 us -> 0 us
  between operations: 44.7 us -> 16.6 us
    pallas_call x0 -> x21, Pallas kernels: none -> 652 us  [the longest x14 569 us: call(): pl.pallas_call(kernel, in_specs=[anywhere] * len(inputs), out_specs=[anyw...]
    ppermute x154 -> x5, waiting for transfers between devices: 499 us -> 2.85 us  [body(): small = small + lax.ppermute(small, axis, [(i, i ^ k) for i in range(n)])]
    dynamic_update_slice x100 -> x1, local copies, waits for them, and re-layouts: 360 us -> 0.23 us  [body(): lax.dynamic_update_slice(jnp.zeros((heads,), f32), bias_terms[:, 0, 0], (...]
    dot_general x33 -> x0, matrix products: 176 us -> none  [the longest x2 24.3 us: body(): jnp.einsum('qhd,khd->hqk', grad_adot, value, preferred_element_type=f32)]
    all_gather x0 -> x5, waiting for transfers between devices: none -> 158 us  [gather_rows(): return lax.all_gather(block, 'fsdp', axis=0, tiled=True)]
    ppermute x154 -> x5, starting transfers between devices: 144 us -> 4.44 us  [body(): small = small + lax.ppermute(small, axis, [(i, i ^ k) for i in range(n)])]
    reduce_scatter x0 -> x5, waiting for transfers between devices: none -> 107 us  [scatter_rows(): return lax.psum_scatter(parts, 'fsdp', scatter_dimension=0, tiled=True)]
    convert_element_type x69 -> x4, other arithmetic: 103 us -> 8.15 us  [the longest x1 4.75 us: body(): down_all = down_all.reshape(hidden_shard, width).astype(f32)]
  transfers between devices with their start and end apart: 154 -> 15, of which waited for: 65 -> 7; matrix products, arithmetic and copies ran while one was open for 49% -> 19% of each run, Pallas kernels for 0% -> 47%
where the time goes in v2:
time: 1320 us; the launch traced here: 1310 us
  Pallas kernels  652 us (49%)
  matrix products  309 us (23%)
  waiting for transfers between devices  269 us (20%)
  local copies, waits for them, and re-layouts  34.4 us (3%)
  other arithmetic  22.3 us (2%)
  between operations  16.6 us (1%)
    pallas_call x14, Pallas kernels, call(): pl.pallas_call(kernel, in_specs=[anywhere] * len(inputs), out_specs=[anyw...  569 us
    all_gather x5, waiting for transfers between devices, gather_rows(): return lax.all_gather(block, 'fsdp', axis=0, tiled=True)  158 us
    dot_general x5, matrix products, mm_nt(): lax.dot_general(left, right, (((1,), (1,)), ((), ())), preferred_element_...  112 us
    reduce_scatter x5, waiting for transfers between devices, scatter_rows(): return lax.psum_scatter(parts, 'fsdp', scatter_dimension=0, tiled=True)  107 us
    dot_general x5, matrix products, mm(): return jnp.dot(left, right, preferred_element_type=f32)  103 us
    dot_general x5, matrix products, mm_tn(): lax.dot_general(left, right, (((0,), (0,)), ((), ())), preferred_element_...  93.6 us
    pallas_call x1, Pallas kernels, attention_backward(): pl.pallas_call(functools.partial(backward_kernel, min(256, seg), segs), g...  33.9 us
    unnamed x94, local copies, waits for them, and re-layouts  27.5 us
  transfers between devices with their start and end apart: 15, of which 7 were waited for; matrix products, arithmetic and copies ran while one was open for 19% of the time, Pallas kernels for 47%

profile of v2, /device:TPU:0, one launch (start us, length us, event | category | flops | bytes accessed | tf_op | source)
XLA Modules:
  0.0 1308.7 jit_solution(7189525813084613073)
XLA Ops:
  20.8 52.2 %gather_team.8 = bf16[2,4,256,2048]{3,2,1,0:T(8,128)(2,1)} custom-call(bf16[2,256,2048]{2,1,0:T(8,128)(2,1)S(1)} %fusion.15.refs_0_), custom_call_target="tpu_custom_call" | custom-call | bytes 125829120 | tf_op jit(solution)/shard_map/gather_team/pallas_call | solution.py:316
  74.9 50.1 %gather_team.9 = bf16[8,4,64,2048]{3,2,1,0:T(8,128)(2,1)} custom-call(bf16[8,64,2048]{2,1,0:T(8,128)(2,1)S(1)} %bitcast.129), custom_call_target="tpu_custom_call" | custom-call | bytes 125829120 | tf_op jit(solution)/shard_map/gather_team/pallas_call | solution.py:316
  129.8 34.0 %all-gather.6.cloned.1.call-done = bf16[2048,1536]{1,0:T(8,128)(2,1)} async-done(((bf16[256,1536]{1,0:T(8,128)(2,1)}), bf16[2048,1536]{1,0:T(8,128)(2,1)}) %all-gather.6.cloned.1.call-update) | async-done | bytes 6291472 | tf_op jit(solution)/shard_map/all_gather | solution.py:657
  163.8 18.6 %convolution_convert_fusion.8.q_ref.k_ref.v_ref = bf16[2048,1536]{1,0:T(8,128)(2,1)} fusion(bf16[2048,2048]{1,0:T(8,128)(2,1)} %bitcast.141, bf16[2048,1536]{1,0:T(8,128)(2,1)} %all-gather.6.cloned.1.call-done), kind=kOutput, calls=%fused_computation.23 | convolution fusion | flops 12888047616 | bytes 20971520 | tf_op jit(solution)/shard_map/dot_general | solution.py:604
  182.3 19.8 %attention_forward.1 = (bf16[2048,512]{1,0:T(8,128)(2,1)S(1)}, f32[4,2,1,1024]{3,2,1,0:T(1,128)S(1)}, f32[4,2,128,128]{3,2,1,0:T(8,128)S(1)}, f32[4,2,1,128]{3,2,1,0:T(1,128)S(1)}) custom-call(f32[4]{0:T(128)S(1)} %add_divide_fusion.gate, s32[1]{0:T(128)} %bitcast.121.resets, bf16[2048,1536]{1,0:T(8,128)(2,1)} %convolution_convert_fusion.8.q_ref.k_ref.v_ref, ...), custom_call_target="tpu_custom_call" | custom-call | flops 4026531840 | bytes 12582912 | tf_op jit(solution)/shard_map/attention_forward/pallas_call | solution.py:133
  202.4 25.7 %exchange_team.2 = bf16[2,256,2048]{2,1,0:T(8,128)(2,1)S(1)} custom-call(bf16[2,4,256,512]{3,2,1,0:T(8,128)(2,1)S(1)} %bitcast.132), custom_call_target="tpu_custom_call" | custom-call | bytes 83886080 | tf_op jit(solution)/shard_map/exchange_team/pallas_call | solution.py:316
  239.9 50.7 %gather_team.10 = bf16[2,4,256,2048]{3,2,1,0:T(8,128)(2,1)} custom-call(bf16[2,256,2048]{2,1,0:T(8,128)(2,1)S(1)} %bitcast.126), custom_call_target="tpu_custom_call" | custom-call | bytes 125829120 | tf_op jit(solution)/shard_map/gather_team/pallas_call | solution.py:316
  290.6 50.8 %gather_team.11 = bf16[2,4,256,2048]{3,2,1,0:T(8,128)(2,1)} custom-call(bf16[2,256,2048]{2,1,0:T(8,128)(2,1)S(1)} %bitcast.123), custom_call_target="tpu_custom_call" | custom-call | bytes 125829120 | tf_op jit(solution)/shard_map/gather_team/pallas_call | solution.py:316
  341.5 24.2 %convolution_convert_fusion.7 = bf16[2048,2048]{1,0:T(8,128)(2,1)} fusion(bf16[2048,2048]{1,0:T(8,128)(2,1)} %bitcast.147, bf16[2048,2048]{1,0:T(8,128)(2,1)} %all-gather.10.cloned.1.call-done), kind=kOutput, calls=%fused_computation.22 | convolution fusion | flops 17184063488 | bytes 25165824 | tf_op jit(solution)/shard_map/dot_general | solution.py:604
  365.7 49.6 %all-gather.12.cloned.1.call-done = bf16[2048,2048]{1,0:T(8,128)(2,1)} async-done(((bf16[256,2048]{1,0:T(8,128)(2,1)}), bf16[2048,2048]{1,0:T(8,128)(2,1)}) %all-gather.12.cloned.1.call-update) | async-done | bytes 8388624 | tf_op jit(solution)/shard_map/all_gather | solution.py:657
  415.3 26.8 %fusion = (bf16[2048,2048]{1,0:T(8,128)(2,1)S(1)}, bf16[2048,2048]{1,0:T(8,128)(2,1)}) fusion(bf16[2048,2048]{1,0:T(8,128)(2,1)} %convolution_convert_fusion.7, bf16[2048,2048]{1,0:T(8,128)(2,1)} %bitcast.148, bf16[2048,2048]{1,0:T(8,128)(2,1)} %all-gather.12.cloned.1.call-done), kind=kOutput, calls=%fused_computation.6 | convolution fusion | flops 17217617920 | bytes 41943040 | tf_op jit(solution)/shard_map/dot_general | solution.py:604
  445.3 20.6 %convolution_convert_fusion.5 = bf16[2048,2048]{1,0:T(8,128)(2,1)} fusion(bf16[2048,2048]{1,0:T(8,128)(2,1)S(1)} %get-tuple-element.58, bf16[2048,2048]{1,0:T(8,128)(2,1)S(1)} %bitcast.152), kind=kOutput, calls=%fused_computation.20 | convolution fusion | flops 17184063488 | bytes 25165824 | tf_op jit(solution)/shard_map/dot_general | solution.py:612
  465.9 74.4 %all-gather.14.cloned.1.call-done = bf16[2048,2048]{1,0:T(8,128)(2,1)} async-done(((bf16[256,2048]{1,0:T(8,128)(2,1)}), bf16[2048,2048]{1,0:T(8,128)(2,1)}) %all-gather.14.cloned.1.call-update) | async-done | bytes 8388624 | tf_op jit(solution)/shard_map/all_gather | solution.py:657
  540.4 32.6 %multiply_convert_fusion = (bf16[2048,2048]{1,0:T(8,128)(2,1)}, bf16[2048,2048]{1,0:T(8,128)(2,1)}) fusion(bf16[2048,2048]{1,0:T(8,128)(2,1)} %convolution_convert_fusion.7, bf16[2048,2048]{1,0:T(8,128)(2,1)} %get-tuple-element.78, bf16[2048,2048]{1,0:T(8,128)(2,1)} %bitcast.151, bf16[2048,2048]{1,0:T(8,128)(2,1)} %all-gather.14.cloned.1.call-done), kind=kOutput, calls=%fused_computation.14 | convolution fusion | flops 17246978048 | bytes 50331648 | tf_op jit(solution)/shard_map/dot_general | solution.py:608
  573.0 23.7 %convolution_convert_fusion.4 = bf16[2048,2048]{1,0:T(8,128)(2,1)} fusion(bf16[2048,2048]{1,0:T(8,128)(2,1)} %bitcast.149, bf16[2048,2048]{1,0:T(8,128)(2,1)} %get-tuple-element.49), kind=kOutput, calls=%fused_computation.19 | convolution fusion | flops 17184063488 | bytes 25165824 | tf_op jit(solution)/shard_map/dot_general | solution.py:612
  596.7 23.8 %convolution_convert_fusion.3 = bf16[2048,2048]{1,0:T(8,128)(2,1)} fusion(bf16[2048,2048]{1,0:T(8,128)(2,1)} %bitcast.150, bf16[2048,2048]{1,0:T(8,128)(2,1)} %get-tuple-element.50), kind=kOutput, calls=%fused_computation.18 | convolution fusion | flops 17184063488 | bytes 25165824 | tf_op jit(solution)/shard_map/dot_general | solution.py:612
  622.7 25.3 %fusion.26 = f32[2048,2048]{1,0:T(8,128)} fusion(bf16[2048,2048]{1,0:T(8,128)(2,1)} %get-tuple-element.49, bf16[2048,2048]{1,0:T(8,128)(2,1)} %all-gather.10.cloned.1.call-done), kind=kOutput, calls=%fused_computation.75 | convolution fusion | flops 17179869184 | bytes 33554432 | tf_op jit(solution)/shard_map/dot_general | solution.py:608
  648.0 25.6 %add_convert_fusion = bf16[2048,2048]{1,0:T(8,128)(2,1)} fusion(f32[2048,2048]{1,0:T(8,128)} %fusion.26, bf16[2048,2048]{1,0:T(8,128)(2,1)} %get-tuple-element.50, bf16[2048,2048]{1,0:T(8,128)(2,1)} %all-gather.12.cloned.1.call-done), kind=kOutput, calls=%fused_computation.13 | convolution fusion | flops 17188257792 | bytes 41943040 | tf_op jit(solution)/shard_map/dot_general | solution.py:608
  673.6 51.8 %scatter_team.4 = f32[2,256,2048]{2,1,0:T(8,128)S(1)} custom-call(bf16[2,4,256,2048]{3,2,1,0:T(8,128)(2,1)} %bitcast.155), custom_call_target="tpu_custom_call" | custom-call | bytes 125829120 | tf_op jit(solution)/shard_map/scatter_team/pallas_call | solution.py:316
  738.8 25.7 %exchange_team.3 = bf16[2,4,256,512]{3,2,1,0:T(8,128)(2,1)S(1)} custom-call(bf16[2,256,2048]{2,1,0:T(8,128)(2,1)S(1)} %bitcast.134), custom_call_target="tpu_custom_call" | custom-call | bytes 83886080 | tf_op jit(solution)/shard_map/exchange_team/pallas_call | solution.py:316
  765.9 33.9 %attention_backward.1 = (bf16[2048,512]{1,0:T(8,128)(2,1)S(1)}, bf16[2048,512]{1,0:T(8,128)(2,1)S(1)}, bf16[2048,512]{1,0:T(8,128)(2,1)}, f32[4,8,128]{2,1,0:T(8,128)S(1)}) custom-call(f32[4]{0:T(128)S(1)} %add_divide_fusion.gate, s32[1]{0:T(128)} %bitcast.122.resets, s32[1]{0:T(128)S(6)} %copy.30.depth, ...), custom_call_target="tpu_custom_call" | custom-call | flops 8053063680 | bytes 12582912 | tf_op jit(solution)/shard_map/attention_backward/pallas_call | solution.py:266
  829.7 50.2 %scatter_team.7 = bf16[8,64,2048]{2,1,0:T(8,128)(2,1)S(1)} custom-call(bf16[8,4,64,2048]{3,2,1,0:T(8,128)(2,1)} %bitcast.153), custom_call_target="tpu_custom_call" | custom-call | bytes 125829120 | tf_op jit(solution)/shard_map/scatter_team/pallas_call | solution.py:316
  881.3 38.7 %reduce-scatter.6.cloned.1.call-done = bf16[256,2048]{1,0:T(8,128)(2,1)} async-done(((bf16[2048,2048]{1,0:T(8,128)(2,1)}), bf16[256,2048]{1,0:T(8,128)(2,1)}) %reduce-scatter.6.cloned.1.call-update) | async-done | bytes 1048592 | tf_op jit(solution)/shard_map/reduce_scatter | solution.py:703
  920.0 19.5 %convolution_convert_fusion.2 = bf16[2048,2048]{1,0:T(8,128)(2,1)} fusion(bf16[2048,1536]{1,0:T(8,128)(2,1)} %copy-done.27, bf16[2048,1536]{1,0:T(8,128)(2,1)} %all-gather.6.cloned.1.call-done), kind=kOutput, calls=%fused_computation.17 | convolution fusion | flops 12889096192 | bytes 20971520 | tf_op jit(solution)/shard_map/dot_general | solution.py:608
  939.5 51.4 %scatter_team.5 = f32[2,256,2048]{2,1,0:T(8,128)S(1)} custom-call(bf16[2,4,256,2048]{3,2,1,0:T(8,128)(2,1)} %bitcast.156), custom_call_target="tpu_custom_call" | custom-call | bytes 125829120 | tf_op jit(solution)/shard_map/scatter_team/pallas_call | solution.py:316
  999.3 24.5 %convolution_convert_fusion.1 = bf16[2048,2048]{1,0:T(8,128)(2,1)} fusion(bf16[2048,2048]{1,0:T(8,128)(2,1)} %copy-done.42, bf16[2048,2048]{1,0:T(8,128)(2,1)} %all-gather.14.cloned.1.call-done), kind=kOutput, calls=%fused_computation.16 | convolution fusion | flops 17184063488 | bytes 25165824 | tf_op jit(solution)/shard_map/dot_general | solution.py:604
  1027.7 50.9 %scatter_team.6 = f32[2,256,2048]{2,1,0:T(8,128)S(1)} custom-call(bf16[2,4,256,2048]{3,2,1,0:T(8,128)(2,1)} %bitcast.154), custom_call_target="tpu_custom_call" | custom-call | bytes 125829120 | tf_op jit(solution)/shard_map/scatter_team/pallas_call | solution.py:316
  1088.9 27.5 %gather_team.15 = bf16[4,1,256,2048]{3,2,1,0:T(8,128)(2,1)S(1)} custom-call(bf16[1,256,2048]{2,1,0:T(8,128)(2,1)S(1)} %bitcast.137), custom_call_target="tpu_custom_call" | custom-call | bytes 62914560 | tf_op jit(solution)/shard_map/gather_team/pallas_call | solution.py:316
  1121.2 27.8 %gather_team.14 = bf16[4,1,256,2048]{3,2,1,0:T(8,128)(2,1)S(1)} custom-call(bf16[1,256,2048]{2,1,0:T(8,128)(2,1)S(1)} %bitcast.136), custom_call_target="tpu_custom_call" | custom-call | bytes 62914560 | tf_op jit(solution)/shard_map/gather_team/pallas_call | solution.py:316
  1150.9 27.8 %gather_team.13 = bf16[4,1,256,2048]{3,2,1,0:T(8,128)(2,1)S(1)} custom-call(bf16[1,256,2048]{2,1,0:T(8,128)(2,1)S(1)} %bitcast.135), custom_call_target="tpu_custom_call" | custom-call | bytes 62914560 | tf_op jit(solution)/shard_map/gather_team/pallas_call | solution.py:316
  1195.5 68.2 %reduce-scatter.8.cloned.1.call-done = bf16[256,1536]{1,0:T(8,128)(2,1)} async-done(((bf16[2048,1536]{1,0:T(8,128)(2,1)}), bf16[256,1536]{1,0:T(8,128)(2,1)}) %reduce-scatter.8.cloned.1.call-update) | async-done | bytes 786448 | tf_op jit(solution)/shard_map/reduce_scatter | solution.py:703
  1265.7 26.6 %gather_team.12 = (bf16[4,1,256,1536]{3,2,1,0:T(8,128)(2,1)S(1)}, bf16[4,1,64,2048]{3,2,1,0:T(8,128)(2,1)S(1)}) custom-call(bf16[1,256,1536]{2,1,0:T(8,128)(2,1)S(1)} %bitcast.138, bf16[1,64,2048]{2,1,0:T(8,128)(2,1)S(1)} %bitcast.139), custom_call_target="tpu_custom_call" | custom-call | bytes 62914560 | tf_op jit(solution)/shard_map/gather_team/pallas_call | solution.py:316
  (171 shorter events, 139.3 us)
Async XLA Ops:
  7.2 65.9 %all-gather.8.cloned.1.call-start = ((), (), s32[]{:S(2)}) async-start(), calls=%async_computation.6 | async-start | bytes 2359296 | tf_op jit(solution)/shard_map/all_gather | solution.py:657
  11.3 152.4 %all-gather.6.cloned.1.call-start = ((), (), s32[]{:S(2)}) async-start(), calls=%async_computation.5 | async-start | bytes 7077888 | tf_op jit(solution)/shard_map/all_gather | solution.py:657
  14.3 327.2 %all-gather.10.cloned.1.call-start = ((), (), s32[]{:S(2)}) async-start(), calls=%async_computation.7 | async-start | bytes 9437184 | tf_op jit(solution)/shard_map/all_gather | solution.py:657
  73.0 52.7 %copy-start.41 = (f32[16]{0:T(128)S(1)}, f32[16]{0:T(128)}, u32[]{:S(2)}) copy-start(f32[16]{0:T(128)} %param.21) | copy-start | bytes 196
  73.0 342.2 %all-gather.12.cloned.1.call-start = ((), (), s32[]{:S(2)}) async-start(), calls=%async_computation.8 | async-start | bytes 9437184 | tf_op jit(solution)/shard_map/all_gather | solution.py:657
  124.9 415.4 %all-gather.14.cloned.1.call-start = ((), (), s32[]{:S(2)}) async-start(), calls=%async_computation.9 | async-start | bytes 9437184 | tf_op jit(solution)/shard_map/all_gather | solution.py:657
  202.1 679.2 %reduce-scatter.10.cloned.1.call-start = ((), (), s32[]{:S(2)}) async-start(), calls=%async_computation.12 | async-start | bytes 9437184 | tf_op jit(solution)/shard_map/reduce_scatter | solution.py:703
  237.5 53.1 %copy-start.39 = (f32[512]{0:T(512)}, f32[512]{0:T(512)S(1)}, u32[]{:S(2)}) copy-start(f32[512]{0:T(512)S(1)} %get-tuple-element.75) | copy-start | bytes 6148
  237.6 53.1 %copy-start.32 = (f32[512]{0:T(512)}, f32[512]{0:T(512)S(1)}, u32[]{:S(2)}) copy-start(f32[512]{0:T(512)S(1)} %fusion.20) | copy-start | bytes 6148
  239.9 50.7 %copy-start.6 = (bf16[1,2,256,2048]{3,2,1,0:T(8,128)(2,1)S(1)}, bf16[1,2,256,2048]{3,2,1,0:T(8,128)(2,1)}, u32[]{:S(2)}) copy-start(bf16[1,2,256,2048]{3,2,1,0:T(8,128)(2,1)} %param.14) | copy-start | bytes 6291460
  415.3 30.1 %copy-start.24 = (bf16[2,4,256,2048]{3,2,1,0:T(8,128)(2,1)S(1)}, bf16[2,4,256,2048]{3,2,1,0:T(8,128)(2,1)}, u32[]{:S(2)}) copy-start(bf16[2,4,256,2048]{3,2,1,0:T(8,128)(2,1)} %gather_team.11) | copy-start | bytes 25165828
  620.5 299.5 %reduce-scatter.6.cloned.1.call-start = ((), (), s32[]{:S(2)}) async-start(), calls=%async_computation.10 | async-start | bytes 9437184 | tf_op jit(solution)/shard_map/reduce_scatter | solution.py:703
  621.3 466.3 %reduce-scatter.14.cloned.1.call-start = ((), (), s32[]{:S(2)}) async-start(), calls=%async_computation.14 | async-start | bytes 9437184 | tf_op jit(solution)/shard_map/reduce_scatter | solution.py:703
  622.0 573.4 %reduce-scatter.12.cloned.1.call-start = ((), (), s32[]{:S(2)}) async-start(), calls=%async_computation.13 | async-start | bytes 2359296 | tf_op jit(solution)/shard_map/reduce_scatter | solution.py:703
  673.6 51.8 %copy-start.21 = (f32[512,2048]{1,0:T(8,128)S(1)}, f32[512,2048]{1,0:T(8,128)}, u32[]{:S(2)}) copy-start(f32[512,2048]{1,0:T(8,128)} %copy-done.20) | copy-start | bytes 12582916
  673.6 51.8 %copy-start.29 = (f32[2048]{0:T(1024)S(1)}, f32[2048]{0:T(1024)}, u32[]{:S(2)}) copy-start(f32[2048]{0:T(1024)} %param.20) | copy-start | bytes 24580
  673.6 51.8 %copy-start.33 = (f32[512]{0:T(512)S(1)}, f32[512]{0:T(512)}, u32[]{:S(2)}) copy-start(f32[512]{0:T(512)} %copy-done.32) | copy-start | bytes 6148
  729.9 74.4 %slice-start = ((s8[8388608]{0:T(1024)(128)(4,1)}), s8[4194304]{0:T(1024)(128)(4,1)S(1)}, s32[]{:S(2)}) async-start(s8[8388608]{0:T(1024)(128)(4,1)} %bitcast.142), calls=%async_computation.15 | async-start | bytes 8388608
  765.9 38.4 %slice-start.1 = ((s8[8388608]{0:T(1024)(128)(4,1)}), s8[4194304]{0:T(1024)(128)(4,1)S(1)}, s32[]{:S(2)}) async-start(s8[8388608]{0:T(1024)(128)(4,1)} %bitcast.142), calls=%async_computation.16 | async-start | bytes 8388608
  881.3 382.4 %reduce-scatter.8.cloned.1.call-start = ((), (), s32[]{:S(2)}) async-start(), calls=%async_computation.11 | async-start | bytes 7077888 | tf_op jit(solution)/shard_map/reduce_scatter | solution.py:703
  939.5 53.8 %copy-start.35 = (f32[2,256]{1,0:T(2,128)S(1)}, f32[2,256]{1,0:T(2,128)}, u32[]{:S(2)}) copy-start(f32[2,256]{1,0:T(2,128)} %copy-done.34) | copy-start | bytes 6148
  996.9 1.3 collective-permute-start
  998.2 27.2 %copy-start.5 = (f32[2,256,2048]{2,1,0:T(8,128)S(1)}, f32[2,256,2048]{2,1,0:T(8,128)}, u32[]{:S(2)}) copy-start(f32[2,256,2048]{2,1,0:T(8,128)} %copy-done.4) | copy-start | bytes 12582916
  998.2 27.2 %copy-start.23 = (bf16[1,2,256,2048]{3,2,1,0:T(8,128)(2,1)S(1)}, bf16[1,2,256,2048]{3,2,1,0:T(8,128)(2,1)}, u32[]{:S(2)}) copy-start(bf16[1,2,256,2048]{3,2,1,0:T(8,128)(2,1)} %param.13) | copy-start | bytes 6291460
  998.2 27.2 %copy-start.31 = (f32[2048]{0:T(1024)S(1)}, f32[2048]{0:T(1024)}, u32[]{:S(2)}) copy-start(f32[2048]{0:T(1024)} %param.19) | copy-start | bytes 24580
  998.2 25.6 %collective-permute-start.1 = (f32[4112]{0:T(1024)S(1)}, f32[4112]{0:T(1024)S(1)}, u32[]{:S(2)}, u32[]{:S(2)}) collective-permute-start(f32[4112]{0:T(1024)S(1)} %fusion.23), channel_id=1, source_target_pairs={{0,16},{8,24},{16,0},{24,8},{1,17},{9,25},{17,1},{25,9},{2,18},{10... | collective-permute-start | bytes 49352 | tf_op jit(solution)/shard_map/ppermute | solution.py:765
  1023.8 3.8 collective-permute-start.2
  1027.7 51.0 %collective-permute-start.3 = (f32[4112]{0:T(1024)S(1)}, f32[4112]{0:T(1024)S(1)}, u32[]{:S(2)}, u32[]{:S(2)}) collective-permute-start(f32[4112]{0:T(1024)S(1)} %add.102), channel_id=1, source_target_pairs={{0,2},{1,3},{2,0},{3,1},{4,6},{5,7},{6,4},{7,5},{8,10},{9,11},{10,... | collective-permute-start | bytes 49352 | tf_op jit(solution)/shard_map/ppermute | solution.py:765
  1027.7 52.7 %copy-start.3 = (f32[2,256,2048]{2,1,0:T(8,128)S(1)}, f32[2,256,2048]{2,1,0:T(8,128)}, u32[]{:S(2)}) copy-start(f32[2,256,2048]{2,1,0:T(8,128)} %copy-done.2) | copy-start | bytes 12582916
  1027.7 52.7 %copy-start.38 = (f32[512]{0:T(512)S(1)}, f32[512]{0:T(512)}, u32[]{:S(2)}) copy-start(f32[512]{0:T(512)} %rsqrt.26) | copy-start | bytes 6148
  1078.7 7.8 collective-permute-start.4
  1116.4 34.6 %copy-start.15 = (bf16[256,2048]{1,0:T(8,128)(2,1)S(1)}, bf16[256,2048]{1,0:T(8,128)(2,1)}, u32[]{:S(2)}) copy-start(bf16[256,2048]{1,0:T(8,128)(2,1)} %reduce-scatter.10.cloned.1.call-done) | copy-start | bytes 3145732
  (28 other events, 106.2 us)
Sparse Core Ops, SparseCore 0:
  11.4 51.9 all-gather.7
  66.2 97.5 all-gather.5
  166.5 123.0 all-gather.9
  292.1 123.0 all-gather.11
  417.2 123.1 all-gather.13
  620.7 147.2 reduce-scatter.9
  772.0 148.0 reduce-scatter.5
  923.6 147.9 reduce-scatter.13
  1076.2 66.5 reduce-scatter.11
  1146.7 116.9 reduce-scatter.7

commit v3 on v2

--- a/solution.py
+++ b/solution.py
@@ -301,248 +301,329 @@
 
 
 MESH = pl.DeviceIdType.MESH
-
-
-class Team:
-    def __init__(self, n):
-        self.n = n
-        self.pairs = n // 2
-        self.me = lax.axis_index("seq")
+dma = pltpu.SemaphoreType.DMA
+
+
+class Axis:
+    def __init__(self, name, rows, cols):
+        self.name, self.rows, self.cols = name, rows, cols
+        self.size = rows * cols
+
+    def at(self, down, right):
+        me = lax.axis_index(self.name)
+        row, col = me // self.cols, lax.rem(me, self.cols)
+        return lax.rem(row + down, self.rows) * self.cols + lax.rem(col + right, self.cols)
+
+    def to(self, down, right):
+        return {"device_id": {self.name: self.at(down, right)}, "device_id_type": MESH}
+
+
+class Gather:
+    def __init__(self, axis, block, outer):
+        self.axis, self.outer, self.inputs = axis, outer, [block]
+        n, self.chunks = axis.size, block.shape[0]
+        lead = (n, self.chunks) if outer else (self.chunks, n)
+        self.outputs = [jax.ShapeDtypeStruct(lead + block.shape[1:], block.dtype)]
+        held, others = max(axis.rows - 1, 1), axis.cols - 1
+        row, col = (held, self.chunks), (others, axis.rows, self.chunks)
+        self.scratch = [dma((self.chunks,)), dma(row), dma(row), dma(col), dma(col)]
+        self.peers = [(k, 0) for k in range(1, axis.rows)] + [(0, j) for j in range(1, axis.cols)]
+        self.bytes = block.size * 2
+
+    def bind(self, ins, outs, scratch):
+        (self.src,), (self.dst,) = ins, outs
+        self.keep, self.row_out, self.row_in, self.col_out, self.col_in = scratch
+
+    def place(self, dev, c):
+        return self.dst.at[dev, c] if self.outer else self.dst.at[c, dev]
+
+    def along(self, k, c):
+        axis = self.axis
+        return pltpu.make_async_remote_copy(
+            src_ref=self.src.at[c],
+            dst_ref=self.place(axis.at(0, 0), c),
+            send_sem=self.row_out.at[k - 1, c],
+            recv_sem=self.row_in.at[k - 1, c],
+            **axis.to(k, 0),
+        )
+
+    def across(self, k, j, c):
+        axis = self.axis
+        spot = self.place(axis.at((axis.rows - k) % axis.rows, 0), c)
+        return pltpu.make_async_remote_copy(
+            src_ref=self.src.at[c] if k == 0 else spot,
+            dst_ref=spot,
+            send_sem=self.col_out.at[j - 1, k, c],
+            recv_sem=self.col_in.at[j - 1, k, c],
+            **axis.to(0, j),
+        )
+
+    def own(self, c):
+        return pltpu.make_async_copy(
+            self.src.at[c], self.place(self.axis.at(0, 0), c), self.keep.at[c]
+        )
+
+    def start(self):
+        for c in range(self.chunks):
+            for k in range(1, self.axis.rows):
+                self.along(k, c).start()
+        for c in range(self.chunks):
+            for j in range(1, self.axis.cols):
+                self.across(0, j, c).start()
+            self.own(c).start()
+
+    def middle(self, part, parts):
+        for c in range(self.chunks * part // parts, self.chunks * (part + 1) // parts):
+            for k in range(1, self.axis.rows):
+                self.along(k, c).wait_recv()
+                for j in range(1, self.axis.cols):
+                    self.across(k, j, c).start()
+
+    def finish(self):
+        for c in range(self.chunks):
+            for k in range(1, self.axis.rows):
+                self.along(k, c).wait_send()
+            for k in range(self.axis.rows):
+                for j in range(1, self.axis.cols):
+                    self.across(k, j, c).wait()
+            self.own(c).wait()
+
+
+class Exchange:
+    def __init__(self, axis, array, shape, source, target):
+        self.axis, self.inputs = axis, [array]
+        self.outputs = [jax.ShapeDtypeStruct(shape, array.dtype)]
+        self.source, self.target = source, target
+        n = axis.size
+        self.scratch = [dma, dma((n - 1,)), dma((n - 1,))]
+        self.peers = [(k, j) for k in range(axis.rows) for j in range(axis.cols)][1:]
+        self.bytes = array.size
+
+    def bind(self, ins, outs, scratch):
+        (self.src,), (self.dst,) = ins, outs
+        self.keep, self.out_sem, self.in_sem = scratch
+
+    def copy(self, i):
+        axis, (k, j) = self.axis, self.peers[i]
+        return pltpu.make_async_remote_copy(
+            src_ref=self.source(self.src, axis.at(k, j)),
+            dst_ref=self.target(self.dst, axis.at(0, 0)),
+            send_sem=self.out_sem.at[i],
+            recv_sem=self.in_sem.at[i],
+            **axis.to(k, j),
+        )
+
+    def own(self):
+        me = self.axis.at(0, 0)
+        return pltpu.make_async_copy(self.source(self.src, me), self.target(self.dst, me), self.keep)
+
+    def start(self):
+        self.own().start()
+        for i in reversed(range(len(self.peers))):
+            self.copy(i).start()
+
+    def middle(self, part, parts):
+        pass
+
+    def finish(self):
+        for i in reversed(range(len(self.peers))):
+            self.copy(i).wait()
+        self.own().wait()
+
+
+class Scatter:
+    def __init__(self, axis, parts, outer, dtype):
+        self.axis, self.outer, self.dtype, self.inputs = axis, outer, dtype, [parts]
+        self.chunks = parts.shape[1 if outer else 0]
+        block = (self.chunks,) + parts.shape[2:]
+        self.outputs = [jax.ShapeDtypeStruct(block, dtype)]
+        rows, others, held = axis.rows, axis.cols - 1, max(axis.rows - 1, 1)
+        row, col = (held, self.chunks), (others, rows, self.chunks)
+        self.scratch = [
+            pltpu.VMEM((rows,) + block, bf16),
+            pltpu.VMEM((others, rows) + block, bf16),
+            pltpu.VMEM((held,) + block, bf16),
+            pltpu.VMEM((held,) + block, bf16),
+            pltpu.VMEM(block, dtype),
+            dma((rows, self.chunks)),
+            dma(col),
+            dma(col),
+            dma(row),
+            dma(row),
+            dma((self.chunks,)),
+        ]
+        self.peers = [(k, 0) for k in range(1, rows)] + [(0, j) for j in range(1, axis.cols)]
+        self.order = [(k, c) for k in list(range(1, rows)) + [0] for c in range(self.chunks)]
+        self.bytes = parts.size // axis.size * 2
+
+    def bind(self, ins, outs, scratch):
+        (self.src,), (self.dst,) = ins, outs
+        self.mine, self.met, self.sent, self.come, self.result = scratch[:5]
+        self.load, self.col_out, self.col_in, self.row_out, self.row_in, self.store = scratch[5:]
+
+    def terms(self, dev, c):
+        return self.src.at[dev, c] if self.outer else self.src.at[c, dev]
+
+    def read(self, k, c):
+        return pltpu.make_async_copy(
+            self.terms(self.axis.at(k, 0), c), self.mine.at[k, c], self.load.at[k, c]
+        )
+
+    def across(self, k, j, c):
+        return pltpu.make_async_remote_copy(
+            src_ref=self.terms(self.axis.at(k, j), c),
+            dst_ref=self.met.at[j - 1, k, c],
+            send_sem=self.col_out.at[j - 1, k, c],
+            recv_sem=self.col_in.at[j - 1, k, c],
+            **self.axis.to(0, j),
+        )
+
+    def along(self, k, c):
+        return pltpu.make_async_remote_copy(
+            src_ref=self.sent.at[k - 1, c],
+            dst_ref=self.come.at[k - 1, c],
+            send_sem=self.row_out.at[k - 1, c],
+            recv_sem=self.row_in.at[k - 1, c],
+            **self.axis.to(k, 0),
+        )
+
+    def write(self, c):
+        return pltpu.make_async_copy(self.result.at[c], self.dst.at[c], self.store.at[c])
+
+    def meet(self, k, c):
+        self.read(k, c).wait()
+        total = self.mine[k, c].astype(f32)
+        for j in range(1, self.axis.cols):
+            self.across(k, j, c).wait_recv()
+            total = total + self.met[j - 1, k, c].astype(f32)
+        return total
+
+    def start(self):
+        for k, c in self.order:
+            for j in range(1, self.axis.cols):
+                self.across(k, j, c).start()
+            self.read(k, c).start()
+
+    def middle(self, part, parts):
+        steps = [step for step in self.order if step[0]]
+        for k, c in steps[len(steps) * part // parts : len(steps) * (part + 1) // parts]:
+            self.sent[k - 1, c] = self.meet(k, c).astype(bf16)
+            self.along(k, c).start()
+
+    def finish(self):
+        for c in range(self.chunks):
+            total = self.meet(0, c)
+            for k in range(1, self.axis.rows):
+                self.along(k, c).wait_recv()
+                total = total + self.come[k - 1, c].astype(f32)
+            self.result[c] = total.astype(self.dtype)
+            self.write(c).start()
+        for k, c in self.order:
+            for j in range(1, self.axis.cols):
+                self.across(k, j, c).wait_send()
+            if k:
+                self.along(k, c).wait_send()
+        for c in range(self.chunks):
+            self.write(c).wait()
+
+
+class Product:
+    def __init__(self, left, right, over, tiles):
+        self.inputs, self.over = [left, right], over
+        self.depth, m, n = left.shape[over[0]], left.shape[1 - over[0]], right.shape[1 - over[1]]
+        self.outputs = [jax.ShapeDtypeStruct((m, n), bf16)]
+        self.tm, self.tn = min(tiles[0], m), min(tiles[1], n)
+        self.grid = (m // self.tm, n // self.tn)
+        self.scratch, self.peers, self.bytes = [], [], 0
+
+    def bind(self, ins, outs, scratch):
+        self.refs = (*ins, *outs)
+
+    def start(self):
+        pass
+
+    def middle(self, part, parts):
+        pass
+
+    def finish(self):
+        pass
+
+    def compute(self):
+        def body(left, right, out):
+            out[...] = contract(left[...], right[...], *self.over).astype(bf16)
+
+        def tile(size, over, index):
+            if over == 0:
+                return pl.BlockSpec((self.depth, size), lambda i, j: (0, (i, j)[index]))
+            return pl.BlockSpec((size, self.depth), lambda i, j: ((i, j)[index], 0))
+
+        pltpu.emit_pipeline(
+            body,
+            grid=self.grid,
+            in_specs=[tile(self.tm, self.over[0], 0), tile(self.tn, self.over[1], 1)],
+            out_specs=[pl.BlockSpec((self.tm, self.tn), lambda i, j: (i, j))],
+        )(*self.refs)
+
+
+class Net:
+    def __init__(self, n_seq, n_fsdp):
+        rows = 4 if n_fsdp % 4 == 0 else 1
+        self.seq = Axis("seq", n_seq // 2, 2)
+        self.fsdp = Axis("fsdp", rows, n_fsdp // rows)
         self.calls = 0
 
-    def call(self, kernel, inputs, out_shapes, scratch, name, cost):
+    def run(self, jobs, room=32):
         self.calls += 1
+        ins = [array for job in jobs for array in job.inputs]
+        outs = [shape for job in jobs for shape in job.outputs]
+        scratch = [one for job in jobs for one in job.scratch]
+        peers = []
+        for job in jobs:
+            for peer in job.peers:
+                if (job.axis, peer) not in peers:
+                    peers.append((job.axis, peer))
+
+        def kernel(*refs):
+            at = [0, len(ins), len(ins) + len(outs)]
+            for job in jobs:
+                taken = []
+                for part, count in enumerate(
+                    (len(job.inputs), len(job.outputs), len(job.scratch))
+                ):
+                    taken.append(refs[at[part] : at[part] + count])
+                    at[part] += count
+                job.bind(*taken)
+            barrier = pltpu.get_barrier_semaphore()
+            for axis, peer in peers:
+                pl.semaphore_signal(barrier, inc=1, **axis.to(*peer))
+            pl.semaphore_wait(barrier, len(peers))
+            for job in jobs:
+                job.start()
+            parts = 4
+            for part in range(parts):
+                for job in jobs:
+                    job.middle(part, parts)
+            for job in jobs:
+                if isinstance(job, Product):
+                    job.compute()
+            for job in jobs:
+                job.finish()
+
         anywhere = pl.BlockSpec(memory_space=pl.ANY)
         return pl.pallas_call(
             kernel,
-            in_specs=[anywhere] * len(inputs),
-            out_specs=[anywhere] * len(out_shapes),
-            out_shape=out_shapes,
+            in_specs=[anywhere] * len(ins),
+            out_specs=[anywhere] * len(outs),
+            out_shape=outs,
             scratch_shapes=scratch,
             compiler_params=pltpu.CompilerParams(
-                collective_id=self.calls, has_side_effects=True, vmem_limit_bytes=48 << 20
+                collective_id=self.calls, has_side_effects=True, vmem_limit_bytes=room << 20
             ),
-            cost_estimate=pl.CostEstimate(flops=0, bytes_accessed=cost, transcendentals=0),
-            name=name,
-        )(*inputs)
-
-    @staticmethod
-    def greet(peers):
-        barrier = pltpu.get_barrier_semaphore()
-        for peer in peers:
-            pl.semaphore_signal(barrier, inc=1, device_id={"seq": peer}, device_id_type=MESH)
-        pl.semaphore_wait(barrier, len(peers))
-
-    def gather(self, blocks, outer):
-        n, pairs, count = self.n, self.pairs, len(blocks)
-        shapes = [
-            jax.ShapeDtypeStruct(
-                ((n, b.shape[0]) if outer else (b.shape[0], n)) + b.shape[1:], b.dtype
-            )
-            for b in blocks
-        ]
-        steps = [(a, c) for a, b in enumerate(blocks) for c in range(b.shape[0])]
-        total = len(steps)
-
-        def kernel(*refs):
-            ins, outs = refs[:count], refs[count : 2 * count]
-            keep, y_out, y_in, c_out, c_in = refs[2 * count :]
-            me = lax.axis_index("seq")
-            core = lax.rem(me, 2)
-            partner = me + 1 - 2 * core
-            ahead = [lax.rem(me + 2 * k, n) for k in range(pairs)]
-            behind = [lax.rem(me + n - 2 * k, n) for k in range(pairs)]
-            self.greet([partner] + ahead[1:])
-
-            def at(a, dev, c):
-                return outs[a].at[dev, c] if outer else outs[a].at[c, dev]
-
-            def remote(src, a, dev, c, out_sem, in_sem, to):
-                return pltpu.make_async_remote_copy(
-                    src_ref=src,
-                    dst_ref=at(a, dev, c),
-                    send_sem=out_sem,
-                    recv_sem=in_sem,
-                    device_id={"seq": to},
-                    device_id_type=MESH,
-                )
-
-            started = []
-            for i, (a, c) in enumerate(steps):
-                for k in range(1, pairs):
-                    copy = remote(
-                        ins[a].at[c], a, me, c, y_out.at[k - 1, i], y_in.at[k - 1, i], ahead[k]
-                    )
-                    copy.start()
-                    started.append(copy)
-            crossed = []
-            for i, (a, c) in enumerate(steps):
-                copy = remote(ins[a].at[c], a, me, c, c_out.at[0, i], c_in.at[0, i], partner)
-                copy.start()
-                crossed.append(copy)
-                copy = pltpu.make_async_copy(ins[a].at[c], at(a, me, c), keep.at[i])
-                copy.start()
-            for i, (a, c) in enumerate(steps):
-                for k in range(1, pairs):
-                    remote(
-                        ins[a].at[c], a, behind[k], c, y_out.at[k - 1, i], y_in.at[k - 1, i], ahead[k]
-                    ).wait_recv()
-                    copy = remote(
-                        at(a, behind[k], c),
-                        a,
-                        behind[k],
-                        c,
-                        c_out.at[k, i],
-                        c_in.at[k, i],
-                        partner,
-                    )
-                    copy.start()
-                    crossed.append(copy)
-            for copy in started:
-                copy.wait_send()
-            for copy in crossed:
-                copy.wait()
-            for i, (a, c) in enumerate(steps):
-                pltpu.make_async_copy(ins[a].at[c], at(a, me, c), keep.at[i]).wait()
-
-        dma = pltpu.SemaphoreType.DMA
-        held = max(pairs - 1, 1)
-        return self.call(
-            kernel,
-            blocks,
-            shapes,
-            [
-                dma((total,)),
-                dma((held, total)),
-                dma((held, total)),
-                dma((pairs, total)),
-                dma((pairs, total)),
-            ],
-            "gather_team",
-            sum(60 * b.size * 2 for b in blocks),
-        )
-
-    def exchange(self, array, out_shape, source, target):
-        n = self.n
-
-        def kernel(in_ref, out_ref, keep, out_sem, in_sem):
-            me = lax.axis_index("seq")
-            core = lax.rem(me, 2)
-            peers = [
-                lax.rem(me - core + 2 * k, n) + (1 - core if flip else core)
-                for k in range(self.pairs)
-                for flip in (False, True)
-            ]
-            self.greet(peers[1:])
-            own = pltpu.make_async_copy(source(in_ref, me), target(out_ref, me), keep)
-            own.start()
-            copies = []
-            for k in reversed(range(1, n)):
-                copy = pltpu.make_async_remote_copy(
-                    src_ref=source(in_ref, peers[k]),
-                    dst_ref=target(out_ref, me),
-                    send_sem=out_sem.at[k - 1],
-                    recv_sem=in_sem.at[k - 1],
-                    device_id={"seq": peers[k]},
-                    device_id_type=MESH,
-                )
-                copy.start()
-                copies.append(copy)
-            for copy in copies:
-                copy.wait()
-            own.wait()
-
-        dma = pltpu.SemaphoreType.DMA
-        return self.call(
-            kernel,
-            [array],
-            [jax.ShapeDtypeStruct(out_shape, array.dtype)],
-            [dma, dma((n - 1,)), dma((n - 1,))],
-            "exchange_team",
-            40 * array.size * 2,
-        )[0]
-
-    def scatter(self, parts, dtype):
-        chunks, n, rows, columns = parts.shape
-        pairs = self.pairs
-        held = max(pairs - 1, 1)
-
-        def kernel(in_ref, out_ref, mine, met, sent, come, result, load, c_out, c_in, y_out, y_in, store):
-            me = lax.axis_index("seq")
-            core = lax.rem(me, 2)
-            partner = me + 1 - 2 * core
-            ahead = [lax.rem(me + 2 * k, n) for k in range(pairs)]
-            self.greet([partner] + ahead[1:])
-            order = [(k, c) for k in list(range(1, pairs)) + [0] for c in range(chunks)]
-
-            def read(k, c):
-                return pltpu.make_async_copy(in_ref.at[c, ahead[k]], mine.at[k, c], load.at[k, c])
-
-            def cross(k, c):
-                return pltpu.make_async_remote_copy(
-                    src_ref=in_ref.at[c, lax.rem(partner + 2 * k, n)],
-                    dst_ref=met.at[k, c],
-                    send_sem=c_out.at[k, c],
-                    recv_sem=c_in.at[k, c],
-                    device_id={"seq": partner},
-                    device_id_type=MESH,
-                )
-
-            def pass_on(k, c):
-                return pltpu.make_async_remote_copy(
-                    src_ref=sent.at[k - 1, c],
-                    dst_ref=come.at[k - 1, c],
-                    send_sem=y_out.at[k - 1, c],
-                    recv_sem=y_in.at[k - 1, c],
-                    device_id={"seq": ahead[k]},
-                    device_id_type=MESH,
-                )
-
-            for k, c in order:
-                cross(k, c).start()
-                read(k, c).start()
-            for k, c in order:
-                cross(k, c).wait_recv()
-                read(k, c).wait()
-                if k:
-                    sent[k - 1, c] = (mine[k, c].astype(f32) + met[k, c].astype(f32)).astype(bf16)
-                    pass_on(k, c).start()
-            for c in range(chunks):
-                total = mine[0, c].astype(f32) + met[0, c].astype(f32)
-                for k in range(1, pairs):
-                    pass_on(k, c).wait_recv()
-                    total = total + come[k - 1, c].astype(f32)
-                result[c] = total.astype(dtype)
-                pltpu.make_async_copy(result.at[c], out_ref.at[c], store.at[c]).start()
-            for k, c in order:
-                cross(k, c).wait_send()
-                if k:
-                    pass_on(k, c).wait_send()
-            for c in range(chunks):
-                pltpu.make_async_copy(result.at[c], out_ref.at[c], store.at[c]).wait()
-
-        dma = pltpu.SemaphoreType.DMA
-        block = (chunks, rows, columns)
-        return self.call(
-            kernel,
-            [parts],
-            [jax.ShapeDtypeStruct(block, dtype)],
-            [
-                pltpu.VMEM((pairs,) + block, bf16),
-                pltpu.VMEM((pairs,) + block, bf16),
-                pltpu.VMEM((held,) + block, bf16),
-                pltpu.VMEM((held,) + block, bf16),
-                pltpu.VMEM(block, dtype),
-                dma((pairs, chunks)),
-                dma((pairs, chunks)),
-                dma((pairs, chunks)),
-                dma((held, chunks)),
-                dma((held, chunks)),
-                dma((chunks,)),
-            ],
-            "scatter_team",
-            60 * parts.size // n * 2,
-        )[0]
+            cost_estimate=pl.CostEstimate(
+                flops=0, bytes_accessed=60 * max(job.bytes for job in jobs), transcendentals=0
+            ),
+            name="net",
+        )(*ins)
 
 
 def own_columns(weight, me, groups, count, each):
@@ -640,8 +721,8 @@
         hidden_shard = w_down.shape[0]
         my_hidden = hidden_shard // n_seq
         out_rows = shard // n_seq
-        team = Team(n_seq)
-        me = team.me
+        net = Net(n_seq, n_fsdp)
+        me = lax.axis_index("seq")
 
         (qkv_own,) = own_columns(w_qkv, me, 1, 3, my_width)
         gate_own, up_own = own_columns(w_gate_up, me, 2, n_fsdp, my_hidden)
@@ -656,20 +737,25 @@
         def gather_rows(block):
             return lax.all_gather(block, "fsdp", axis=0, tiled=True)
 
-        def gather_tokens(value):
-            (out,) = team.gather([value.reshape(segs, local, width)], False)
-            return out.reshape(total_rows, width)
-
-        def scatter_tokens(value):
-            return team.scatter(value.reshape(segs, n_seq, local, width), f32).reshape(rows, width)
-
-        w_o = gather_rows(tie(out_own, h_one_own))
-        w_q = gather_rows(tie(qkv_own, h_one_own))
-        h_one = gather_tokens(h_one_own)
-        w_g = gather_rows(tie(gate_own, h_one))
-        (whole_o,) = team.gather([tie(w_o, h_one).reshape(n_fsdp, out_rows, width)], False)
-        whole_o = whole_o.reshape(width, width)
-        w_u = gather_rows(tie(up_own, whole_o))
+        def token_parts(value):
+            return value.reshape(segs, n_seq, local, width)
+
+        def gather_own(value):
+            return Gather(net.seq, value.reshape(segs, local, width), False)
+
+        w_g = gather_rows(gate_own)
+        h_one, grad_y_all, w_o, w_q = net.run(
+            [
+                gather_own(h_one_own),
+                gather_own(grad_y),
+                Gather(net.fsdp, out_own.reshape(1, out_rows, width), True),
+                Gather(net.fsdp, qkv_own.reshape(4, shard // 4, 3 * my_width), True),
+            ]
+        )
+        h_one = h_one.reshape(total_rows, width)
+        grad_y_all = grad_y_all.reshape(total_rows, width)
+        w_q = w_q.reshape(width, 3 * my_width)
+        w_u = gather_rows(tie(up_own, w_q))
 
         qkv = mm(h_one, w_q).astype(bf16)
         gate = jax.nn.sigmoid(lax.dynamic_slice(gate_bias, (me * my_heads,), (my_heads,)))
@@ -677,7 +763,8 @@
         norms = lax.dynamic_slice(norms_in[0], (me * my_heads, 0), (my_heads, hdim))
         attn_heads, lse, mems, nrms = attention_forward(qkv, gate, resets[0], memory, norms, segs)
 
-        w_d = gather_rows(tie(down_own, attn_heads))
+        half = width // 2
+        w_d_left = gather_rows(tie(down_own[:, :half], attn_heads))
 
         def columns_of(ref, i):
             return ref.at[:, :, pl.ds(pl.multiple_of(i * my_width, my_width), my_width)]
@@ -685,19 +772,31 @@
         def tokens_of(ref, i):
             return ref.at[:, i]
 
-        attn = team.exchange(
-            attn_heads.reshape(segs, n_seq, local, my_width),
-            (segs, local, width),
-            tokens_of,
-            columns_of,
-        ).reshape(rows, width)
+        attn, whole_o, w_d_right = net.run(
+            [
+                Exchange(
+                    net.seq,
+                    attn_heads.reshape(segs, n_seq, local, my_width),
+                    (segs, local, width),
+                    tokens_of,
+                    columns_of,
+                ),
+                Gather(net.seq, w_o.reshape(n_fsdp, out_rows, width), False),
+                Gather(net.fsdp, down_own[:, half:].reshape(4, my_hidden // 4, half), True),
+            ]
+        )
+        attn = attn.reshape(rows, width)
+        whole_o = whole_o.reshape(width, width)
         x_one = x_flat + mm(attn, whole_o)
         r_two = rms(x_one)
-        h_two = gather_tokens((r_two * gain_ffn).astype(bf16))
-        grad_y_all = gather_tokens(tie(grad_y, h_two))
+        h_two_own = (r_two * gain_ffn).astype(bf16)
+        (h_two,) = net.run([gather_own(h_two_own)])
+        h_two = h_two.reshape(total_rows, width)
         gate_part = mm(h_two, w_g).astype(bf16)
         up_part = mm(h_two, w_u).astype(bf16)
         hidden = swiglu(gate_part.astype(f32), up_part.astype(f32)).astype(bf16)
+
+        w_d = jnp.concatenate([w_d_left, w_d_right.reshape(-1, half)], axis=1)
 
         def scatter_rows(parts):
             return lax.psum_scatter(parts, "fsdp", scatter_dimension=0, tiled=True)
@@ -710,10 +809,17 @@
         grad_gate, grad_up = grad_gate.astype(bf16), grad_up.astype(bf16)
         gate_parts = mm_tn(h_two, grad_gate).astype(bf16)
         gate_term = scatter_rows(gate_parts)
-        up_parts = mm_tn(h_two, tie(grad_up, gate_parts)).astype(bf16)
+        grad_gate, grad_up, _ = lax.optimization_barrier((grad_gate, grad_up, gate_parts))
+        grad_h_two = (mm_nt(grad_gate, w_g) + mm_nt(grad_up, w_u)).astype(bf16)
+        grad_h_two, up_parts = net.run(
+            [
+                Scatter(net.seq, token_parts(grad_h_two), False, f32),
+                Product(h_two, grad_up, (0, 0), (1024, 512)),
+            ],
+            56,
+        )
         up_term = scatter_rows(up_parts)
-        grad_gate, grad_up, _ = lax.optimization_barrier((grad_gate, grad_up, up_parts))
-        grad_h_two = scatter_tokens((mm_nt(grad_gate, w_g) + mm_nt(grad_up, w_u)).astype(bf16))
+        grad_h_two = grad_h_two.reshape(rows, width)
 
         gain_ffn_term = jnp.sum(grad_h_two * r_two, axis=0)
         _, norm_two_back = jax.vjp(rms, x_one)
@@ -721,35 +827,58 @@
         grad_o = grad_x_one.astype(bf16)
 
         grad_attn_parts = mm_nt(grad_o, whole_o).astype(bf16)
-        grad_attn = team.exchange(
-            grad_attn_parts.reshape(segs, local, width),
-            (segs, n_seq, local, my_width),
-            columns_of,
-            tokens_of,
-        ).reshape(total_rows, my_width)
+        grad_attn, output = net.run(
+            [
+                Exchange(
+                    net.seq,
+                    grad_attn_parts.reshape(segs, local, width),
+                    (segs, n_seq, local, my_width),
+                    columns_of,
+                    tokens_of,
+                ),
+                Product(hidden, w_d, (1, 0), (1024, 512)),
+            ],
+            56,
+        )
+        grad_attn = grad_attn.reshape(total_rows, my_width)
         grads_q, grads_k, grads_v, bias_terms = attention_backward(
             qkv, grad_attn, gate, resets[0], depth, lse, mems, nrms, segs
         )
         grad_qkv_rows = jnp.concatenate([grads_q, grads_k, grads_v], axis=1)
-        qkv_parts = mm_tn(h_one, grad_qkv_rows).astype(bf16)
-        qkv_term = scatter_rows(tie(qkv_parts, gate_term))
-
-        out_parts = mm_tn(attn, tie(grad_o, qkv_parts)).astype(bf16)
-        out_sum = team.scatter(out_parts.reshape(n_fsdp, n_seq, out_rows, width), bf16)
-        out_term = scatter_rows(tie(out_sum, up_term).reshape(-1, width))
-        grad_qkv_rows = tie(grad_qkv_rows, qkv_parts)
-        grad_h_one = scatter_tokens(mm_nt(grad_qkv_rows, w_q).astype(bf16))
-        output = x_one + scatter_tokens(mm(tie(hidden, grad_h_one), w_d).astype(bf16))
-        output = output.astype(bf16).reshape(tokens.shape)
+        out_parts = mm_tn(attn, tie(grad_o, grads_q)).astype(bf16)
+        out_sum, qkv_parts, grad_h_one = net.run(
+            [
+                Scatter(net.seq, out_parts.reshape(n_fsdp, n_seq, out_rows, width), False, bf16),
+                Product(h_one, grad_qkv_rows, (0, 0), (1024, 512)),
+                Product(grad_qkv_rows, w_q, (1, 1), (1024, 512)),
+            ],
+            56,
+        )
+        grad_h_one, output, qkv_term, out_term, down_all = net.run(
+            [
+                Scatter(net.seq, token_parts(grad_h_one), False, f32),
+                Scatter(net.seq, token_parts(output), False, f32),
+                Scatter(
+                    net.fsdp, qkv_parts.reshape(n_fsdp, 4, shard // 4, 3 * my_width), True, bf16
+                ),
+                Scatter(net.fsdp, out_sum[:, None], True, bf16),
+                Gather(net.seq, down_term[None], True),
+            ],
+            56,
+        )
+        grad_h_one = grad_h_one.reshape(rows, width)
+        output = (x_one + output.reshape(rows, width)).astype(bf16).reshape(tokens.shape)
+        qkv_term = qkv_term.reshape(shard, 3 * my_width)
+        out_term = out_term.reshape(out_rows, width)
         gain_attn_term = jnp.sum(grad_h_one * r_one, axis=0)
         _, norm_one_back = jax.vjp(rms, x_flat)
         grad_x = grad_x_one + norm_one_back(grad_h_one * gain_attn)[0]
         input_grad = grad_x.astype(bf16).reshape(tokens.shape)
 
-        (down_all,) = team.gather([down_term[None]], True)
-        (gate_all,) = team.gather([gate_term[None]], True)
-        (up_all,) = team.gather([up_term[None]], True)
-        qkv_all, out_all = team.gather([qkv_term[None], out_term[None]], True)
+        qkv_all, out_all, gate_all = net.run(
+            [Gather(net.seq, term[None], True) for term in (qkv_term, out_term, gate_term)]
+        )
+        (up_all,) = net.run([Gather(net.seq, up_term[None], True)])
         down_all = down_all.reshape(hidden_shard, width).astype(f32)
         out_all = out_all.reshape(shard, width).astype(f32)
         gate_up_all = spread_columns([gate_all[:, 0], up_all[:, 0]], n_fsdp, my_hidden, shard)

time: 1320 us -> 1160 us (0.88)
  waiting for transfers between devices: 269 us -> 3.24 us
  Pallas kernels: 652 us -> 818 us
  matrix products: 309 us -> 216 us
  other arithmetic: 22.3 us -> 40.9 us
    pallas_call x14 -> x9, Pallas kernels: 569 us -> 735 us  [run(): pl.pallas_call(kernel, in_specs=[anywhere] * len(ins), out_specs=[anywher...]
    all_gather x5 -> x3, waiting for transfers between devices: 158 us -> 0.02 us  [gather_rows(): return lax.all_gather(block, 'fsdp', axis=0, tiled=True)]
    reduce_scatter x5 -> x3, waiting for transfers between devices: 107 us -> 0.02 us  [scatter_rows(): return lax.psum_scatter(parts, 'fsdp', scatter_dimension=0, tiled=True)]
    dot_general x5 -> x3, matrix products: 93.6 us -> 50.3 us  [mm_tn(): lax.dot_general(left, right, (((0,), (0,)), ((), ())), preferred_element_...]
    dot_general x5 -> x4, matrix products: 103 us -> 76.4 us  [mm(): return jnp.dot(left, right, preferred_element_type=f32)]
    dot_general x5 -> x4, matrix products: 112 us -> 89.4 us  [mm_nt(): lax.dot_general(left, right, (((1,), (1,)), ((), ())), preferred_element_...]
    unnamed x94 -> x100, local copies, waits for them, and re-layouts: 27.5 us -> 35.4 us
  transfers between devices with their start and end apart: 15 -> 11, of which waited for: 7 -> 2; matrix products, arithmetic and copies ran while one was open for 19% -> 23% of each run, Pallas kernels for 47% -> 71%
where the time goes in v3:
time: 1160 us; the launch traced here: 1150 us
  Pallas kernels  818 us (71%)
  matrix products  216 us (19%)
  local copies, waits for them, and re-layouts  41 us (4%)
  other arithmetic  40.9 us (4%)
  between operations  16.4 us (1%)
  starting transfers between devices  12.1 us (1%)
    pallas_call x9, Pallas kernels, run(): pl.pallas_call(kernel, in_specs=[anywhere] * len(ins), out_specs=[anywher...  735 us
    dot_general x4, matrix products, mm_nt(): lax.dot_general(left, right, (((1,), (1,)), ((), ())), preferred_element_...  89.4 us
    dot_general x4, matrix products, mm(): return jnp.dot(left, right, preferred_element_type=f32)  76.4 us
    dot_general x3, matrix products, mm_tn(): lax.dot_general(left, right, (((0,), (0,)), ((), ())), preferred_element_...  50.3 us
    unnamed x100, local copies, waits for them, and re-layouts  35.4 us
    pallas_call x1, Pallas kernels, attention_backward(): pl.pallas_call(functools.partial(backward_kernel, min(256, seg), segs), g...  34 us
  transfers between devices with their start and end apart: 11, of which 2 were waited for; matrix products, arithmetic and copies ran while one was open for 23% of the time, Pallas kernels for 71%

profile of v3, /device:TPU:0, one launch (start us, length us, event | category | flops | bytes accessed | tf_op | source)
XLA Modules:
  0.0 1148.3 jit_solution(12837820307854683990)
XLA Ops:
  7.2 5.9 own_columns.3
  21.2 196.3 %net.9 = (bf16[2,4,256,2048]{3,2,1,0:T(8,128)(2,1)S(1)}, bf16[2,4,256,2048]{3,2,1,0:T(8,128)(2,1)}, bf16[8,1,64,2048]{3,2,1,0:T(8,128)(2,1)S(1)}, bf16[8,4,64,1536]{3,2,1,0:T(8,128)(2,1)S(1)}) custom-call(bf16[2,256,2048]{2,1,0:T(8,128)(2,1)S(1)} %fusion.16.refs_0_, bf16[2,256,2048]{2,1,0:T(8,128)(2,1)S(1)} %bitcast.124, ...), custom_call_target="tpu_custom_call" | custom-call | bytes 125829120 | tf_op jit(solution)/shard_map/net/pallas_call | solution.py:613
  229.7 18.5 %convolution_convert_fusion.5.q_ref.k_ref.v_ref = bf16[2048,1536]{1,0:T(8,128)(2,1)} fusion(bf16[2048,2048]{1,0:T(8,128)(2,1)} %bitcast.126, bf16[2048,1536]{1,0:T(8,128)(2,1)} %bitcast.129), kind=kOutput, calls=%fused_computation.21 | convolution fusion | flops 12888047616 | bytes 20971520 | tf_op jit(solution)/shard_map/dot_general | solution.py:685
  248.2 19.8 %attention_forward.1 = (bf16[2048,512]{1,0:T(8,128)(2,1)S(1)}, f32[4,2,1,1024]{3,2,1,0:T(1,128)S(1)}, f32[4,2,128,128]{3,2,1,0:T(8,128)S(1)}, f32[4,2,1,128]{3,2,1,0:T(1,128)S(1)}) custom-call(f32[4]{0:T(128)S(1)} %add_divide_fusion.gate, s32[1]{0:T(128)} %bitcast.118.resets, bf16[2048,1536]{1,0:T(8,128)(2,1)} %convolution_convert_fusion.5.q_ref.k_ref.v_ref, ...), custom_call_target="tpu_custom_call" | custom-call | flops 4026531840 | bytes 12582912 | tf_op jit(solution)/shard_map/attention_forward/pallas_call | solution.py:133
  274.3 111.8 %net.10 = (bf16[2,256,2048]{2,1,0:T(8,128)(2,1)S(1)}, bf16[8,4,64,2048]{3,2,1,0:T(8,128)(2,1)S(1)}, bf16[8,4,64,1024]{3,2,1,0:T(8,128)(2,1)S(1)}) custom-call(bf16[2,4,256,512]{3,2,1,0:T(8,128)(2,1)S(1)} %bitcast.137, bf16[8,64,2048]{2,1,0:T(8,128)(2,1)S(1)} %bitcast.136, bf16[4,64,1024]{2,1,0:T(8,128)(2,1)S(1)} %bitcast.138), custom_call_target="tpu_custom_call" | custom-call | bytes 125829120 | tf_op jit(solution)/shard_map/net/pallas_call | solution.py:613
  386.2 7.9 multiply_reduce_fusion.1
  396.1 50.3 %net.11 = bf16[2,4,256,2048]{3,2,1,0:T(8,128)(2,1)S(1)} custom-call(bf16[2,256,2048]{2,1,0:T(8,128)(2,1)S(1)} %bitcast.128), custom_call_target="tpu_custom_call" | custom-call | bytes 125829120 | tf_op jit(solution)/shard_map/net/pallas_call | solution.py:613
  449.7 23.5 %convolution_convert_fusion.4 = bf16[2048,2048]{1,0:T(8,128)(2,1)} fusion(bf16[2048,2048]{1,0:T(8,128)(2,1)} %bitcast.120, bf16[2048,2048]{1,0:T(8,128)(2,1)} %all-gather.4.cloned.1.call-done), kind=kOutput, calls=%fused_computation.20 | convolution fusion | flops 17184063488 | bytes 25165824 | tf_op jit(solution)/shard_map/dot_general | solution.py:685
  473.2 26.5 %fusion = (bf16[2048,2048]{1,0:T(8,128)(2,1)S(1)}, bf16[2048,2048]{1,0:T(8,128)(2,1)}) fusion(bf16[2048,2048]{1,0:T(8,128)(2,1)} %convolution_convert_fusion.4, bf16[2048,2048]{1,0:T(8,128)(2,1)} %bitcast.121, bf16[2048,2048]{1,0:T(8,128)(2,1)} %all-gather.6.cloned.1.call-done), kind=kOutput, calls=%fused_computation.6 | convolution fusion | flops 17217617920 | bytes 41943040 | tf_op jit(solution)/shard_map/dot_general | solution.py:685
  503.0 22.2 %convolution_convert_fusion.2 = bf16[2048,2048]{1,0:T(8,128)(2,1)} fusion(bf16[2048,2048]{1,0:T(8,128)(2,1)S(1)} %get-tuple-element.101.refs_1_, bf16[2048,2048]{1,0:T(8,128)(2,1)} %bitcast.162), kind=kOutput, calls=%fused_computation.18 | convolution fusion | flops 17184063488 | bytes 25165824 | tf_op jit(solution)/shard_map/dot_general | solution.py:693
  525.3 32.9 %multiply_convert_fusion = (bf16[2048,2048]{1,0:T(8,128)(2,1)}, bf16[2048,2048]{1,0:T(8,128)(2,1)S(1)}) fusion(bf16[2048,2048]{1,0:T(8,128)(2,1)} %convolution_convert_fusion.4, bf16[2048,2048]{1,0:T(8,128)(2,1)} %get-tuple-element.102, bf16[2048,2048]{1,0:T(8,128)(2,1)} %bitcast.163, bf16[2048,1024]{1,0:T(8,128)(2,1)} %bitcast.132, ...), kind=kOutput, calls=%fused_computation.14 | convolution fusion | flops 17263755264 | bytes 50331648 | tf_op jit(solution)/shard_map/dot_general | solution.py:689
  561.5 21.4 %convolution_convert_fusion.1 = bf16[2048,2048]{1,0:T(8,128)(2,1)} fusion(bf16[2048,2048]{1,0:T(8,128)(2,1)} %bitcast.122, bf16[2048,2048]{1,0:T(8,128)(2,1)S(1)} %get-tuple-element.60), kind=kOutput, calls=%fused_computation.17 | convolution fusion | flops 17184063488 | bytes 25165824 | tf_op jit(solution)/shard_map/dot_general | solution.py:693
  583.0 24.8 %fusion.27 = f32[2048,2048]{1,0:T(8,128)} fusion(bf16[2048,2048]{1,0:T(8,128)(2,1)} %copy-done.46, bf16[2048,2048]{1,0:T(8,128)(2,1)} %all-gather.4.cloned.1.call-done), kind=kOutput, calls=%fused_computation.71 | convolution fusion | flops 17179869184 | bytes 33554432 | tf_op jit(solution)/shard_map/dot_general | solution.py:689
  607.8 25.7 %add_convert_fusion = bf16[2048,2048]{1,0:T(8,128)(2,1)} fusion(f32[2048,2048]{1,0:T(8,128)} %fusion.27, bf16[2048,2048]{1,0:T(8,128)(2,1)} %get-tuple-element.61.refs_2_, bf16[2048,2048]{1,0:T(8,128)(2,1)} %all-gather.6.cloned.1.call-done), kind=kOutput, calls=%fused_computation.13 | convolution fusion | flops 17188257792 | bytes 41943040 | tf_op jit(solution)/shard_map/dot_general | solution.py:689
  633.5 52.5 %net.12 = (f32[2,256,2048]{2,1,0:T(8,128)}, bf16[2048,2048]{1,0:T(8,128)(2,1)}) custom-call(bf16[2,4,256,2048]{3,2,1,0:T(8,128)(2,1)} %bitcast.152, bf16[2048,2048]{1,0:T(8,128)(2,1)} %bitcast.123, bf16[2048,2048]{1,0:T(8,128)(2,1)} %get-tuple-element.61.refs_2_), custom_call_target="tpu_custom_call" | custom-call | bytes 125829120 | tf_op jit(solution)/shard_map/net/pallas_call | solution.py:613
  686.8 8.3 pad_maximum_fusion.refs_2_
  695.1 5.0 fusion.13
  704.1 6.0 convolution_convert_fusion.6
  710.1 25.9 %net.13 = (bf16[2,4,256,512]{3,2,1,0:T(8,128)(2,1)}, bf16[2048,2048]{1,0:T(8,128)(2,1)}) custom-call(bf16[2,256,2048]{2,1,0:T(8,128)(2,1)} %bitcast.157, bf16[2048,2048]{1,0:T(8,128)(2,1)} %copy-done.32, bf16[2048,2048]{1,0:T(8,128)(2,1)} %pad_maximum_fusion.refs_2_), custom_call_target="tpu_custom_call" | custom-call | bytes 62914560 | tf_op jit(solution)/shard_map/net/pallas_call | solution.py:613
  736.0 34.0 %attention_backward.1 = (bf16[2048,512]{1,0:T(8,128)(2,1)S(1)}, bf16[2048,512]{1,0:T(8,128)(2,1)S(1)}, bf16[2048,512]{1,0:T(8,128)(2,1)}, f32[4,8,128]{2,1,0:T(8,128)S(1)}) custom-call(f32[4]{0:T(128)S(1)} %add_divide_fusion.gate, s32[1]{0:T(128)} %bitcast.119.resets, s32[1]{0:T(128)S(6)} %copy.28.depth, ...), custom_call_target="tpu_custom_call" | custom-call | flops 8053063680 | bytes 12582912 | tf_op jit(solution)/shard_map/attention_backward/pallas_call | solution.py:266
  770.0 4.6 pad_maximum_fusion.1.refs_2_.refs_3_
  774.6 6.8 convolution_convert_fusion
  781.4 50.8 %net.14 = (bf16[8,64,2048]{2,1,0:T(8,128)(2,1)}, bf16[2048,1536]{1,0:T(8,128)(2,1)}, bf16[2048,2048]{1,0:T(8,128)(2,1)}) custom-call(bf16[8,4,64,2048]{3,2,1,0:T(8,128)(2,1)} %bitcast.151, bf16[2048,2048]{1,0:T(8,128)(2,1)} %bitcast.127, bf16[2048,1536]{1,0:T(8,128)(2,1)} %pad_maximum_fusion.1.refs_2_.refs_3_, ...), custom_call_target="tpu_custom_call" | custom-call | bytes 125829120 | tf_op jit(solution)/shard_map/net/pallas_call | solution.py:613
  832.9 170.0 %net.15 = (f32[2,256,2048]{2,1,0:T(8,128)}, f32[2,256,2048]{2,1,0:T(8,128)}, bf16[4,64,1536]{2,1,0:T(8,128)(2,1)}, bf16[1,64,2048]{2,1,0:T(8,128)(2,1)}, bf16[4,1,256,2048]{3,2,1,0:T(8,128)(2,1)}) custom-call(bf16[2,4,256,2048]{3,2,1,0:T(8,128)(2,1)} %bitcast.150, bf16[2,4,256,2048]{3,2,1,0:T(8,128)(2,1)} %bitcast.149, bf16[8,4,64,1536]{3,2,1,0:T(8,128)(2,1)} %bitcast.153, ...), custom_call_target="tpu_custom_call" | custom-call | bytes 125829120 | tf_op jit(solution)/shard_map/net/pallas_call | solution.py:613
  1011.0 6.3 fusion.9
  1017.3 9.0 collective-permute-start.3
  1026.3 4.7 bitcast_convert_fusion
  1033.4 50.1 %net.16 = (bf16[4,1,256,1536]{3,2,1,0:T(8,128)(2,1)S(1)}, bf16[4,1,64,2048]{3,2,1,0:T(8,128)(2,1)S(1)}, bf16[4,1,256,2048]{3,2,1,0:T(8,128)(2,1)S(1)}) custom-call(bf16[1,256,1536]{2,1,0:T(8,128)(2,1)S(1)} %bitcast.141, bf16[1,64,2048]{2,1,0:T(8,128)(2,1)S(1)} %copy-done.19, bf16[1,256,2048]{2,1,0:T(8,128)(2,1)S(1)} %bitcast.140), custom_call_target="tpu_custom_call" | custom-call | bytes 62914560 | tf_op jit(solution)/shard_map/net/pallas_call | solution.py:613
  1088.7 7.3 spread_columns.4.refs_0_
  1097.3 27.5 %net.17 = bf16[4,1,256,2048]{3,2,1,0:T(8,128)(2,1)S(1)} custom-call(bf16[1,256,2048]{2,1,0:T(8,128)(2,1)S(1)} %bitcast.139), custom_call_target="tpu_custom_call" | custom-call | bytes 62914560 | tf_op jit(solution)/shard_map/net/pallas_call | solution.py:613
  1126.8 5.8 spread_columns.3
  1132.5 7.4 spread_columns.5
  (156 shorter events, 62.4 us)
Async XLA Ops:
  7.2 11.8 %copy-start = (bf16[256,2048]{1,0:T(8,128)(2,1)S(1)}, bf16[256,2048]{1,0:T(8,128)(2,1)}, u32[]{:S(2)}) copy-start(bf16[256,2048]{1,0:T(8,128)(2,1)} %param.16) | copy-start | bytes 3145732
  7.2 442.5 %all-gather.4.cloned.1.call-start = ((), (), s32[]{:S(2)}) async-start(), calls=%async_computation.3 | async-start | bytes 9437184 | tf_op jit(solution)/shard_map/all_gather | solution.py:738
  13.1 8.0 copy-start.3
  13.2 460.1 %all-gather.6.cloned.1.call-start = ((), (), s32[]{:S(2)}) async-start(), calls=%async_computation.4 | async-start | bytes 9437184 | tf_op jit(solution)/shard_map/all_gather | solution.py:738
  16.2 209.4 %copy-start.45 = (f32[16]{0:T(128)S(1)}, f32[16]{0:T(128)}, u32[]{:S(2)}) copy-start(f32[16]{0:T(128)} %param.21) | copy-start | bytes 196
  225.0 300.4 %all-gather.8.cloned.1.call-start = ((), (), s32[]{:S(2)}) async-start(), calls=%async_computation.5 | async-start | bytes 4718592 | tf_op jit(solution)/shard_map/all_gather | solution.py:738
  269.3 563.5 %reduce-scatter.4.cloned.1.call-start = ((), (), s32[]{:S(2)}) async-start(), calls=%async_computation.6 | async-start | bytes 9437184 | tf_op jit(solution)/shard_map/reduce_scatter | solution.py:802
  386.2 7.9 copy-start.8
  386.2 7.9 copy-start.20
  386.2 7.9 copy-start.21
  386.2 7.9 copy-start.34
  394.1 52.3 %copy-start.43 = (f32[512]{0:T(512)}, f32[512]{0:T(512)S(1)}, u32[]{:S(2)}) copy-start(f32[512]{0:T(512)S(1)} %get-tuple-element.99) | copy-start | bytes 6148
  394.1 52.3 %copy-start.38 = (f32[512]{0:T(512)}, f32[512]{0:T(512)S(1)}, u32[]{:S(2)}) copy-start(f32[512]{0:T(512)S(1)} %fusion.19) | copy-start | bytes 6148
  525.2 505.8 %reduce-scatter.6.cloned.1.call-start = ((), (), s32[]{:S(2)}) async-start(), calls=%async_computation.7 | async-start | bytes 9437184 | tf_op jit(solution)/shard_map/reduce_scatter | solution.py:802
  582.9 513.1 %reduce-scatter.8.cloned.1.call-start = ((), (), s32[]{:S(2)}) async-start(), calls=%async_computation.8 | async-start | bytes 9437184 | tf_op jit(solution)/shard_map/reduce_scatter | solution.py:802
  686.7 8.4 copy-start.35
  686.7 8.4 copy-start.39
  695.1 6.4 copy-start.29
  695.1 7.6 slice-start
  710.1 25.9 %copy-start.24 = (f32[4,2,128,128]{3,2,1,0:T(8,128)S(1)}, f32[4,2,128,128]{3,2,1,0:T(8,128)}, u32[]{:S(2)}) copy-start(f32[4,2,128,128]{3,2,1,0:T(8,128)} %copy-done.23) | copy-start | bytes 1572868
  832.8 170.0 %copy-start.28 = (bf16[1,2,256,2048]{3,2,1,0:T(8,128)(2,1)S(1)}, bf16[1,2,256,2048]{3,2,1,0:T(8,128)(2,1)}, u32[]{:S(2)}) copy-start(bf16[1,2,256,2048]{3,2,1,0:T(8,128)(2,1)} %param.13) | copy-start | bytes 6291460
  832.9 170.0 %copy-start.41 = (f32[2,256]{1,0:T(2,128)S(1)}, f32[2,256]{1,0:T(2,128)}, u32[]{:S(2)}) copy-start(f32[2,256]{1,0:T(2,128)} %copy-done.40) | copy-start | bytes 6148
  1002.9 8.1 copy-start.27
  1002.9 8.1 copy-start.30
  1005.9 1.3 collective-permute-start
  1007.1 3.8 collective-permute-start.1
  1010.9 6.4 collective-permute-start.2
  1011.0 15.3 %copy-start.33 = (bf16[4,1,256,2048]{3,2,1,0:T(8,128)(2,1)S(1)}, bf16[4,1,256,2048]{3,2,1,0:T(8,128)(2,1)}, u32[]{:S(2)}) copy-start(bf16[4,1,256,2048]{3,2,1,0:T(8,128)(2,1)} %get-tuple-element.83) | copy-start | bytes 12582916
  1017.3 68.2 %collective-permute-start.3 = (f32[4112]{0:T(1024)S(1)}, f32[4112]{0:T(1024)S(1)}, u32[]{:S(2)}, u32[]{:S(2)}) collective-permute-start(f32[4112]{0:T(1024)S(1)} %add.98), channel_id=1, source_target_pairs={{0,2},{1,3},{2,0},{3,1},{4,6},{5,7},{6,4},{7,5},{8,10},{9,11},{10,... | collective-permute-start | bytes 49352 | tf_op jit(solution)/shard_map/ppermute | solution.py:894
  1085.5 10.5 copy-start.10
  1085.5 54.4 %collective-permute-start.4 = (f32[4112]{0:T(1024)S(1)}, f32[4112]{0:T(1024)S(1)}, u32[]{:S(2)}, u32[]{:S(2)}) collective-permute-start(f32[4112]{0:T(1024)S(1)} %add.99), channel_id=1, source_target_pairs={{0,4},{1,5},{2,6},{3,7},{4,0},{5,1},{6,2},{7,3},{8,12},{9,13},{10,... | collective-permute-start | bytes 49352 | tf_op jit(solution)/shard_map/ppermute | solution.py:894
  1132.5 8.5 copy-start.1
  (28 other events, 76.0 us)
Sparse Core Ops, SparseCore 0:
  13.3 204.5 all-gather.3
  225.1 176.7 all-gather.5
  404.1 72.4 all-gather.7
  525.4 160.1 reduce-scatter.3
  689.4 147.9 reduce-scatter.5
  841.0 203.4 reduce-scatter.7

commit v4 on v3

--- a/solution.py
+++ b/solution.py
@@ -432,7 +432,7 @@
 
 
 class Scatter:
-    def __init__(self, axis, parts, outer, dtype):
+    def __init__(self, axis, parts, outer, dtype, ahead=None):
         self.axis, self.outer, self.dtype, self.inputs = axis, outer, dtype, [parts]
         self.chunks = parts.shape[1 if outer else 0]
         block = (self.chunks,) + parts.shape[2:]
@@ -454,6 +454,7 @@
         ]
         self.peers = [(k, 0) for k in range(1, rows)] + [(0, j) for j in range(1, axis.cols)]
         self.order = [(k, c) for k in list(range(1, rows)) + [0] for c in range(self.chunks)]
+        self.ahead = min(ahead or len(self.order), len(self.order))
         self.bytes = parts.size // axis.size * 2
 
     def bind(self, ins, outs, scratch):
@@ -490,18 +491,25 @@
     def write(self, c):
         return pltpu.make_async_copy(self.result.at[c], self.dst.at[c], self.store.at[c])
 
+    def leave(self, i):
+        if i < len(self.order):
+            k, c = self.order[i]
+            for j in range(1, self.axis.cols):
+                self.across(k, j, c).start()
+
     def meet(self, k, c):
         self.read(k, c).wait()
         total = self.mine[k, c].astype(f32)
         for j in range(1, self.axis.cols):
             self.across(k, j, c).wait_recv()
             total = total + self.met[j - 1, k, c].astype(f32)
+        self.leave(self.order.index((k, c)) + self.ahead)
         return total
 
     def start(self):
-        for k, c in self.order:
-            for j in range(1, self.axis.cols):
-                self.across(k, j, c).start()
+        for i, (k, c) in enumerate(self.order):
+            if i < self.ahead:
+                self.leave(i)
             self.read(k, c).start()
 
     def middle(self, part, parts):
@@ -528,12 +536,14 @@
 
 
 class Product:
-    def __init__(self, left, right, over, tiles):
-        self.inputs, self.over = [left, right], over
-        self.depth, m, n = left.shape[over[0]], left.shape[1 - over[0]], right.shape[1 - over[1]]
+    def __init__(self, pairs, over, tiles, rows=None):
+        self.inputs, self.over = [matrix for pair in pairs for matrix in pair], over
+        left, right = pairs[0]
+        self.depth, n = left.shape[over[0]], right.shape[1 - over[1]]
+        first, m = rows or (0, left.shape[1 - over[0]])
         self.outputs = [jax.ShapeDtypeStruct((m, n), bf16)]
         self.tm, self.tn = min(tiles[0], m), min(tiles[1], n)
-        self.grid = (m // self.tm, n // self.tn)
+        self.grid, self.skip = (m // self.tm, n // self.tn), first // self.tm
         self.scratch, self.peers, self.bytes = [], [], 0
 
     def bind(self, ins, outs, scratch):
@@ -549,18 +559,25 @@
         pass
 
     def compute(self):
-        def body(left, right, out):
-            out[...] = contract(left[...], right[...], *self.over).astype(bf16)
+        def body(*refs):
+            total = contract(refs[0][...], refs[1][...], *self.over)
+            for i in range(2, len(refs) - 1, 2):
+                total = total + contract(refs[i][...], refs[i + 1][...], *self.over)
+            refs[-1][...] = total.astype(bf16)
 
         def tile(size, over, index):
+            def at(i, j):
+                return (i + self.skip, j)[index]
+
             if over == 0:
-                return pl.BlockSpec((self.depth, size), lambda i, j: (0, (i, j)[index]))
-            return pl.BlockSpec((size, self.depth), lambda i, j: ((i, j)[index], 0))
-
+                return pl.BlockSpec((self.depth, size), lambda i, j: (0, at(i, j)))
+            return pl.BlockSpec((size, self.depth), lambda i, j: (at(i, j), 0))
+
+        pair = [tile(self.tm, self.over[0], 0), tile(self.tn, self.over[1], 1)]
         pltpu.emit_pipeline(
             body,
             grid=self.grid,
-            in_specs=[tile(self.tm, self.over[0], 0), tile(self.tn, self.over[1], 1)],
+            in_specs=pair * (len(self.inputs) // 2),
             out_specs=[pl.BlockSpec((self.tm, self.tn), lambda i, j: (i, j))],
         )(*self.refs)
 
@@ -620,7 +637,7 @@
                 collective_id=self.calls, has_side_effects=True, vmem_limit_bytes=room << 20
             ),
             cost_estimate=pl.CostEstimate(
-                flops=0, bytes_accessed=60 * max(job.bytes for job in jobs), transcendentals=0
+                flops=0, bytes_accessed=12 * max(job.bytes for job in jobs), transcendentals=0
             ),
             name="net",
         )(*ins)
@@ -654,31 +671,24 @@
     )(me.reshape(1), *([weight] * groups))
 
 
-def spread_columns(pieces, count, each, block_rows):
-    devices, rows, _ = pieces[0].shape
-    groups = len(pieces)
-    if each % 128:
-        cut = jnp.stack(pieces).reshape(groups, devices, rows, count, each)
-        return jnp.transpose(cut, (2, 0, 3, 1, 4)).reshape(rows, -1).astype(f32)
+def spread_columns(arrays, groups, group, count, each, block_rows):
+    devices, rows, _ = arrays[0].shape
     wide = devices * each
 
     def kernel(in_ref, *refs):
         for j in range(devices):
             refs[-1][:, j * each : (j + 1) * each] = in_ref[j].astype(f32)
 
-    out = None
-    for g, piece in enumerate(pieces):
-        out = pl.pallas_call(
-            kernel,
-            grid=(count, rows // block_rows),
-            in_specs=[pl.BlockSpec((devices, block_rows, each), lambda i, r: (0, r, i))]
-            + ([] if out is None else [pl.BlockSpec(memory_space=pl.ANY)]),
-            out_specs=pl.BlockSpec((block_rows, wide), lambda i, r, g=g: (r, g * count + i)),
-            out_shape=jax.ShapeDtypeStruct((rows, groups * count * wide), f32),
-            input_output_aliases={} if out is None else {1: 0},
-            name="spread_columns",
-        )(*([piece] if out is None else [piece, out]))
-    return out
+    return pl.pallas_call(
+        kernel,
+        grid=(count, rows // block_rows),
+        in_specs=[pl.BlockSpec((devices, block_rows, each), lambda i, r: (0, r, i))]
+        + [pl.BlockSpec(memory_space=pl.ANY)] * (len(arrays) - 1),
+        out_specs=pl.BlockSpec((block_rows, wide), lambda i, r: (r, group * count + i)),
+        out_shape=jax.ShapeDtypeStruct((rows, groups * count * wide), f32),
+        input_output_aliases={1: 0} if len(arrays) > 1 else {},
+        name="spread_columns",
+    )(*arrays)
 
 
 def mm(left, right):
@@ -764,7 +774,7 @@
         attn_heads, lse, mems, nrms = attention_forward(qkv, gate, resets[0], memory, norms, segs)
 
         half = width // 2
-        w_d_left = gather_rows(tie(down_own[:, :half], attn_heads))
+        w_d = gather_rows(tie(down_own, attn_heads))
 
         def columns_of(ref, i):
             return ref.at[:, :, pl.ds(pl.multiple_of(i * my_width, my_width), my_width)]
@@ -772,7 +782,7 @@
         def tokens_of(ref, i):
             return ref.at[:, i]
 
-        attn, whole_o, w_d_right = net.run(
+        attn, whole_o = net.run(
             [
                 Exchange(
                     net.seq,
@@ -782,7 +792,6 @@
                     columns_of,
                 ),
                 Gather(net.seq, w_o.reshape(n_fsdp, out_rows, width), False),
-                Gather(net.fsdp, down_own[:, half:].reshape(4, my_hidden // 4, half), True),
             ]
         )
         attn = attn.reshape(rows, width)
@@ -796,8 +805,6 @@
         up_part = mm(h_two, w_u).astype(bf16)
         hidden = swiglu(gate_part.astype(f32), up_part.astype(f32)).astype(bf16)
 
-        w_d = jnp.concatenate([w_d_left, w_d_right.reshape(-1, half)], axis=1)
-
         def scatter_rows(parts):
             return lax.psum_scatter(parts, "fsdp", scatter_dimension=0, tiled=True)
 
@@ -807,19 +814,33 @@
         _, swiglu_back = jax.vjp(swiglu, gate_part.astype(f32), up_part.astype(f32))
         grad_gate, grad_up = swiglu_back(grad_hidden)
         grad_gate, grad_up = grad_gate.astype(bf16), grad_up.astype(bf16)
-        gate_parts = mm_tn(h_two, grad_gate).astype(bf16)
-        gate_term = scatter_rows(gate_parts)
-        grad_gate, grad_up, _ = lax.optimization_barrier((grad_gate, grad_up, gate_parts))
-        grad_h_two = (mm_nt(grad_gate, w_g) + mm_nt(grad_up, w_u)).astype(bf16)
-        grad_h_two, up_parts = net.run(
-            [
-                Scatter(net.seq, token_parts(grad_h_two), False, f32),
-                Product(h_two, grad_up, (0, 0), (1024, 512)),
-            ],
-            56,
-        )
+
+        def output_terms(s):
+            return Product([(hidden, w_d)], (1, 0), (512, 512), (s * seg, seg))
+
+        def h_two_terms(s):
+            pairs = [(grad_gate, w_g), (grad_up, w_u)]
+            return Product(pairs, (1, 1), (512, 512), (s * seg, seg))
+
+        gate_product = Product([(h_two, grad_gate)], (0, 0), (1024, 512))
+        up_product = Product([(h_two, grad_up)], (0, 0), (1024, 512))
+        beside = [[output_terms(s)] for s in range(1, segs)]
+        beside += [[h_two_terms(s)] for s in range(segs)] + [[up_product]]
+        beside[0].append(gate_product)
+        terms = mm(hidden[:seg], tie(w_d, grad_up)).astype(bf16)
+        sums, gate_parts = [], None
+        for products in beside:
+            parts = terms.reshape(n_seq, 2, local // 2, width)
+            results = net.run([Scatter(net.seq, parts, True, f32)] + products, 56)
+            sums.append(results[0])
+            terms = results[1]
+            if products[-1] is gate_product:
+                gate_parts = results[-1]
+                gate_term = scatter_rows(gate_parts)
+        up_parts = terms
         up_term = scatter_rows(up_parts)
-        grad_h_two = grad_h_two.reshape(rows, width)
+        output = jnp.stack(sums[:segs]).reshape(rows, width)
+        grad_h_two = jnp.stack(sums[segs:]).reshape(rows, width)
 
         gain_ffn_term = jnp.sum(grad_h_two * r_two, axis=0)
         _, norm_two_back = jax.vjp(rms, x_one)
@@ -827,7 +848,7 @@
         grad_o = grad_x_one.astype(bf16)
 
         grad_attn_parts = mm_nt(grad_o, whole_o).astype(bf16)
-        grad_attn, output = net.run(
+        grad_attn, out_parts = net.run(
             [
                 Exchange(
                     net.seq,
@@ -836,38 +857,37 @@
                     columns_of,
                     tokens_of,
                 ),
-                Product(hidden, w_d, (1, 0), (1024, 512)),
+                Product([(attn, grad_o)], (0, 0), (1024, 512)),
             ],
             56,
         )
-        grad_attn = grad_attn.reshape(total_rows, my_width)
+        grad_attn = tie(grad_attn.reshape(total_rows, my_width), down_term)
         grads_q, grads_k, grads_v, bias_terms = attention_backward(
             qkv, grad_attn, gate, resets[0], depth, lse, mems, nrms, segs
         )
         grad_qkv_rows = jnp.concatenate([grads_q, grads_k, grads_v], axis=1)
-        out_parts = mm_tn(attn, tie(grad_o, grads_q)).astype(bf16)
         out_sum, qkv_parts, grad_h_one = net.run(
             [
                 Scatter(net.seq, out_parts.reshape(n_fsdp, n_seq, out_rows, width), False, bf16),
-                Product(h_one, grad_qkv_rows, (0, 0), (1024, 512)),
-                Product(grad_qkv_rows, w_q, (1, 1), (1024, 512)),
+                Product([(h_one, grad_qkv_rows)], (0, 0), (1024, 512)),
+                Product([(grad_qkv_rows, w_q)], (1, 1), (1024, 512)),
             ],
             56,
         )
-        grad_h_one, output, qkv_term, out_term, down_all = net.run(
+        grad_h_one, qkv_term, out_term, down_all, gate_all = net.run(
             [
                 Scatter(net.seq, token_parts(grad_h_one), False, f32),
-                Scatter(net.seq, token_parts(output), False, f32),
                 Scatter(
-                    net.fsdp, qkv_parts.reshape(n_fsdp, 4, shard // 4, 3 * my_width), True, bf16
+                    net.fsdp, qkv_parts.reshape(n_fsdp, 4, shard // 4, 3 * my_width), True, bf16, 5
                 ),
-                Scatter(net.fsdp, out_sum[:, None], True, bf16),
+                Scatter(net.fsdp, out_sum[:, None], True, bf16, 2),
                 Gather(net.seq, down_term[None], True),
+                Gather(net.seq, gate_term[None], True),
             ],
             56,
         )
         grad_h_one = grad_h_one.reshape(rows, width)
-        output = (x_one + output.reshape(rows, width)).astype(bf16).reshape(tokens.shape)
+        output = (x_one + output).astype(bf16).reshape(tokens.shape)
         qkv_term = qkv_term.reshape(shard, 3 * my_width)
         out_term = out_term.reshape(out_rows, width)
         gain_attn_term = jnp.sum(grad_h_one * r_one, axis=0)
@@ -875,24 +895,45 @@
         grad_x = grad_x_one + norm_one_back(grad_h_one * gain_attn)[0]
         input_grad = grad_x.astype(bf16).reshape(tokens.shape)
 
-        qkv_all, out_all, gate_all = net.run(
-            [Gather(net.seq, term[None], True) for term in (qkv_term, out_term, gate_term)]
-        )
-        (up_all,) = net.run([Gather(net.seq, up_term[None], True)])
+        bias_all = lax.dynamic_update_slice(
+            jnp.zeros((heads,), f32), bias_terms[:, 0, 0], (me * my_heads,)
+        )
+        small = jnp.concatenate([gain_attn_term, gain_ffn_term, bias_all])
+        wide = -(-small.shape[0] // 1024) * 128
+        small = jnp.pad(small, (0, 8 * wide - small.shape[0])).reshape(1, 8, wide)
+
+        qkv_all, out_all, small = net.run(
+            [
+                Gather(net.seq, qkv_term[None], True),
+                Gather(net.seq, out_term[None], True),
+                Gather(net.seq, small, True),
+            ]
+        )
         down_all = down_all.reshape(hidden_shard, width).astype(f32)
         out_all = out_all.reshape(shard, width).astype(f32)
-        gate_up_all = spread_columns([gate_all[:, 0], up_all[:, 0]], n_fsdp, my_hidden, shard)
-        qkv_all = spread_columns([qkv_all[:, 0]], 3, my_width, shard // 2)
-
-        bias_all = lax.dynamic_update_slice(
-            jnp.zeros((heads,), f32), bias_terms[:, 0, 0], (me * my_heads,)
-        )
-        small = jnp.concatenate([gain_attn_term, gain_ffn_term, bias_all])
-        for axis, n in (("seq", n_seq), ("fsdp", n_fsdp)):
-            k = 1
-            while k < n:
-                small = small + lax.ppermute(small, axis, [(i, i ^ k) for i in range(n)])
-                k *= 2
+        qkv_all = spread_columns([qkv_all[:, 0]], 1, 0, 3, my_width, shard // 2)
+        aligned = my_hidden % 128 == 0
+        gate_up_all = gate_all[:, 0]
+        if aligned:
+            gate_up_all = spread_columns([gate_up_all], 2, 0, n_fsdp, my_hidden, shard)
+        up_term = tie(
+            up_term, down_all, out_all, qkv_all, gate_up_all, output, input_grad, small
+        )
+        up_all, small = net.run(
+            [
+                Gather(net.seq, up_term[None], True),
+                Gather(net.fsdp, jnp.sum(small, axis=0), True),
+            ]
+        )
+        small = jnp.sum(small, axis=0).reshape(-1)
+        if aligned:
+            last = [up_all[:, 0], gate_up_all]
+            gate_up_all = spread_columns(last, 2, 1, n_fsdp, my_hidden, shard)
+        else:
+            cut = jnp.stack([gate_up_all, up_all[:, 0]])
+            cut = cut.reshape(2, n_seq, shard, n_fsdp, my_hidden)
+            gate_up_all = jnp.transpose(cut, (2, 0, 3, 1, 4)).reshape(shard, -1).astype(f32)
+
         return (
             output,
             input_grad,
@@ -902,7 +943,7 @@
             down_all,
             small[:width],
             small[width : 2 * width],
-            small[2 * width :],
+            small[2 * width : 2 * width + heads],
         )
 
     return body

time: 1160 us -> 1090 us (0.940)
  matrix products: 216 us -> 148 us
  Pallas kernels: 818 us -> 833 us
  starting transfers between devices: 12.1 us -> 0.46 us
    dot_general x4 -> x2, matrix products: 89.4 us -> 38.8 us  [mm_nt(): lax.dot_general(left, right, (((1,), (1,)), ((), ())), preferred_element_...]
    dot_general x3 -> x1, matrix products: 50.3 us -> 22.2 us  [mm_tn(): lax.dot_general(left, right, (((0,), (0,)), ((), ())), preferred_element_...]
    pallas_call x9 -> x12, Pallas kernels: 735 us -> 750 us  [run(): pl.pallas_call(kernel, in_specs=[anywhere] * len(ins), out_specs=[anywher...]
    dot_general x4 -> x5, matrix products: 76.4 us -> 87.3 us  [mm(): return jnp.dot(left, right, preferred_element_type=f32)]
    unnamed x100 -> x88, local copies, waits for them, and re-layouts: 35.4 us -> 29.7 us
  transfers between devices with their start and end apart: 11 -> 6, of which waited for: 2 -> 1; matrix products, arithmetic and copies ran while one was open for 23% -> 18% of each run, Pallas kernels for 71% -> 72%
where the time goes in v4:
time: 1090 us; the launch traced here: 1080 us
  Pallas kernels  833 us (76%)
  matrix products  148 us (14%)
  other arithmetic  41 us (4%)
  local copies, waits for them, and re-layouts  35.1 us (3%)
  between operations  16.4 us (2%)
    pallas_call x12, Pallas kernels, run(): pl.pallas_call(kernel, in_specs=[anywhere] * len(ins), out_specs=[anywher...  750 us
    dot_general x5, matrix products, mm(): return jnp.dot(left, right, preferred_element_type=f32)  87.3 us
    dot_general x2, matrix products, mm_nt(): lax.dot_general(left, right, (((1,), (1,)), ((), ())), preferred_element_...  38.8 us
    pallas_call x1, Pallas kernels, attention_backward(): pl.pallas_call(functools.partial(backward_kernel, min(256, seg), segs), g...  33.9 us
    unnamed x88, local copies, waits for them, and re-layouts  29.7 us
    dot_general x1, matrix products, mm_tn(): lax.dot_general(left, right, (((0,), (0,)), ((), ())), preferred_element_...  22.2 us
  transfers between devices with their start and end apart: 6, of which 1 were waited for; matrix products, arithmetic and copies ran while one was open for 18% of the time, Pallas kernels for 72%

profile of v4, /device:TPU:0, one launch (start us, length us, event | category | flops | bytes accessed | tf_op | source)
XLA Modules:
  0.0 1079.5 jit_solution(5093231669966698697)
XLA Ops:
  7.2 5.9 own_columns.3
  21.1 196.3 %net.12 = (bf16[2,4,256,2048]{3,2,1,0:T(8,128)(2,1)S(1)}, bf16[2,4,256,2048]{3,2,1,0:T(8,128)(2,1)}, bf16[8,1,64,2048]{3,2,1,0:T(8,128)(2,1)S(1)}, bf16[8,4,64,1536]{3,2,1,0:T(8,128)(2,1)S(1)}) custom-call(bf16[2,256,2048]{2,1,0:T(8,128)(2,1)S(1)} %fusion.18.refs_0_, bf16[2,256,2048]{2,1,0:T(8,128)(2,1)S(1)} %bitcast.123, ...), custom_call_target="tpu_custom_call" | custom-call | bytes 25165824 | tf_op jit(solution)/shard_map/net/pallas_call | solution.py:630
  229.7 18.6 %convolution_convert_fusion.3.q_ref.k_ref.v_ref = bf16[2048,1536]{1,0:T(8,128)(2,1)} fusion(bf16[2048,2048]{1,0:T(8,128)(2,1)} %bitcast.124, bf16[2048,1536]{1,0:T(8,128)(2,1)} %bitcast.127), kind=kOutput, calls=%fused_computation.17 | convolution fusion | flops 12888047616 | bytes 20971520 | tf_op jit(solution)/shard_map/dot_general | solution.py:695
  248.3 19.8 %attention_forward.1 = (bf16[2048,512]{1,0:T(8,128)(2,1)S(1)}, f32[4,2,1,1024]{3,2,1,0:T(1,128)S(1)}, f32[4,2,128,128]{3,2,1,0:T(8,128)S(1)}, f32[4,2,1,128]{3,2,1,0:T(1,128)S(1)}) custom-call(f32[4]{0:T(128)S(1)} %add_divide_fusion.gate, s32[1]{0:T(128)} %bitcast.117.resets, bf16[2048,1536]{1,0:T(8,128)(2,1)} %convolution_convert_fusion.3.q_ref.k_ref.v_ref, ...), custom_call_target="tpu_custom_call" | custom-call | flops 4026531840 | bytes 12582912 | tf_op jit(solution)/shard_map/attention_forward/pallas_call | solution.py:133
  272.9 72.2 %net.13 = (bf16[2,256,2048]{2,1,0:T(8,128)(2,1)S(1)}, bf16[8,4,64,2048]{3,2,1,0:T(8,128)(2,1)S(1)}) custom-call(bf16[2,4,256,512]{3,2,1,0:T(8,128)(2,1)S(1)} %bitcast.135, bf16[8,64,2048]{2,1,0:T(8,128)(2,1)S(1)} %bitcast.134), custom_call_target="tpu_custom_call" | custom-call | bytes 25165824 | tf_op jit(solution)/shard_map/net/pallas_call | solution.py:630
  345.2 4.6 multiply_reduce_fusion.1
  351.8 50.3 %net.14 = bf16[2,4,256,2048]{3,2,1,0:T(8,128)(2,1)S(1)} custom-call(bf16[2,256,2048]{2,1,0:T(8,128)(2,1)S(1)} %bitcast.126), custom_call_target="tpu_custom_call" | custom-call | bytes 25165824 | tf_op jit(solution)/shard_map/net/pallas_call | solution.py:630
  405.5 23.6 %convolution_convert_fusion.2 = bf16[2048,2048]{1,0:T(8,128)(2,1)} fusion(bf16[2048,2048]{1,0:T(8,128)(2,1)} %bitcast.119, bf16[2048,2048]{1,0:T(8,128)(2,1)} %all-gather.4.cloned.1.call-done.refs_2_), kind=kOutput, calls=%fused_computation.16 | convolution fusion | flops 17184063488 | bytes 25165824 | tf_op jit(solution)/shard_map/dot_general | solution.py:695
  429.1 26.5 %fusion = (bf16[2048,2048]{1,0:T(8,128)(2,1)S(1)}, bf16[2048,2048]{1,0:T(8,128)(2,1)}) fusion(bf16[2048,2048]{1,0:T(8,128)(2,1)} %convolution_convert_fusion.2, bf16[2048,2048]{1,0:T(8,128)(2,1)} %bitcast.120, bf16[2048,2048]{1,0:T(8,128)(2,1)} %all-gather.6.cloned.1.call-done.refs_4_), kind=kOutput, calls=%fused_computation.6 | convolution fusion | flops 17217617920 | bytes 41943040 | tf_op jit(solution)/shard_map/dot_general | solution.py:695
  458.9 22.2 %convolution_convert_fusion = bf16[2048,2048]{1,0:T(8,128)(2,1)} fusion(bf16[2048,2048]{1,0:T(8,128)(2,1)S(1)} %get-tuple-element.115.refs_1_, bf16[2048,2048]{1,0:T(8,128)(2,1)} %bitcast.165), kind=kOutput, calls=%fused_computation.14 | convolution fusion | flops 17184063488 | bytes 25165824 | tf_op jit(solution)/shard_map/dot_general | solution.py:703
  481.1 4.9 all-gather.8.cloned.1.call-done.refs_2_
  486.0 32.8 %fusion.6 = (bf16[2048,2048]{1,0:T(8,128)(2,1)}, bf16[2048,2048]{1,0:T(8,128)(2,1)}) fusion(bf16[2048,2048]{1,0:T(8,128)(2,1)} %convolution_convert_fusion.2, bf16[2048,2048]{1,0:T(8,128)(2,1)} %get-tuple-element.116, bf16[2048,2048]{1,0:T(8,128)(2,1)} %bitcast.166, bf16[2048,2048]{1,0:T(8,128)(2,1)} %all-gather.8.cloned.1.call-done.refs_2_), kind=kOutput, calls=%fused_computation.12 | convolution fusion | flops 17246978048 | bytes 50331648 | tf_op jit(solution)/shard_map/dot_general | solution.py:699
  518.9 13.9 %fusion.21 = bf16[1024,2048]{1,0:T(8,128)(2,1)} fusion(bf16[2048,2048]{1,0:T(8,128)(2,1)} %all-gather.8.cloned.1.call-done.refs_2_, bf16[2048,2048]{1,0:T(8,128)(2,1)} %copy-done.28), kind=kOutput, calls=%fused_computation.50 | convolution fusion | flops 8592031744 | bytes 16777216 | tf_op jit(solution)/shard_map/dot_general | solution.py:695
  532.8 45.2 %net.15 = (f32[2,128,2048]{2,1,0:T(8,128)}, bf16[1024,2048]{1,0:T(8,128)(2,1)}, bf16[2048,2048]{1,0:T(8,128)(2,1)}) custom-call(bf16[4,2,128,2048]{3,2,1,0:T(8,128)(2,1)} %bitcast.151, bf16[2048,2048]{1,0:T(8,128)(2,1)} %copy-done.28, bf16[2048,2048]{1,0:T(8,128)(2,1)} %all-gather.8.cloned.1.call-done.refs_2_, bf16[2048,2048]{1,0:T(8,128)(2,1)} %bitcast.121, ...), custom_call_target="tpu_custom_call" | custom-call | bytes 12582912 | tf_op jit(solution)/shard_map/net/pallas_call | solution.py:630
  578.1 31.6 %net.16 = (f32[2,128,2048]{2,1,0:T(8,128)}, bf16[1024,2048]{1,0:T(8,128)(2,1)}) custom-call(bf16[4,2,128,2048]{3,2,1,0:T(8,128)(2,1)} %bitcast.148, bf16[2048,2048]{1,0:T(8,128)(2,1)} %get-tuple-element.103.refs_4_.refs_1_, bf16[2048,2048]{1,0:T(8,128)(2,1)} %all-gather.4.cloned.1.call-done.refs_2_, bf16[2048,2048]{1,0:T(8,128)(2,1)} %get-tuple-element.104.refs_3_.refs_2_, ...), custom_call_target="tpu_custom_call" | custom-call | bytes 12582912 | tf_op jit(solution)/shard_map/net/pallas_call | solution.py:630
  609.7 30.0 %net.17 = (f32[2,128,2048]{2,1,0:T(8,128)}, bf16[1024,2048]{1,0:T(8,128)(2,1)}) custom-call(bf16[4,2,128,2048]{3,2,1,0:T(8,128)(2,1)} %bitcast.150, bf16[2048,2048]{1,0:T(8,128)(2,1)} %get-tuple-element.103.refs_4_.refs_1_, bf16[2048,2048]{1,0:T(8,128)(2,1)} %all-gather.4.cloned.1.call-done.refs_2_, bf16[2048,2048]{1,0:T(8,128)(2,1)} %get-tuple-element.104.refs_3_.refs_2_, ...), custom_call_target="tpu_custom_call" | custom-call | bytes 12582912 | tf_op jit(solution)/shard_map/net/pallas_call | solution.py:630
  639.7 30.0 %net.18 = (f32[2,128,2048]{2,1,0:T(8,128)}, bf16[2048,2048]{1,0:T(8,128)(2,1)}) custom-call(bf16[4,2,128,2048]{3,2,1,0:T(8,128)(2,1)} %bitcast.149, bf16[2048,2048]{1,0:T(8,128)(2,1)} %bitcast.122, bf16[2048,2048]{1,0:T(8,128)(2,1)} %get-tuple-element.104.refs_3_.refs_2_), custom_call_target="tpu_custom_call" | custom-call | bytes 12582912 | tf_op jit(solution)/shard_map/net/pallas_call | solution.py:630
  670.4 6.6 pad_maximum_fusion.1
  682.4 6.0 convolution_convert_fusion.4
  688.3 25.9 %net.19 = (bf16[2,4,256,512]{3,2,1,0:T(8,128)(2,1)}, bf16[2048,2048]{1,0:T(8,128)(2,1)}) custom-call(bf16[2,256,2048]{2,1,0:T(8,128)(2,1)} %bitcast.155, bf16[512,2048]{1,0:T(8,128)(2,1)} %bitcast.133, bf16[512,2048]{1,0:T(8,128)(2,1)} %copy-done.27), custom_call_target="tpu_custom_call" | custom-call | bytes 12582912 | tf_op jit(solution)/shard_map/net/pallas_call | solution.py:630
  714.3 33.9 %attention_backward.1 = (bf16[2048,512]{1,0:T(8,128)(2,1)S(1)}, bf16[2048,512]{1,0:T(8,128)(2,1)S(1)}, bf16[2048,512]{1,0:T(8,128)(2,1)}, f32[4,8,128]{2,1,0:T(8,128)S(1)}) custom-call(f32[4]{0:T(128)S(1)} %add_divide_fusion.gate, s32[1]{0:T(128)} %bitcast.118.resets, s32[1]{0:T(128)S(6)} %copy.28.depth, ...), custom_call_target="tpu_custom_call" | custom-call | flops 8053063680 | bytes 12582912 | tf_op jit(solution)/shard_map/attention_backward/pallas_call | solution.py:266
  748.1 4.4 pad_maximum_fusion.refs_2_.refs_3_
  752.5 50.9 %net.20 = (bf16[8,64,2048]{2,1,0:T(8,128)(2,1)}, bf16[2048,1536]{1,0:T(8,128)(2,1)}, bf16[2048,2048]{1,0:T(8,128)(2,1)}) custom-call(bf16[8,4,64,2048]{3,2,1,0:T(8,128)(2,1)} %bitcast.144, bf16[2048,2048]{1,0:T(8,128)(2,1)} %bitcast.125, bf16[2048,1536]{1,0:T(8,128)(2,1)} %pad_maximum_fusion.refs_2_.refs_3_, ...), custom_call_target="tpu_custom_call" | custom-call | bytes 25165824 | tf_op jit(solution)/shard_map/net/pallas_call | solution.py:630
  803.5 143.5 %net.21 = (f32[2,256,2048]{2,1,0:T(8,128)}, bf16[4,64,1536]{2,1,0:T(8,128)(2,1)}, bf16[1,64,2048]{2,1,0:T(8,128)(2,1)}, bf16[4,1,256,2048]{3,2,1,0:T(8,128)(2,1)}, bf16[4,1,256,2048]{3,2,1,0:T(8,128)(2,1)}) custom-call(bf16[2,4,256,2048]{3,2,1,0:T(8,128)(2,1)} %bitcast.145, bf16[8,4,64,1536]{3,2,1,0:T(8,128)(2,1)} %bitcast.146, ...), custom_call_target="tpu_custom_call" | custom-call | bytes 25165824 | tf_op jit(solution)/shard_map/net/pallas_call | solution.py:630
  950.3 3.5 fusion.19
  955.0 26.8 %net.22 = (bf16[4,1,256,1536]{3,2,1,0:T(8,128)(2,1)S(1)}, bf16[4,1,64,2048]{3,2,1,0:T(8,128)(2,1)S(1)}, f32[4,1,8,640]{3,2,1,0:T(8,128)S(1)}) custom-call(bf16[1,256,1536]{2,1,0:T(8,128)(2,1)S(1)} %bitcast.137, bf16[1,64,2048]{2,1,0:T(8,128)(2,1)S(1)} %copy-done.16, f32[1,8,640]{2,1,0:T(8,128)S(1)} %reshape.220.refs_2_), custom_call_target="tpu_custom_call" | custom-call | bytes 9437184 | tf_op jit(solution)/shard_map/net/pallas_call | solution.py:630
  983.5 5.8 spread_columns.3
  989.3 7.3 spread_columns.4.refs_0_
  998.3 7.8 bitcast_convert_fusion
  1006.8 6.2 fusion.9
  1014.2 47.6 %net.23 = (bf16[4,1,256,2048]{3,2,1,0:T(8,128)(2,1)S(1)}, f32[8,1,8,640]{3,2,1,0:T(8,128)S(1)}) custom-call(bf16[1,256,2048]{2,1,0:T(8,128)(2,1)S(1)} %bitcast.136, f32[1,8,640]{2,1,0:T(8,128)S(1)} %bitcast.138), custom_call_target="tpu_custom_call" | custom-call | bytes 12582912 | tf_op jit(solution)/shard_map/net/pallas_call | solution.py:630
  1064.9 7.4 spread_columns.5
  (133 shorter events, 51.3 us)
Async XLA Ops:
  7.2 11.8 %copy-start = (bf16[256,2048]{1,0:T(8,128)(2,1)S(1)}, bf16[256,2048]{1,0:T(8,128)(2,1)}, u32[]{:S(2)}) copy-start(bf16[256,2048]{1,0:T(8,128)(2,1)} %param.16) | copy-start | bytes 3145732
  7.2 398.4 %all-gather.4.cloned.1.call-start = ((), (), s32[]{:S(2)}) async-start(), calls=%async_computation.3 | async-start | bytes 9437184 | tf_op jit(solution)/shard_map/all_gather | solution.py:748
  13.2 5.8 copy-start.31
  13.2 415.9 %all-gather.6.cloned.1.call-start = ((), (), s32[]{:S(2)}) async-start(), calls=%async_computation.4 | async-start | bytes 9437184 | tf_op jit(solution)/shard_map/all_gather | solution.py:748
  16.1 5.0 copy-start.3
  16.1 5.0 copy-start.7
  21.1 204.5 %copy-start.40 = (f32[16]{0:T(128)S(1)}, f32[16]{0:T(128)}, u32[]{:S(2)}) copy-start(f32[16]{0:T(128)} %param.21) | copy-start | bytes 196
  217.5 3.4 copy-start.4
  224.9 261.1 %all-gather.8.cloned.1.call-start = ((), (), s32[]{:S(2)}) async-start(), calls=%async_computation.5 | async-start | bytes 9437184 | tf_op jit(solution)/shard_map/all_gather | solution.py:748
  269.4 444.8 %reduce-scatter.4.cloned.1.call-start = ((), (), s32[]{:S(2)}) async-start(), calls=%async_computation.6 | async-start | bytes 9437184 | tf_op jit(solution)/shard_map/reduce_scatter | solution.py:809
  272.9 72.3 %copy-start.23 = (bf16[1,2,256,2048]{3,2,1,0:T(8,128)(2,1)S(1)}, bf16[1,2,256,2048]{3,2,1,0:T(8,128)(2,1)}, u32[]{:S(2)}) copy-start(bf16[1,2,256,2048]{3,2,1,0:T(8,128)(2,1)} %param.13) | copy-start | bytes 6291460
  345.1 4.7 copy-start.9
  345.1 4.7 copy-start.17
  345.1 4.7 copy-start.29
  349.8 52.3 %copy-start.38 = (f32[512]{0:T(512)}, f32[512]{0:T(512)S(1)}, u32[]{:S(2)}) copy-start(f32[512]{0:T(512)S(1)} %get-tuple-element.113) | copy-start | bytes 6148
  349.8 52.3 %copy-start.33 = (f32[512]{0:T(512)}, f32[512]{0:T(512)S(1)}, u32[]{:S(2)}) copy-start(f32[512]{0:T(512)S(1)} %fusion.24) | copy-start | bytes 6148
  402.1 3.4 copy-start.2
  481.1 322.4 %reduce-scatter.6.cloned.1.call-start = ((), (), s32[]{:S(2)}) async-start(), calls=%async_computation.7 | async-start | bytes 9437184 | tf_op jit(solution)/shard_map/reduce_scatter | solution.py:809
  578.1 434.9 %reduce-scatter.8.cloned.1.call-start = ((), (), s32[]{:S(2)}) async-start(), calls=%async_computation.8 | async-start | bytes 9437184 | tf_op jit(solution)/shard_map/reduce_scatter | solution.py:809
  670.4 6.6 copy-start.19
  670.4 6.6 copy-start.30
  670.4 6.6 copy-start.34
  677.0 3.7 slice-start
  682.4 6.0 copy-start.27
  803.5 143.5 %copy-start.24 = (bf16[1,2,256,2048]{3,2,1,0:T(8,128)(2,1)S(1)}, bf16[1,2,256,2048]{3,2,1,0:T(8,128)(2,1)}, u32[]{:S(2)}) copy-start(bf16[1,2,256,2048]{3,2,1,0:T(8,128)(2,1)} %param.13) | copy-start | bytes 6291460
  803.5 143.5 %copy-start.32 = (f32[2048]{0:T(1024)S(1)}, f32[2048]{0:T(1024)}, u32[]{:S(2)}) copy-start(f32[2048]{0:T(1024)} %param.19) | copy-start | bytes 24580
  950.0 3.9 copy-start.16
  996.6 9.4 copy-start.26
  998.3 7.8 copy-start.20
  998.3 7.8 copy-start.22
  998.3 8.5 copy-start.25
  1064.9 7.4 copy-start.1
  (17 other events, 32.6 us)
Sparse Core Ops, SparseCore 0:
  13.3 204.5 all-gather.3
  225.0 135.0 all-gather.5
  362.9 123.1 all-gather.7
  489.5 151.3 reduce-scatter.3
  644.8 147.9 reduce-scatter.5
  796.3 216.5 reduce-scatter.7

commit v5 on v4

--- a/solution.py
+++ b/solution.py
@@ -296,6 +296,24 @@
     )(gate, resets, depth, qkv, qkv, qkv, grad_attn, lse, mems, nrms)
 
 
+def ring_order(n):
+    if n % 4 or n < 8:
+        return list(range(n))
+    wide = n // 4
+    walk = []
+    for r in range(4):
+        cols = range(1, wide) if r % 2 == 0 else range(wide - 1, 0, -1)
+        walk += [r * wide + c for c in cols]
+    return walk + [r * wide for r in reversed(range(4))]
+
+
+def reorder(value, order, axis):
+    size = value.shape[axis] // len(order)
+    return jnp.concatenate(
+        [lax.slice_in_dim(value, i * size, (i + 1) * size, axis=axis) for i in order], axis=axis
+    )
+
+
 def tie(value, *others):
     return lax.optimization_barrier((value,) + others)[0]
 
@@ -643,52 +661,62 @@
         )(*ins)
 
 
-def own_columns(weight, me, groups, count, each):
-    shard = weight.shape[0]
+def own_columns(weight, me, groups, order, each):
+    shard, count = weight.shape[0], len(order)
     per = weight.shape[1] // (groups * count * each)
     if each % 128:
         cut = weight.reshape(shard, groups, count, per, each)
         cut = lax.dynamic_index_in_dim(cut, me, 3, keepdims=False)
-        return [cut[:, g].reshape(shard, count * each) for g in range(groups)]
-
-    def kernel(me_ref, *refs):
+        return [reorder(cut[:, g], order, 1).reshape(shard, count * each) for g in range(groups)]
+
+    def kernel(me_ref, order_ref, *refs):
         for g in range(groups):
             refs[groups + g][...] = refs[g][...]
 
     def source(g):
-        return pl.BlockSpec((shard, each), lambda i, me_ref: (0, (g * count + i) * per + me_ref[0]))
+        def at(i, me_ref, order_ref):
+            return 0, (g * count + order_ref[i]) * per + me_ref[0]
+
+        return pl.BlockSpec((shard, each), at)
+
+    return pl.pallas_call(
+        kernel,
+        grid_spec=pltpu.PrefetchScalarGridSpec(
+            num_scalar_prefetch=2,
+            grid=(count,),
+            in_specs=[source(g) for g in range(groups)],
+            out_specs=[pl.BlockSpec((shard, each), lambda i, *refs: (0, i))] * groups,
+        ),
+        out_shape=[jax.ShapeDtypeStruct((shard, count * each), weight.dtype)] * groups,
+        name="own_columns",
+    )(me.reshape(1), jnp.array(order, jnp.int32), *([weight] * groups))
+
+
+def spread_columns(arrays, groups, group, order, each, block_rows):
+    devices, rows, _ = arrays[0].shape
+    wide, count = devices * each, len(order)
+
+    def kernel(order_ref, in_ref, *refs):
+        for j in range(devices):
+            refs[-1][:, j * each : (j + 1) * each] = in_ref[j].astype(f32)
 
     return pl.pallas_call(
         kernel,
         grid_spec=pltpu.PrefetchScalarGridSpec(
             num_scalar_prefetch=1,
-            grid=(count,),
-            in_specs=[source(g) for g in range(groups)],
-            out_specs=[pl.BlockSpec((shard, each), lambda i, me_ref: (0, i))] * groups,
+            grid=(count, rows // block_rows),
+            in_specs=[
+                pl.BlockSpec((devices, block_rows, each), lambda i, r, order_ref: (0, r, i))
+            ]
+            + [pl.BlockSpec(memory_space=pl.ANY)] * (len(arrays) - 1),
+            out_specs=pl.BlockSpec(
+                (block_rows, wide), lambda i, r, order_ref: (r, group * count + order_ref[i])
+            ),
         ),
-        out_shape=[jax.ShapeDtypeStruct((shard, count * each), weight.dtype)] * groups,
-        name="own_columns",
-    )(me.reshape(1), *([weight] * groups))
-
-
-def spread_columns(arrays, groups, group, count, each, block_rows):
-    devices, rows, _ = arrays[0].shape
-    wide = devices * each
-
-    def kernel(in_ref, *refs):
-        for j in range(devices):
-            refs[-1][:, j * each : (j + 1) * each] = in_ref[j].astype(f32)
-
-    return pl.pallas_call(
-        kernel,
-        grid=(count, rows // block_rows),
-        in_specs=[pl.BlockSpec((devices, block_rows, each), lambda i, r: (0, r, i))]
-        + [pl.BlockSpec(memory_space=pl.ANY)] * (len(arrays) - 1),
-        out_specs=pl.BlockSpec((block_rows, wide), lambda i, r: (r, group * count + i)),
         out_shape=jax.ShapeDtypeStruct((rows, groups * count * wide), f32),
-        input_output_aliases={1: 0} if len(arrays) > 1 else {},
+        input_output_aliases={2: 0} if len(arrays) > 1 else {},
         name="spread_columns",
-    )(*arrays)
+    )(jnp.array(order, jnp.int32), *arrays)
 
 
 def mm(left, right):
@@ -734,18 +762,20 @@
         net = Net(n_seq, n_fsdp)
         me = lax.axis_index("seq")
 
-        (qkv_own,) = own_columns(w_qkv, me, 1, 3, my_width)
-        gate_own, up_own = own_columns(w_gate_up, me, 2, n_fsdp, my_hidden)
+        ring = ring_order(n_fsdp)
+        back = [ring.index(i) for i in range(n_fsdp)]
+        (qkv_own,) = own_columns(w_qkv, me, 1, range(3), my_width)
+        gate_own, up_own = own_columns(w_gate_up, me, 2, ring, my_hidden)
         down_own = lax.dynamic_slice(w_down, (me * my_hidden, 0), (my_hidden, width))
         out_own = lax.dynamic_slice(w_out, (me * out_rows, 0), (out_rows, width))
 
         x_flat = tokens.reshape(rows, width).astype(f32)
         r_one = rms(x_flat)
-        h_one_own = (r_one * gain_attn).astype(bf16)
+        h_one_own = reorder((r_one * gain_attn).astype(bf16), ring, 1)
         grad_y = cotangent.reshape(rows, width)
 
         def gather_rows(block):
-            return lax.all_gather(block, "fsdp", axis=0, tiled=True)
+            return lax.all_gather(block, "fsdp", axis=0, tiled=True, axis_index_groups=[ring])
 
         def token_parts(value):
             return value.reshape(segs, n_seq, local, width)
@@ -753,19 +783,15 @@
         def gather_own(value):
             return Gather(net.seq, value.reshape(segs, local, width), False)
 
-        w_g = gather_rows(gate_own)
-        h_one, grad_y_all, w_o, w_q = net.run(
-            [
-                gather_own(h_one_own),
-                gather_own(grad_y),
-                Gather(net.fsdp, out_own.reshape(1, out_rows, width), True),
-                Gather(net.fsdp, qkv_own.reshape(4, shard // 4, 3 * my_width), True),
-            ]
-        )
+        w_o = gather_rows(tie(out_own, h_one_own))
+        w_q = gather_rows(tie(qkv_own, h_one_own))
+        (h_one,) = net.run([gather_own(h_one_own)])
         h_one = h_one.reshape(total_rows, width)
-        grad_y_all = grad_y_all.reshape(total_rows, width)
-        w_q = w_q.reshape(width, 3 * my_width)
-        w_u = gather_rows(tie(up_own, w_q))
+        w_g = gather_rows(tie(gate_own, h_one))
+        w_o = reorder(tie(w_o, h_one), back, 0)
+        (whole_o,) = net.run([Gather(net.seq, w_o.reshape(n_fsdp, out_rows, width), False)])
+        whole_o = whole_o.reshape(width, width)
+        w_u = gather_rows(tie(up_own, whole_o))
 
         qkv = mm(h_one, w_q).astype(bf16)
         gate = jax.nn.sigmoid(lax.dynamic_slice(gate_bias, (me * my_heads,), (my_heads,)))
@@ -782,7 +808,7 @@
         def tokens_of(ref, i):
             return ref.at[:, i]
 
-        attn, whole_o = net.run(
+        (attn,) = net.run(
             [
                 Exchange(
                     net.seq,
@@ -791,22 +817,25 @@
                     tokens_of,
                     columns_of,
                 ),
-                Gather(net.seq, w_o.reshape(n_fsdp, out_rows, width), False),
             ]
         )
         attn = attn.reshape(rows, width)
-        whole_o = whole_o.reshape(width, width)
         x_one = x_flat + mm(attn, whole_o)
         r_two = rms(x_one)
-        h_two_own = (r_two * gain_ffn).astype(bf16)
+        h_two_own = reorder((r_two * gain_ffn).astype(bf16), ring, 1)
         (h_two,) = net.run([gather_own(h_two_own)])
         h_two = h_two.reshape(total_rows, width)
-        gate_part = mm(h_two, w_g).astype(bf16)
+        grad_y_all, gate_part = net.run(
+            [gather_own(tie(grad_y, h_two)), Product([(h_two, w_g)], (1, 0), (1024, 512))], 56
+        )
+        grad_y_all = grad_y_all.reshape(total_rows, width)
         up_part = mm(h_two, w_u).astype(bf16)
         hidden = swiglu(gate_part.astype(f32), up_part.astype(f32)).astype(bf16)
 
         def scatter_rows(parts):
-            return lax.psum_scatter(parts, "fsdp", scatter_dimension=0, tiled=True)
+            return lax.psum_scatter(
+                parts, "fsdp", scatter_dimension=0, tiled=True, axis_index_groups=[ring]
+            )
 
         down_parts = mm_tn(hidden, grad_y_all).astype(bf16)
         down_term = scatter_rows(down_parts)
@@ -840,7 +869,7 @@
         up_parts = terms
         up_term = scatter_rows(up_parts)
         output = jnp.stack(sums[:segs]).reshape(rows, width)
-        grad_h_two = jnp.stack(sums[segs:]).reshape(rows, width)
+        grad_h_two = reorder(jnp.stack(sums[segs:]).reshape(rows, width), back, 1)
 
         gain_ffn_term = jnp.sum(grad_h_two * r_two, axis=0)
         _, norm_two_back = jax.vjp(rms, x_one)
@@ -866,6 +895,7 @@
             qkv, grad_attn, gate, resets[0], depth, lse, mems, nrms, segs
         )
         grad_qkv_rows = jnp.concatenate([grads_q, grads_k, grads_v], axis=1)
+        out_parts = tie(out_parts, gate_term)
         out_sum, qkv_parts, grad_h_one = net.run(
             [
                 Scatter(net.seq, out_parts.reshape(n_fsdp, n_seq, out_rows, width), False, bf16),
@@ -874,22 +904,19 @@
             ],
             56,
         )
-        grad_h_one, qkv_term, out_term, down_all, gate_all = net.run(
+        qkv_term = scatter_rows(qkv_parts)
+        grad_h_one, out_term, down_all, gate_all, up_all = net.run(
             [
-                Scatter(net.seq, token_parts(grad_h_one), False, f32),
-                Scatter(
-                    net.fsdp, qkv_parts.reshape(n_fsdp, 4, shard // 4, 3 * my_width), True, bf16, 5
-                ),
+                Scatter(net.seq, token_parts(tie(grad_h_one, up_term)), False, f32),
                 Scatter(net.fsdp, out_sum[:, None], True, bf16, 2),
                 Gather(net.seq, down_term[None], True),
                 Gather(net.seq, gate_term[None], True),
+                Gather(net.seq, up_term[None], True),
             ],
             56,
         )
-        grad_h_one = grad_h_one.reshape(rows, width)
+        grad_h_one = reorder(grad_h_one.reshape(rows, width), back, 1)
         output = (x_one + output).astype(bf16).reshape(tokens.shape)
-        qkv_term = qkv_term.reshape(shard, 3 * my_width)
-        out_term = out_term.reshape(out_rows, width)
         gain_attn_term = jnp.sum(grad_h_one * r_one, axis=0)
         _, norm_one_back = jax.vjp(rms, x_flat)
         grad_x = grad_x_one + norm_one_back(grad_h_one * gain_attn)[0]
@@ -902,37 +929,27 @@
         wide = -(-small.shape[0] // 1024) * 128
         small = jnp.pad(small, (0, 8 * wide - small.shape[0])).reshape(1, 8, wide)
 
+        down_all = down_all.reshape(hidden_shard, width).astype(f32)
+        aligned = my_hidden % 128 == 0
+        if aligned:
+            gate_up_all = spread_columns([gate_all[:, 0]], 2, 0, ring, my_hidden, shard)
+            gate_up_all = spread_columns([up_all[:, 0], gate_up_all], 2, 1, ring, my_hidden, shard)
+        else:
+            cut = jnp.stack([gate_all, up_all]).reshape(2, n_seq, shard, n_fsdp, my_hidden)
+            cut = reorder(cut, back, 3)
+            gate_up_all = jnp.transpose(cut, (2, 0, 3, 1, 4)).reshape(shard, -1).astype(f32)
+        qkv_term = tie(qkv_term, down_all, gate_up_all, output, input_grad)
+        (small,) = net.run([Gather(net.fsdp, small, True)])
         qkv_all, out_all, small = net.run(
             [
                 Gather(net.seq, qkv_term[None], True),
-                Gather(net.seq, out_term[None], True),
-                Gather(net.seq, small, True),
+                Gather(net.seq, out_term, True),
+                Gather(net.seq, jnp.sum(small, axis=0), True),
             ]
         )
-        down_all = down_all.reshape(hidden_shard, width).astype(f32)
+        small = jnp.sum(small, axis=0).reshape(-1)
         out_all = out_all.reshape(shard, width).astype(f32)
-        qkv_all = spread_columns([qkv_all[:, 0]], 1, 0, 3, my_width, shard // 2)
-        aligned = my_hidden % 128 == 0
-        gate_up_all = gate_all[:, 0]
-        if aligned:
-            gate_up_all = spread_columns([gate_up_all], 2, 0, n_fsdp, my_hidden, shard)
-        up_term = tie(
-            up_term, down_all, out_all, qkv_all, gate_up_all, output, input_grad, small
-        )
-        up_all, small = net.run(
-            [
-                Gather(net.seq, up_term[None], True),
-                Gather(net.fsdp, jnp.sum(small, axis=0), True),
-            ]
-        )
-        small = jnp.sum(small, axis=0).reshape(-1)
-        if aligned:
-            last = [up_all[:, 0], gate_up_all]
-            gate_up_all = spread_columns(last, 2, 1, n_fsdp, my_hidden, shard)
-        else:
-            cut = jnp.stack([gate_up_all, up_all[:, 0]])
-            cut = cut.reshape(2, n_seq, shard, n_fsdp, my_hidden)
-            gate_up_all = jnp.transpose(cut, (2, 0, 3, 1, 4)).reshape(shard, -1).astype(f32)
+        qkv_all = spread_columns([qkv_all[:, 0]], 1, 0, range(3), my_width, shard // 2)
 
         return (
             output,

time: 1090 us -> 951 us (0.87)
  Pallas kernels: 833 us -> 705 us
  local copies, waits for them, and re-layouts: 35.1 us -> 61.1 us
  matrix products: 148 us -> 126 us
    pallas_call x12 -> x14, Pallas kernels: 750 us -> 619 us  [run(): pl.pallas_call(kernel, in_specs=[anywhere] * len(ins), out_specs=[anywher...]
    dot_general x5 -> x4, matrix products: 87.3 us -> 66.9 us  [mm(): return jnp.dot(left, right, preferred_element_type=f32)]
    unnamed x88 -> x123, local copies, waits for them, and re-layouts: 29.7 us -> 47.9 us
  transfers between devices with their start and end apart: 6 -> 9, of which waited for: 1 -> 0; matrix products, arithmetic and copies ran while one was open for 18% -> 19% of each run, Pallas kernels for 72% -> 71%
where the time goes in v5:
time: 951 us; the launch traced here: 943 us
  Pallas kernels  705 us (74%)
  matrix products  126 us (13%)
  local copies, waits for them, and re-layouts  61.1 us (6%)
  other arithmetic  32.3 us (3%)
  between operations  16.5 us (2%)
    pallas_call x14, Pallas kernels, run(): pl.pallas_call(kernel, in_specs=[anywhere] * len(ins), out_specs=[anywher...  619 us
    dot_general x4, matrix products, mm(): return jnp.dot(left, right, preferred_element_type=f32)  66.9 us
    unnamed x123, local copies, waits for them, and re-layouts  47.9 us
    dot_general x2, matrix products, mm_nt(): lax.dot_general(left, right, (((1,), (1,)), ((), ())), preferred_element_...  38.8 us
    pallas_call x1, Pallas kernels, attention_backward(): pl.pallas_call(functools.partial(backward_kernel, min(256, seg), segs), g...  33.8 us
    pallas_call x3, Pallas kernels, spread_columns(): pl.pallas_call(kernel, grid_spec=pltpu.PrefetchScalarGridSpec(num_scalar_...  22.7 us
    dot_general x1, matrix products, mm_tn(): lax.dot_general(left, right, (((0,), (0,)), ((), ())), preferred_element_...  20.7 us
    pallas_call x1, Pallas kernels, attention_forward(): pl.pallas_call(functools.partial(forward_kernel, min(256, seg), segs), gr...  19.8 us
  transfers between devices with their start and end apart: 9, of which 0 were waited for; matrix products, arithmetic and copies ran while one was open for 19% of the time, Pallas kernels for 71%

profile of v5, /device:TPU:0, one launch (start us, length us, event | category | flops | bytes accessed | tf_op | source)
XLA Modules:
  0.0 942.6 jit_solution(6453936752311996231)
XLA Ops:
  14.5 3.5 own_columns.2
  18.1 51.7 %net.14 = bf16[2,4,256,2048]{3,2,1,0:T(8,128)(2,1)S(1)} custom-call(bf16[2,256,2048]{2,1,0:T(8,128)(2,1)S(1)} %bitcast.107), custom_call_target="tpu_custom_call" | custom-call | bytes 25165824 | tf_op jit(solution)/shard_map/net/pallas_call | solution.py:648
  73.3 6.5 own_columns.3
  87.6 49.6 %net.16 = bf16[8,4,64,2048]{3,2,1,0:T(8,128)(2,1)S(1)} custom-call(bf16[8,64,2048]{2,1,0:T(8,128)(2,1)S(1)} %bitcast.108), custom_call_target="tpu_custom_call" | custom-call | bytes 25165824 | tf_op jit(solution)/shard_map/net/pallas_call | solution.py:648
  145.5 18.6 %convolution_convert_fusion.2.q_ref.k_ref.v_ref = bf16[2048,1536]{1,0:T(8,128)(2,1)} fusion(bf16[2048,2048]{1,0:T(8,128)(2,1)} %bitcast.98, bf16[2048,1536]{1,0:T(8,128)(2,1)} %all-gather.6.cloned.1.call-done.refs_4_), kind=kOutput, calls=%fused_computation.16 | convolution fusion | flops 12888047616 | bytes 20971520 | tf_op jit(solution)/shard_map/dot_general | solution.py:723
  164.1 19.8 %attention_forward.1 = (bf16[2048,512]{1,0:T(8,128)(2,1)S(1)}, f32[4,2,1,1024]{3,2,1,0:T(1,128)S(1)}, f32[4,2,128,128]{3,2,1,0:T(8,128)S(1)}, f32[4,2,1,128]{3,2,1,0:T(1,128)S(1)}) custom-call(f32[4]{0:T(128)S(1)} %add_divide_fusion.gate, s32[1]{0:T(128)} %bitcast.92.resets, bf16[2048,1536]{1,0:T(8,128)(2,1)} %convolution_convert_fusion.2.q_ref.k_ref.v_ref, ...), custom_call_target="tpu_custom_call" | custom-call | flops 4026531840 | bytes 12582912 | tf_op jit(solution)/shard_map/attention_forward/pallas_call | solution.py:133
  184.2 25.7 %net.15 = bf16[2,256,2048]{2,1,0:T(8,128)(2,1)S(1)} custom-call(bf16[2,4,256,512]{3,2,1,0:T(8,128)(2,1)S(1)} %bitcast.110), custom_call_target="tpu_custom_call" | custom-call | bytes 12582912 | tf_op jit(solution)/shard_map/net/pallas_call | solution.py:648
  209.9 7.9 multiply_reduce_fusion.2
  220.0 49.8 %net.17 = bf16[2,4,256,2048]{3,2,1,0:T(8,128)(2,1)S(1)} custom-call(bf16[2,256,2048]{2,1,0:T(8,128)(2,1)S(1)} %bitcast.109), custom_call_target="tpu_custom_call" | custom-call | bytes 25165824 | tf_op jit(solution)/shard_map/net/pallas_call | solution.py:648
  273.1 72.2 %net.18 = (bf16[2,4,256,2048]{3,2,1,0:T(8,128)(2,1)}, bf16[2048,2048]{1,0:T(8,128)(2,1)}) custom-call(bf16[2,256,2048]{2,1,0:T(8,128)(2,1)} %bitcast.114, bf16[2048,2048]{1,0:T(8,128)(2,1)} %bitcast.94, bf16[2048,2048]{1,0:T(8,128)(2,1)} %all-gather.10.cloned.1.call-done.refs_2_), custom_call_target="tpu_custom_call" | custom-call | bytes 25165824 | tf_op jit(solution)/shard_map/net/pallas_call | solution.py:648
  345.4 26.5 %fusion = (bf16[2048,2048]{1,0:T(8,128)(2,1)S(1)}, bf16[2048,2048]{1,0:T(8,128)(2,1)}) fusion(bf16[2048,2048]{1,0:T(8,128)(2,1)} %get-tuple-element.63, bf16[2048,2048]{1,0:T(8,128)(2,1)} %bitcast.95, bf16[2048,2048]{1,0:T(8,128)(2,1)} %all-gather.12.cloned.1.call-done.refs_4_), kind=kOutput, calls=%fused_computation.6 | convolution fusion | flops 17217617920 | bytes 41943040 | tf_op jit(solution)/shard_map/dot_general | solution.py:723
  375.2 20.7 %convolution_convert_fusion = bf16[2048,2048]{1,0:T(8,128)(2,1)} fusion(bf16[2048,2048]{1,0:T(8,128)(2,1)S(1)} %get-tuple-element.126.refs_1_, bf16[2048,2048]{1,0:T(8,128)(2,1)S(1)} %bitcast.163), kind=kOutput, calls=%fused_computation.14 | convolution fusion | flops 17184063488 | bytes 25165824 | tf_op jit(solution)/shard_map/dot_general | solution.py:731
  396.0 32.9 %fusion.6 = (bf16[2048,2048]{1,0:T(8,128)(2,1)}, bf16[2048,2048]{1,0:T(8,128)(2,1)}) fusion(bf16[2048,2048]{1,0:T(8,128)(2,1)} %get-tuple-element.63, bf16[2048,2048]{1,0:T(8,128)(2,1)} %get-tuple-element.127, bf16[2048,2048]{1,0:T(8,128)(2,1)} %bitcast.162, bf16[2048,2048]{1,0:T(8,128)(2,1)} %all-gather.14.cloned.1.call-done.refs_2_), kind=kOutput, calls=%fused_computation.12 | convolution fusion | flops 17246978048 | bytes 50331648 | tf_op jit(solution)/shard_map/dot_general | solution.py:727
  428.8 13.9 %fusion.19 = bf16[1024,2048]{1,0:T(8,128)(2,1)} fusion(bf16[2048,2048]{1,0:T(8,128)(2,1)} %all-gather.14.cloned.1.call-done.refs_2_, bf16[2048,2048]{1,0:T(8,128)(2,1)} %copy-done.20), kind=kOutput, calls=%fused_computation.46 | convolution fusion | flops 8592031744 | bytes 16777216 | tf_op jit(solution)/shard_map/dot_general | solution.py:723
  442.7 44.7 %net.19 = (f32[2,128,2048]{2,1,0:T(8,128)}, bf16[1024,2048]{1,0:T(8,128)(2,1)}, bf16[2048,2048]{1,0:T(8,128)(2,1)}) custom-call(bf16[4,2,128,2048]{3,2,1,0:T(8,128)(2,1)} %bitcast.137, bf16[2048,2048]{1,0:T(8,128)(2,1)} %copy-done.20, bf16[2048,2048]{1,0:T(8,128)(2,1)} %all-gather.14.cloned.1.call-done.refs_2_, bf16[2048,2048]{1,0:T(8,128)(2,1)} %bitcast.96, ...), custom_call_target="tpu_custom_call" | custom-call | bytes 12582912 | tf_op jit(solution)/shard_map/net/pallas_call | solution.py:648
  487.5 31.3 %net.20 = (f32[2,128,2048]{2,1,0:T(8,128)}, bf16[1024,2048]{1,0:T(8,128)(2,1)}) custom-call(bf16[4,2,128,2048]{3,2,1,0:T(8,128)(2,1)} %bitcast.134, bf16[2048,2048]{1,0:T(8,128)(2,1)} %get-tuple-element.107.refs_4_.refs_1_, bf16[2048,2048]{1,0:T(8,128)(2,1)} %all-gather.10.cloned.1.call-done.refs_2_, bf16[2048,2048]{1,0:T(8,128)(2,1)} %get-tuple-element.108.refs_3_.refs_2_, ...), custom_call_target="tpu_custom_call" | custom-call | bytes 12582912 | tf_op jit(solution)/shard_map/net/pallas_call | solution.py:648
  518.8 29.9 %net.21 = (f32[2,128,2048]{2,1,0:T(8,128)}, bf16[1024,2048]{1,0:T(8,128)(2,1)}) custom-call(bf16[4,2,128,2048]{3,2,1,0:T(8,128)(2,1)} %bitcast.136, bf16[2048,2048]{1,0:T(8,128)(2,1)} %get-tuple-element.107.refs_4_.refs_1_, bf16[2048,2048]{1,0:T(8,128)(2,1)} %all-gather.10.cloned.1.call-done.refs_2_, bf16[2048,2048]{1,0:T(8,128)(2,1)} %get-tuple-element.108.refs_3_.refs_2_, ...), custom_call_target="tpu_custom_call" | custom-call | bytes 12582912 | tf_op jit(solution)/shard_map/net/pallas_call | solution.py:648
  548.8 30.2 %net.22 = (f32[2,128,2048]{2,1,0:T(8,128)}, bf16[2048,2048]{1,0:T(8,128)(2,1)}) custom-call(bf16[4,2,128,2048]{3,2,1,0:T(8,128)(2,1)} %bitcast.135, bf16[2048,2048]{1,0:T(8,128)(2,1)} %bitcast.97, bf16[2048,2048]{1,0:T(8,128)(2,1)} %get-tuple-element.108.refs_3_.refs_2_), custom_call_target="tpu_custom_call" | custom-call | bytes 12582912 | tf_op jit(solution)/shard_map/net/pallas_call | solution.py:648
  590.6 5.9 convolution_convert_fusion.3
  596.5 25.9 %net.23 = (bf16[2,4,256,512]{3,2,1,0:T(8,128)(2,1)}, bf16[2048,2048]{1,0:T(8,128)(2,1)}) custom-call(bf16[2,256,2048]{2,1,0:T(8,128)(2,1)} %bitcast.141, bf16[512,2048]{1,0:T(8,128)(2,1)} %bitcast.105, bf16[512,2048]{1,0:T(8,128)(2,1)} %copy-done.19), custom_call_target="tpu_custom_call" | custom-call | bytes 12582912 | tf_op jit(solution)/shard_map/net/pallas_call | solution.py:648
  622.4 33.8 %attention_backward.1 = (bf16[2048,512]{1,0:T(8,128)(2,1)S(1)}, bf16[2048,512]{1,0:T(8,128)(2,1)S(1)}, bf16[2048,512]{1,0:T(8,128)(2,1)}, f32[4,8,128]{2,1,0:T(8,128)S(1)}) custom-call(f32[4]{0:T(128)S(1)} %add_divide_fusion.gate, s32[1]{0:T(128)} %bitcast.93.resets, s32[1]{0:T(128)S(6)} %copy.75.depth, ...), custom_call_target="tpu_custom_call" | custom-call | flops 8053063680 | bytes 12582912 | tf_op jit(solution)/shard_map/attention_backward/pallas_call | solution.py:266
  656.3 4.4 pad_maximum_fusion.refs_2_.refs_3_
  660.6 50.8 %net.24 = (bf16[8,64,2048]{2,1,0:T(8,128)(2,1)}, bf16[2048,1536]{1,0:T(8,128)(2,1)}, bf16[2048,2048]{1,0:T(8,128)(2,1)}) custom-call(bf16[8,4,64,2048]{3,2,1,0:T(8,128)(2,1)} %bitcast.131, bf16[2048,2048]{1,0:T(8,128)(2,1)} %bitcast.99, bf16[2048,1536]{1,0:T(8,128)(2,1)} %pad_maximum_fusion.refs_2_.refs_3_, ...), custom_call_target="tpu_custom_call" | custom-call | bytes 25165824 | tf_op jit(solution)/shard_map/net/pallas_call | solution.py:648
  713.1 3.9 pad_maximum_fusion.1
  717.4 121.1 %net.25 = (f32[2,256,2048]{2,1,0:T(8,128)}, bf16[1,64,2048]{2,1,0:T(8,128)(2,1)}, bf16[4,1,256,2048]{3,2,1,0:T(8,128)(2,1)}, bf16[4,1,256,2048]{3,2,1,0:T(8,128)(2,1)}, bf16[4,1,256,2048]{3,2,1,0:T(8,128)(2,1)}) custom-call(bf16[2,4,256,2048]{3,2,1,0:T(8,128)(2,1)} %bitcast.132, bf16[8,1,64,2048]{3,2,1,0:T(8,128)(2,1)} %bitcast.152, ...), custom_call_target="tpu_custom_call" | custom-call | bytes 25165824 | tf_op jit(solution)/shard_map/net/pallas_call | solution.py:648
  844.8 9.5 %net.26 = f32[8,1,8,640]{3,2,1,0:T(8,128)S(1)} custom-call(f32[1,8,640]{2,1,0:T(8,128)S(1)} %reshape.313.refs_0_), custom_call_target="tpu_custom_call" | custom-call | bytes 122880 | tf_op jit(solution)/shard_map/net/pallas_call | solution.py:648
  854.4 8.0 spread_columns.3.refs_0_
  862.4 8.1 spread_columns.4
  883.9 5.6 bitcast_convert_fusion
  890.9 5.9 fusion.9
  898.0 26.6 %net.27 = (bf16[4,1,256,1536]{3,2,1,0:T(8,128)(2,1)S(1)}, bf16[4,1,64,2048]{3,2,1,0:T(8,128)(2,1)S(1)}, f32[4,1,8,640]{3,2,1,0:T(8,128)S(1)}) custom-call(bf16[1,256,1536]{2,1,0:T(8,128)(2,1)S(1)} %bitcast.111, bf16[1,64,2048]{2,1,0:T(8,128)(2,1)S(1)} %copy-done.8, f32[1,8,640]{2,1,0:T(8,128)S(1)} %bitcast.112), custom_call_target="tpu_custom_call" | custom-call | bytes 9437184 | tf_op jit(solution)/shard_map/net/pallas_call | solution.py:648
  927.4 6.6 spread_columns.5
  (187 shorter events, 74.5 us)
Async XLA Ops:
  7.2 5.9 copy-start
  7.2 72.6 %all-gather.8.cloned.1.call-start = ((), (), s32[]{:S(2)}) async-start(), calls=%async_computation.5 | async-start | bytes 2359296 | tf_op jit(solution)/shard_map/all_gather | solution.py:778
  13.9 131.6 %all-gather.6.cloned.1.call-start = ((), (), s32[]{:S(2)}) async-start(), calls=%async_computation.4 | async-start | bytes 7077888 | tf_op jit(solution)/shard_map/all_gather | solution.py:778
  18.1 255.1 %all-gather.10.cloned.1.call-start = ((), (), s32[]{:S(2)}) async-start(), calls=%async_computation.6 | async-start | bytes 9437184 | tf_op jit(solution)/shard_map/all_gather | solution.py:778
  69.9 3.4 copy-start.3
  79.8 265.6 %all-gather.12.cloned.1.call-start = ((), (), s32[]{:S(2)}) async-start(), calls=%async_computation.7 | async-start | bytes 9437184 | tf_op jit(solution)/shard_map/all_gather | solution.py:778
  87.6 53.8 %copy-start.37 = (f32[16]{0:T(128)S(1)}, f32[16]{0:T(128)}, u32[]{:S(2)}) copy-start(f32[16]{0:T(128)} %param.26) | copy-start | bytes 196
  137.3 3.4 copy-start.4
  140.7 255.3 %all-gather.14.cloned.1.call-start = ((), (), s32[]{:S(2)}) async-start(), calls=%async_computation.8 | async-start | bytes 9437184 | tf_op jit(solution)/shard_map/all_gather | solution.py:778
  183.9 438.5 %reduce-scatter.7.cloned.1.call-start = ((), (), s32[]{:S(2)}) async-start(), calls=%async_computation.10 | async-start | bytes 9437184 | tf_op jit(solution)/shard_map/reduce_scatter | solution.py:836
  184.2 25.7 %copy-start.14 = (bf16[1,2,256,2048]{3,2,1,0:T(8,128)(2,1)S(1)}, bf16[1,2,256,2048]{3,2,1,0:T(8,128)(2,1)}, u32[]{:S(2)}) copy-start(bf16[1,2,256,2048]{3,2,1,0:T(8,128)(2,1)} %param.18) | copy-start | bytes 6291460
  209.9 7.9 copy-start.5
  209.9 8.0 copy-start.24
  269.9 3.3 copy-start.2
  345.4 29.8 %copy-start.36 = (bf16[2,4,256,2048]{3,2,1,0:T(8,128)(2,1)S(1)}, bf16[2,4,256,2048]{3,2,1,0:T(8,128)(2,1)}, u32[]{:S(2)}) copy-start(bf16[2,4,256,2048]{3,2,1,0:T(8,128)(2,1)} %get-tuple-element.67) | copy-start | bytes 25165828
  371.9 3.3 copy-start.20
  395.9 264.7 %reduce-scatter.5.cloned.1.call-start = ((), (), s32[]{:S(2)}) async-start(), calls=%async_computation.9 | async-start | bytes 9437184 | tf_op jit(solution)/shard_map/reduce_scatter | solution.py:836
  487.5 229.9 %reduce-scatter.9.cloned.1.call-start = ((), (), s32[]{:S(2)}) async-start(), calls=%async_computation.11 | async-start | bytes 9437184 | tf_op jit(solution)/shard_map/reduce_scatter | solution.py:836
  579.0 317.9 %reduce-scatter.11.cloned.1.call-start = ((), (), s32[]{:S(2)}) async-start(), calls=%async_computation.12 | async-start | bytes 7077888 | tf_op jit(solution)/shard_map/reduce_scatter | solution.py:836
  584.7 3.2 copy-start.16
  584.7 4.4 slice-start
  587.9 2.7 slice-start.1
  590.6 5.9 copy-start.19
  862.4 8.1 copy-start.32
  870.5 13.4 %copy-start.21 = (bf16[4,1,256,2048]{3,2,1,0:T(8,128)(2,1)S(1)}, bf16[4,1,256,2048]{3,2,1,0:T(8,128)(2,1)}, u32[]{:S(2)}) copy-start(bf16[4,1,256,2048]{3,2,1,0:T(8,128)(2,1)} %get-tuple-element.94) | copy-start | bytes 12582916
  874.4 15.1 %copy-start.30 = (f32[512]{0:T(512)S(1)}, f32[512]{0:T(512)}, u32[]{:S(2)}) copy-start(f32[512]{0:T(512)} %copy-done.29) | copy-start | bytes 6148
  880.0 9.5 %copy-start.18 = (f32[2,2,128,2048]{3,2,1,0:T(8,128)S(1)}, f32[2,2,128,2048]{3,2,1,0:T(8,128)}, u32[]{:S(2)}) copy-start(f32[2,2,128,2048]{3,2,1,0:T(8,128)} %pad_maximum_fusion.1) | copy-start | bytes 12582916
  883.9 5.6 copy-start.11
  883.9 6.1 copy-start.13
  883.9 7.1 copy-start.17
  890.9 5.9 copy-start.8
  927.4 8.2 copy-start.1
  (17 other events, 29.5 us)
Sparse Core Ops, SparseCore 0:
  14.0 36.1 all-gather.7
  52.3 66.5 all-gather.5
  121.0 87.2 all-gather.9
  209.6 87.2 all-gather.11
  298.9 87.1 all-gather.13
  396.0 88.9 reduce-scatter.6
  487.6 89.9 reduce-scatter.4
  579.8 88.3 reduce-scatter.8
  711.6 91.6 reduce-scatter.10

commit v6 on v5

--- a/solution.py
+++ b/solution.py
@@ -314,6 +314,29 @@
     )
 
 
+def move_blocks(value, order, axis):
+    n = len(order)
+    block = (value.shape[0] // n, value.shape[1]) if axis == 0 else (value.shape[0], value.shape[1] // n)
+
+    def kernel(order_ref, in_ref, out_ref):
+        out_ref[...] = in_ref[...]
+
+    def at(i):
+        return (i, 0) if axis == 0 else (0, i)
+
+    return pl.pallas_call(
+        kernel,
+        grid_spec=pltpu.PrefetchScalarGridSpec(
+            num_scalar_prefetch=1,
+            grid=(n,),
+            in_specs=[pl.BlockSpec(block, lambda i, order_ref: at(order_ref[i]))],
+            out_specs=pl.BlockSpec(block, lambda i, order_ref: at(i)),
+        ),
+        out_shape=jax.ShapeDtypeStruct(value.shape, value.dtype),
+        name="move_blocks",
+    )(jnp.array(order, jnp.int32), value)
+
+
 def tie(value, *others):
     return lax.optimization_barrier((value,) + others)[0]
 
@@ -634,13 +657,16 @@
             pl.semaphore_wait(barrier, len(peers))
             for job in jobs:
                 job.start()
+            products = [job for job in jobs if not job.peers]
+            late = [job for job in jobs if products and isinstance(job, Gather)]
             parts = 4
-            for part in range(parts):
-                for job in jobs:
-                    job.middle(part, parts)
-            for job in jobs:
-                if isinstance(job, Product):
-                    job.compute()
+            for some in ([job for job in jobs if job not in late], late):
+                for part in range(parts):
+                    for job in some:
+                        job.middle(part, parts)
+                if some is not late:
+                    for job in products:
+                        job.compute()
             for job in jobs:
                 job.finish()
 
@@ -788,7 +814,7 @@
         (h_one,) = net.run([gather_own(h_one_own)])
         h_one = h_one.reshape(total_rows, width)
         w_g = gather_rows(tie(gate_own, h_one))
-        w_o = reorder(tie(w_o, h_one), back, 0)
+        w_o = move_blocks(tie(w_o, h_one), back, 0)
         (whole_o,) = net.run([Gather(net.seq, w_o.reshape(n_fsdp, out_rows, width), False)])
         whole_o = whole_o.reshape(width, width)
         w_u = gather_rows(tie(up_own, whole_o))
@@ -915,7 +941,7 @@
             ],
             56,
         )
-        grad_h_one = reorder(grad_h_one.reshape(rows, width), back, 1)
+        grad_h_one = move_blocks(grad_h_one.reshape(rows, width), back, 1)
         output = (x_one + output).astype(bf16).reshape(tokens.shape)
         gain_attn_term = jnp.sum(grad_h_one * r_one, axis=0)
         _, norm_one_back = jax.vjp(rms, x_flat)
@@ -938,18 +964,14 @@
             cut = jnp.stack([gate_all, up_all]).reshape(2, n_seq, shard, n_fsdp, my_hidden)
             cut = reorder(cut, back, 3)
             gate_up_all = jnp.transpose(cut, (2, 0, 3, 1, 4)).reshape(shard, -1).astype(f32)
-        qkv_term = tie(qkv_term, down_all, gate_up_all, output, input_grad)
+        qkv_all = lax.all_gather(tie(qkv_term, grad_h_one), "seq", axis=0)
+        out_all = lax.all_gather(out_term.reshape(out_rows, width), "seq", axis=0)
         (small,) = net.run([Gather(net.fsdp, small, True)])
-        qkv_all, out_all, small = net.run(
-            [
-                Gather(net.seq, qkv_term[None], True),
-                Gather(net.seq, out_term, True),
-                Gather(net.seq, jnp.sum(small, axis=0), True),
-            ]
-        )
+        (small,) = net.run([Gather(net.seq, jnp.sum(small, axis=0), True)])
         small = jnp.sum(small, axis=0).reshape(-1)
         out_all = out_all.reshape(shard, width).astype(f32)
-        qkv_all = spread_columns([qkv_all[:, 0]], 1, 0, range(3), my_width, shard // 2)
+        qkv_all = tie(qkv_all, down_all, gate_up_all, output, input_grad, small)
+        qkv_all = spread_columns([qkv_all], 1, 0, range(3), my_width, shard // 2)
 
         return (
             output,

time: 951 us -> 913 us (0.960)
  local copies, waits for them, and re-layouts: 61.1 us -> 32 us
  Pallas kernels: 705 us -> 691 us
    pallas_call x14, Pallas kernels: 619 us -> 591 us  [run(): pl.pallas_call(kernel, in_specs=[anywhere] * len(ins), out_specs=[anywher...]
    unnamed x123 -> x90, local copies, waits for them, and re-layouts: 47.9 us -> 25.2 us
    pallas_call x0 -> x2, Pallas kernels: none -> 13.7 us  [move_blocks(): pl.pallas_call(kernel, grid_spec=pltpu.PrefetchScalarGridSpec(num_scalar_...]
  transfers between devices with their start and end apart: 9 -> 11, of which waited for: 0 -> 0; matrix products, arithmetic and copies ran while one was open for 19% -> 18% of each run, Pallas kernels for 71% -> 76%
where the time goes in v6:
time: 913 us; the launch traced here: 905 us
  Pallas kernels  691 us (76%)
  matrix products  126 us (14%)
  other arithmetic  38.5 us (4%)
  local copies, waits for them, and re-layouts  32 us (4%)
  between operations  16.5 us (2%)
    pallas_call x14, Pallas kernels, run(): pl.pallas_call(kernel, in_specs=[anywhere] * len(ins), out_specs=[anywher...  591 us
    dot_general x4, matrix products, mm(): return jnp.dot(left, right, preferred_element_type=f32)  67 us
    dot_general x2, matrix products, mm_nt(): lax.dot_general(left, right, (((1,), (1,)), ((), ())), preferred_element_...  38.7 us
    pallas_call x1, Pallas kernels, attention_backward(): pl.pallas_call(functools.partial(backward_kernel, min(256, seg), segs), g...  33.9 us
    unnamed x90, local copies, waits for them, and re-layouts  25.2 us
    pallas_call x3, Pallas kernels, spread_columns(): pl.pallas_call(kernel, grid_spec=pltpu.PrefetchScalarGridSpec(num_scalar_...  22.7 us
    dot_general x1, matrix products, mm_tn(): lax.dot_general(left, right, (((0,), (0,)), ((), ())), preferred_element_...  20.7 us
    pallas_call x1, Pallas kernels, attention_forward(): pl.pallas_call(functools.partial(forward_kernel, min(256, seg), segs), gr...  19.8 us
  transfers between devices with their start and end apart: 11, of which 0 were waited for; matrix products, arithmetic and copies ran while one was open for 18% of the time, Pallas kernels for 76%

profile of v6, /device:TPU:0, one launch (start us, length us, event | category | flops | bytes accessed | tf_op | source)
XLA Modules:
  0.0 905.5 jit_solution(8546946327055454911)
XLA Ops:
  17.5 51.7 %net.14 = bf16[2,4,256,2048]{3,2,1,0:T(8,128)(2,1)S(1)} custom-call(bf16[2,256,2048]{2,1,0:T(8,128)(2,1)S(1)} %bitcast.103), custom_call_target="tpu_custom_call" | custom-call | bytes 25165824 | tf_op jit(solution)/shard_map/net/pallas_call | solution.py:674
  72.6 6.5 own_columns.3
  79.2 6.3 move_blocks.2
  87.1 49.6 %net.16 = bf16[8,4,64,2048]{3,2,1,0:T(8,128)(2,1)S(1)} custom-call(bf16[8,64,2048]{2,1,0:T(8,128)(2,1)S(1)} %bitcast.102), custom_call_target="tpu_custom_call" | custom-call | bytes 25165824 | tf_op jit(solution)/shard_map/net/pallas_call | solution.py:674
  144.9 18.6 %convolution_convert_fusion.2.q_ref.k_ref.v_ref = bf16[2048,1536]{1,0:T(8,128)(2,1)} fusion(bf16[2048,2048]{1,0:T(8,128)(2,1)} %bitcast.94, bf16[2048,1536]{1,0:T(8,128)(2,1)} %all-gather.9.cloned.1.call-done.refs_4_), kind=kOutput, calls=%fused_computation.16 | convolution fusion | flops 12888047616 | bytes 20971520 | tf_op jit(solution)/shard_map/dot_general | solution.py:749
  163.6 19.8 %attention_forward.1 = (bf16[2048,512]{1,0:T(8,128)(2,1)S(1)}, f32[4,2,1,1024]{3,2,1,0:T(1,128)S(1)}, f32[4,2,128,128]{3,2,1,0:T(8,128)S(1)}, f32[4,2,1,128]{3,2,1,0:T(1,128)S(1)}) custom-call(f32[4]{0:T(128)S(1)} %add_divide_fusion.gate, s32[1]{0:T(128)} %bitcast.88.resets, bf16[2048,1536]{1,0:T(8,128)(2,1)} %convolution_convert_fusion.2.q_ref.k_ref.v_ref, ...), custom_call_target="tpu_custom_call" | custom-call | flops 4026531840 | bytes 12582912 | tf_op jit(solution)/shard_map/attention_forward/pallas_call | solution.py:133
  183.7 25.7 %net.15 = bf16[2,256,2048]{2,1,0:T(8,128)(2,1)S(1)} custom-call(bf16[2,4,256,512]{3,2,1,0:T(8,128)(2,1)S(1)} %bitcast.105), custom_call_target="tpu_custom_call" | custom-call | bytes 12582912 | tf_op jit(solution)/shard_map/net/pallas_call | solution.py:674
  209.4 7.9 multiply_reduce_fusion.2
  219.5 49.8 %net.17 = bf16[2,4,256,2048]{3,2,1,0:T(8,128)(2,1)S(1)} custom-call(bf16[2,256,2048]{2,1,0:T(8,128)(2,1)S(1)} %bitcast.104), custom_call_target="tpu_custom_call" | custom-call | bytes 25165824 | tf_op jit(solution)/shard_map/net/pallas_call | solution.py:674
  272.6 65.7 %net.18 = (bf16[2,4,256,2048]{3,2,1,0:T(8,128)(2,1)}, bf16[2048,2048]{1,0:T(8,128)(2,1)}) custom-call(bf16[2,256,2048]{2,1,0:T(8,128)(2,1)} %bitcast.108, bf16[2048,2048]{1,0:T(8,128)(2,1)} %bitcast.90, bf16[2048,2048]{1,0:T(8,128)(2,1)} %all-gather.13.cloned.1.call-done.refs_2_), custom_call_target="tpu_custom_call" | custom-call | bytes 25165824 | tf_op jit(solution)/shard_map/net/pallas_call | solution.py:674
  338.4 26.6 %fusion = (bf16[2048,2048]{1,0:T(8,128)(2,1)S(1)}, bf16[2048,2048]{1,0:T(8,128)(2,1)}) fusion(bf16[2048,2048]{1,0:T(8,128)(2,1)} %get-tuple-element.61, bf16[2048,2048]{1,0:T(8,128)(2,1)} %bitcast.91, bf16[2048,2048]{1,0:T(8,128)(2,1)} %all-gather.15.cloned.1.call-done.refs_4_), kind=kOutput, calls=%fused_computation.6 | convolution fusion | flops 17217617920 | bytes 41943040 | tf_op jit(solution)/shard_map/dot_general | solution.py:749
  368.2 20.7 %convolution_convert_fusion = bf16[2048,2048]{1,0:T(8,128)(2,1)} fusion(bf16[2048,2048]{1,0:T(8,128)(2,1)S(1)} %get-tuple-element.111.refs_1_, bf16[2048,2048]{1,0:T(8,128)(2,1)S(1)} %bitcast.141), kind=kOutput, calls=%fused_computation.14 | convolution fusion | flops 17184063488 | bytes 25165824 | tf_op jit(solution)/shard_map/dot_general | solution.py:757
  389.1 32.8 %fusion.6 = (bf16[2048,2048]{1,0:T(8,128)(2,1)}, bf16[2048,2048]{1,0:T(8,128)(2,1)}) fusion(bf16[2048,2048]{1,0:T(8,128)(2,1)} %get-tuple-element.61, bf16[2048,2048]{1,0:T(8,128)(2,1)} %get-tuple-element.112, bf16[2048,2048]{1,0:T(8,128)(2,1)} %bitcast.140, bf16[2048,2048]{1,0:T(8,128)(2,1)} %all-gather.17.cloned.1.call-done.refs_2_), kind=kOutput, calls=%fused_computation.12 | convolution fusion | flops 17246978048 | bytes 50331648 | tf_op jit(solution)/shard_map/dot_general | solution.py:753
  421.9 13.9 %fusion.19 = bf16[1024,2048]{1,0:T(8,128)(2,1)} fusion(bf16[2048,2048]{1,0:T(8,128)(2,1)} %all-gather.17.cloned.1.call-done.refs_2_, bf16[2048,2048]{1,0:T(8,128)(2,1)} %copy-done.17), kind=kOutput, calls=%fused_computation.45 | convolution fusion | flops 8592031744 | bytes 16777216 | tf_op jit(solution)/shard_map/dot_general | solution.py:749
  435.8 45.0 %net.19 = (f32[2,128,2048]{2,1,0:T(8,128)}, bf16[1024,2048]{1,0:T(8,128)(2,1)}, bf16[2048,2048]{1,0:T(8,128)(2,1)}) custom-call(bf16[4,2,128,2048]{3,2,1,0:T(8,128)(2,1)} %bitcast.123, bf16[2048,2048]{1,0:T(8,128)(2,1)} %copy-done.17, bf16[2048,2048]{1,0:T(8,128)(2,1)} %all-gather.17.cloned.1.call-done.refs_2_, bf16[2048,2048]{1,0:T(8,128)(2,1)} %bitcast.92, ...), custom_call_target="tpu_custom_call" | custom-call | bytes 12582912 | tf_op jit(solution)/shard_map/net/pallas_call | solution.py:674
  480.9 31.0 %net.20 = (f32[2,128,2048]{2,1,0:T(8,128)}, bf16[1024,2048]{1,0:T(8,128)(2,1)}) custom-call(bf16[4,2,128,2048]{3,2,1,0:T(8,128)(2,1)} %bitcast.120, bf16[2048,2048]{1,0:T(8,128)(2,1)} %get-tuple-element.103.refs_4_.refs_1_, bf16[2048,2048]{1,0:T(8,128)(2,1)} %all-gather.13.cloned.1.call-done.refs_2_, bf16[2048,2048]{1,0:T(8,128)(2,1)} %get-tuple-element.104.refs_3_.refs_2_, ...), custom_call_target="tpu_custom_call" | custom-call | bytes 12582912 | tf_op jit(solution)/shard_map/net/pallas_call | solution.py:674
  511.9 30.0 %net.21 = (f32[2,128,2048]{2,1,0:T(8,128)}, bf16[1024,2048]{1,0:T(8,128)(2,1)}) custom-call(bf16[4,2,128,2048]{3,2,1,0:T(8,128)(2,1)} %bitcast.122, bf16[2048,2048]{1,0:T(8,128)(2,1)} %get-tuple-element.103.refs_4_.refs_1_, bf16[2048,2048]{1,0:T(8,128)(2,1)} %all-gather.13.cloned.1.call-done.refs_2_, bf16[2048,2048]{1,0:T(8,128)(2,1)} %get-tuple-element.104.refs_3_.refs_2_, ...), custom_call_target="tpu_custom_call" | custom-call | bytes 12582912 | tf_op jit(solution)/shard_map/net/pallas_call | solution.py:674
  542.0 30.1 %net.22 = (f32[2,128,2048]{2,1,0:T(8,128)}, bf16[2048,2048]{1,0:T(8,128)(2,1)}) custom-call(bf16[4,2,128,2048]{3,2,1,0:T(8,128)(2,1)} %bitcast.121, bf16[2048,2048]{1,0:T(8,128)(2,1)} %bitcast.93, bf16[2048,2048]{1,0:T(8,128)(2,1)} %get-tuple-element.104.refs_3_.refs_2_), custom_call_target="tpu_custom_call" | custom-call | bytes 12582912 | tf_op jit(solution)/shard_map/net/pallas_call | solution.py:674
  583.8 5.9 convolution_convert_fusion.3
  589.7 25.9 %net.23 = (bf16[2,4,256,512]{3,2,1,0:T(8,128)(2,1)}, bf16[2048,2048]{1,0:T(8,128)(2,1)}) custom-call(bf16[2,256,2048]{2,1,0:T(8,128)(2,1)} %bitcast.129, bf16[512,2048]{1,0:T(8,128)(2,1)} %bitcast.101, bf16[512,2048]{1,0:T(8,128)(2,1)} %copy-done.16), custom_call_target="tpu_custom_call" | custom-call | bytes 12582912 | tf_op jit(solution)/shard_map/net/pallas_call | solution.py:674
  615.6 33.9 %attention_backward.1 = (bf16[2048,512]{1,0:T(8,128)(2,1)S(1)}, bf16[2048,512]{1,0:T(8,128)(2,1)S(1)}, bf16[2048,512]{1,0:T(8,128)(2,1)}, f32[4,8,128]{2,1,0:T(8,128)S(1)}) custom-call(f32[4]{0:T(128)S(1)} %add_divide_fusion.gate, s32[1]{0:T(128)} %bitcast.89.resets, s32[1]{0:T(128)S(6)} %copy.55.depth, ...), custom_call_target="tpu_custom_call" | custom-call | flops 8053063680 | bytes 12582912 | tf_op jit(solution)/shard_map/attention_backward/pallas_call | solution.py:266
  653.8 50.8 %net.24 = (bf16[8,64,2048]{2,1,0:T(8,128)(2,1)}, bf16[2048,1536]{1,0:T(8,128)(2,1)}, bf16[2048,2048]{1,0:T(8,128)(2,1)}) custom-call(bf16[8,4,64,2048]{3,2,1,0:T(8,128)(2,1)} %bitcast.117, bf16[2048,2048]{1,0:T(8,128)(2,1)} %bitcast.95, bf16[2048,1536]{1,0:T(8,128)(2,1)} %pad_maximum_fusion.refs_2_.refs_3_, ...), custom_call_target="tpu_custom_call" | custom-call | bytes 25165824 | tf_op jit(solution)/shard_map/net/pallas_call | solution.py:674
  704.8 120.9 %net.25 = (f32[2,256,2048]{2,1,0:T(8,128)}, bf16[1,64,2048]{2,1,0:T(8,128)(2,1)}, bf16[4,1,256,2048]{3,2,1,0:T(8,128)(2,1)}, bf16[4,1,256,2048]{3,2,1,0:T(8,128)(2,1)}, bf16[4,1,256,2048]{3,2,1,0:T(8,128)(2,1)}) custom-call(bf16[2,4,256,2048]{3,2,1,0:T(8,128)(2,1)} %bitcast.118, bf16[8,1,64,2048]{3,2,1,0:T(8,128)(2,1)} %bitcast.132, ...), custom_call_target="tpu_custom_call" | custom-call | bytes 25165824 | tf_op jit(solution)/shard_map/net/pallas_call | solution.py:674
  825.8 7.4 move_blocks.3
  833.2 4.8 pad_maximum_fusion.1
  842.0 9.5 %net.26 = f32[8,1,8,640]{3,2,1,0:T(8,128)S(1)} custom-call(f32[1,8,640]{2,1,0:T(8,128)S(1)} %reshape.186.refs_0_), custom_call_target="tpu_custom_call" | custom-call | bytes 122880 | tf_op jit(solution)/shard_map/net/pallas_call | solution.py:674
  851.5 5.1 net.27
  856.7 8.0 spread_columns.3.refs_0_
  865.2 8.1 spread_columns.4
  873.9 7.7 bitcast_convert_fusion
  882.8 6.2 fusion.9
  891.9 6.6 spread_columns.5
  (158 shorter events, 56.3 us)
Async XLA Ops:
  7.2 5.4 copy-start
  7.2 72.0 %all-gather.11.cloned.1.call-start = ((), (), s32[]{:S(2)}) async-start(), calls=%async_computation.5 | async-start | bytes 2359296 | tf_op jit(solution)/shard_map/all_gather | solution.py:804
  13.3 131.6 %all-gather.9.cloned.1.call-start = ((), (), s32[]{:S(2)}) async-start(), calls=%async_computation.4 | async-start | bytes 7077888 | tf_op jit(solution)/shard_map/all_gather | solution.py:804
  17.4 255.1 %all-gather.13.cloned.1.call-start = ((), (), s32[]{:S(2)}) async-start(), calls=%async_computation.6 | async-start | bytes 9437184 | tf_op jit(solution)/shard_map/all_gather | solution.py:804
  69.2 3.4 copy-start.3
  79.1 259.2 %all-gather.15.cloned.1.call-start = ((), (), s32[]{:S(2)}) async-start(), calls=%async_computation.7 | async-start | bytes 9437184 | tf_op jit(solution)/shard_map/all_gather | solution.py:804
  87.1 53.7 %copy-start.31 = (f32[16]{0:T(128)S(1)}, f32[16]{0:T(128)}, u32[]{:S(2)}) copy-start(f32[16]{0:T(128)} %param.28) | copy-start | bytes 196
  136.7 3.4 copy-start.4
  140.2 248.9 %all-gather.17.cloned.1.call-start = ((), (), s32[]{:S(2)}) async-start(), calls=%async_computation.8 | async-start | bytes 9437184 | tf_op jit(solution)/shard_map/all_gather | solution.py:804
  183.4 432.2 %reduce-scatter.7.cloned.1.call-start = ((), (), s32[]{:S(2)}) async-start(), calls=%async_computation.10 | async-start | bytes 9437184 | tf_op jit(solution)/shard_map/reduce_scatter | solution.py:862
  183.7 25.7 %copy-start.13 = (bf16[1,2,256,2048]{3,2,1,0:T(8,128)(2,1)S(1)}, bf16[1,2,256,2048]{3,2,1,0:T(8,128)(2,1)}, u32[]{:S(2)}) copy-start(bf16[1,2,256,2048]{3,2,1,0:T(8,128)(2,1)} %param.20) | copy-start | bytes 6291460
  209.3 7.9 copy-start.5
  209.4 8.0 copy-start.19
  269.3 3.3 copy-start.2
  338.3 29.9 %copy-start.30 = (bf16[2,4,256,2048]{3,2,1,0:T(8,128)(2,1)S(1)}, bf16[2,4,256,2048]{3,2,1,0:T(8,128)(2,1)}, u32[]{:S(2)}) copy-start(bf16[2,4,256,2048]{3,2,1,0:T(8,128)(2,1)} %get-tuple-element.65) | copy-start | bytes 25165828
  364.9 3.3 copy-start.17
  389.0 264.8 %reduce-scatter.5.cloned.1.call-start = ((), (), s32[]{:S(2)}) async-start(), calls=%async_computation.9 | async-start | bytes 9437184 | tf_op jit(solution)/shard_map/reduce_scatter | solution.py:862
  480.8 223.9 %reduce-scatter.9.cloned.1.call-start = ((), (), s32[]{:S(2)}) async-start(), calls=%async_computation.11 | async-start | bytes 9437184 | tf_op jit(solution)/shard_map/reduce_scatter | solution.py:862
  572.1 261.0 %reduce-scatter.11.cloned.1.call-start = ((), (), s32[]{:S(2)}) async-start(), calls=%async_computation.12 | async-start | bytes 7077888 | tf_op jit(solution)/shard_map/reduce_scatter | solution.py:862
  577.9 3.2 copy-start.15
  577.9 4.4 slice-start
  583.8 5.9 copy-start.16
  704.7 184.4 %all-gather.19.cloned.1.call-start = ((), (), s32[]{:S(2)}) async-start(), calls=%async_computation.13 | async-start | bytes 1310720 | tf_op jit(solution)/shard_map/all_gather | solution.py:968
  825.8 66.1 %all-gather.21.cloned.1.call-start = ((), (), s32[]{:S(2)}) async-start(), calls=%async_computation.14 | async-start | bytes 3932160 | tf_op jit(solution)/shard_map/all_gather | solution.py:967
  833.2 5.2 copy-start.14
  833.2 5.2 copy-start.21
  833.2 5.2 copy-start.25
  865.2 8.1 copy-start.27
  873.9 7.7 copy-start.9
  873.9 7.7 copy-start.11
  873.9 8.9 copy-start.12
  891.9 6.6 copy-start.1
  (13 other events, 24.8 us)
Sparse Core Ops, SparseCore 0:
  13.4 36.1 all-gather.10
  51.7 66.5 all-gather.8
  120.4 87.2 all-gather.12
  209.1 87.2 all-gather.14
  298.3 87.2 all-gather.16
  389.1 88.9 reduce-scatter.6
  481.0 89.3 reduce-scatter.4
  572.7 88.4 reduce-scatter.8
  704.8 88.7 reduce-scatter.10
  825.9 14.8 all-gather.18
  842.3 28.9 all-gather.20

commit v7 on v6

--- a/solution.py
+++ b/solution.py
@@ -931,13 +931,12 @@
             56,
         )
         qkv_term = scatter_rows(qkv_parts)
-        grad_h_one, out_term, down_all, gate_all, up_all = net.run(
+        grad_h_one, out_term, down_all, gate_all = net.run(
             [
                 Scatter(net.seq, token_parts(tie(grad_h_one, up_term)), False, f32),
                 Scatter(net.fsdp, out_sum[:, None], True, bf16, 2),
                 Gather(net.seq, down_term[None], True),
                 Gather(net.seq, gate_term[None], True),
-                Gather(net.seq, up_term[None], True),
             ],
             56,
         )
@@ -957,21 +956,25 @@
 
         down_all = down_all.reshape(hidden_shard, width).astype(f32)
         aligned = my_hidden % 128 == 0
+        gate_up_all = gate_all[:, 0]
         if aligned:
-            gate_up_all = spread_columns([gate_all[:, 0]], 2, 0, ring, my_hidden, shard)
-            gate_up_all = spread_columns([up_all[:, 0], gate_up_all], 2, 1, ring, my_hidden, shard)
-        else:
-            cut = jnp.stack([gate_all, up_all]).reshape(2, n_seq, shard, n_fsdp, my_hidden)
-            cut = reorder(cut, back, 3)
-            gate_up_all = jnp.transpose(cut, (2, 0, 3, 1, 4)).reshape(shard, -1).astype(f32)
+            gate_up_all = spread_columns([gate_up_all], 2, 0, ring, my_hidden, shard)
+        up_all = lax.all_gather(tie(up_term, grad_h_one), "seq", axis=0)
         qkv_all = lax.all_gather(tie(qkv_term, grad_h_one), "seq", axis=0)
-        out_all = lax.all_gather(out_term.reshape(out_rows, width), "seq", axis=0)
-        (small,) = net.run([Gather(net.fsdp, small, True)])
+        small, out_all = net.run([Gather(net.fsdp, small, True), Gather(net.seq, out_term, True)])
         (small,) = net.run([Gather(net.seq, jnp.sum(small, axis=0), True)])
         small = jnp.sum(small, axis=0).reshape(-1)
         out_all = out_all.reshape(shard, width).astype(f32)
-        qkv_all = tie(qkv_all, down_all, gate_up_all, output, input_grad, small)
+        done = (down_all, gate_up_all, output, input_grad, small, out_all)
+        qkv_all = tie(qkv_all, *done)
+        up_all = tie(up_all, *done)
         qkv_all = spread_columns([qkv_all], 1, 0, range(3), my_width, shard // 2)
+        if aligned:
+            gate_up_all = spread_columns([up_all, gate_up_all], 2, 1, ring, my_hidden, shard)
+        else:
+            cut = jnp.stack([gate_up_all, up_all]).reshape(2, n_seq, shard, n_fsdp, my_hidden)
+            cut = reorder(cut, back, 3)
+            gate_up_all = jnp.transpose(cut, (2, 0, 3, 1, 4)).reshape(shard, -1).astype(f32)
 
         return (
             output,

time: 913 us -> 909 us (level)
  Pallas kernels: 691 us -> 675 us
  waiting for transfers between devices: 0.29 us -> 12.1 us
    pallas_call x14, Pallas kernels: 591 us -> 575 us  [run(): pl.pallas_call(kernel, in_specs=[anywhere] * len(ins), out_specs=[anywher...]
    all_gather x1, waiting for transfers between devices: 0.01 us -> 11.2 us  [body(): qkv_all = lax.all_gather(tie(qkv_term, grad_h_one), 'seq', axis=0)]
    unnamed x90 -> x96, local copies, waits for them, and re-layouts: 25.2 us -> 25.5 us
  transfers between devices with their start and end apart: 11 -> 11, of which waited for: 0 -> 1; matrix products, arithmetic and copies ran while one was open for 18% -> 18% of each run, Pallas kernels for 76% -> 73%
where the time goes in v7:
time: 909 us; the launch traced here: 901 us
  Pallas kernels  675 us (74%)
  matrix products  126 us (14%)
  other arithmetic  37.9 us (4%)
  local copies, waits for them, and re-layouts  32.3 us (4%)
  between operations  16.5 us (2%)
  waiting for transfers between devices  12.1 us (1%)
    pallas_call x14, Pallas kernels, run(): pl.pallas_call(kernel, in_specs=[anywhere] * len(ins), out_specs=[anywher...  575 us
    dot_general x4, matrix products, mm(): return jnp.dot(left, right, preferred_element_type=f32)  67 us
    dot_general x2, matrix products, mm_nt(): lax.dot_general(left, right, (((1,), (1,)), ((), ())), preferred_element_...  38.7 us
    pallas_call x1, Pallas kernels, attention_backward(): pl.pallas_call(functools.partial(backward_kernel, min(256, seg), segs), g...  33.8 us
    unnamed x96, local copies, waits for them, and re-layouts  25.5 us
    pallas_call x3, Pallas kernels, spread_columns(): pl.pallas_call(kernel, grid_spec=pltpu.PrefetchScalarGridSpec(num_scalar_...  22.7 us
    dot_general x1, matrix products, mm_tn(): lax.dot_general(left, right, (((0,), (0,)), ((), ())), preferred_element_...  20.7 us
    pallas_call x1, Pallas kernels, attention_forward(): pl.pallas_call(functools.partial(forward_kernel, min(256, seg), segs), gr...  19.8 us
  transfers between devices with their start and end apart: 11, of which 1 were waited for; matrix products, arithmetic and copies ran while one was open for 18% of the time, Pallas kernels for 73%

profile of v7, /device:TPU:0, one launch (start us, length us, event | category | flops | bytes accessed | tf_op | source)
XLA Modules:
  0.0 901.0 jit_solution(7324737642722462450)
XLA Ops:
  17.5 51.7 %net.14 = bf16[2,4,256,2048]{3,2,1,0:T(8,128)(2,1)S(1)} custom-call(bf16[2,256,2048]{2,1,0:T(8,128)(2,1)S(1)} %bitcast.102), custom_call_target="tpu_custom_call" | custom-call | bytes 25165824 | tf_op jit(solution)/shard_map/net/pallas_call | solution.py:674
  72.7 6.5 own_columns.3
  79.3 6.3 move_blocks.2
  87.2 49.6 %net.16 = bf16[8,4,64,2048]{3,2,1,0:T(8,128)(2,1)S(1)} custom-call(bf16[8,64,2048]{2,1,0:T(8,128)(2,1)S(1)} %bitcast.101), custom_call_target="tpu_custom_call" | custom-call | bytes 25165824 | tf_op jit(solution)/shard_map/net/pallas_call | solution.py:674
  145.0 18.6 %convolution_convert_fusion.2.q_ref.k_ref.v_ref = bf16[2048,1536]{1,0:T(8,128)(2,1)} fusion(bf16[2048,2048]{1,0:T(8,128)(2,1)} %bitcast.93, bf16[2048,1536]{1,0:T(8,128)(2,1)} %all-gather.10.cloned.1.call-done.refs_4_), kind=kOutput, calls=%fused_computation.16 | convolution fusion | flops 12888047616 | bytes 20971520 | tf_op jit(solution)/shard_map/dot_general | solution.py:749
  163.7 19.8 %attention_forward.1 = (bf16[2048,512]{1,0:T(8,128)(2,1)S(1)}, f32[4,2,1,1024]{3,2,1,0:T(1,128)S(1)}, f32[4,2,128,128]{3,2,1,0:T(8,128)S(1)}, f32[4,2,1,128]{3,2,1,0:T(1,128)S(1)}) custom-call(f32[4]{0:T(128)S(1)} %add_divide_fusion.gate, s32[1]{0:T(128)} %bitcast.87.resets, bf16[2048,1536]{1,0:T(8,128)(2,1)} %convolution_convert_fusion.2.q_ref.k_ref.v_ref, ...), custom_call_target="tpu_custom_call" | custom-call | flops 4026531840 | bytes 12582912 | tf_op jit(solution)/shard_map/attention_forward/pallas_call | solution.py:133
  183.8 25.7 %net.15 = bf16[2,256,2048]{2,1,0:T(8,128)(2,1)S(1)} custom-call(bf16[2,4,256,512]{3,2,1,0:T(8,128)(2,1)S(1)} %bitcast.104), custom_call_target="tpu_custom_call" | custom-call | bytes 12582912 | tf_op jit(solution)/shard_map/net/pallas_call | solution.py:674
  209.5 7.9 multiply_reduce_fusion.2
  219.6 49.8 %net.17 = bf16[2,4,256,2048]{3,2,1,0:T(8,128)(2,1)S(1)} custom-call(bf16[2,256,2048]{2,1,0:T(8,128)(2,1)S(1)} %bitcast.103), custom_call_target="tpu_custom_call" | custom-call | bytes 25165824 | tf_op jit(solution)/shard_map/net/pallas_call | solution.py:674
  272.6 65.8 %net.18 = (bf16[2,4,256,2048]{3,2,1,0:T(8,128)(2,1)}, bf16[2048,2048]{1,0:T(8,128)(2,1)}) custom-call(bf16[2,256,2048]{2,1,0:T(8,128)(2,1)} %bitcast.107, bf16[2048,2048]{1,0:T(8,128)(2,1)} %bitcast.89, bf16[2048,2048]{1,0:T(8,128)(2,1)} %all-gather.14.cloned.1.call-done.refs_2_), custom_call_target="tpu_custom_call" | custom-call | bytes 25165824 | tf_op jit(solution)/shard_map/net/pallas_call | solution.py:674
  338.5 26.5 %fusion = (bf16[2048,2048]{1,0:T(8,128)(2,1)S(1)}, bf16[2048,2048]{1,0:T(8,128)(2,1)}) fusion(bf16[2048,2048]{1,0:T(8,128)(2,1)} %get-tuple-element.64, bf16[2048,2048]{1,0:T(8,128)(2,1)} %bitcast.90, bf16[2048,2048]{1,0:T(8,128)(2,1)} %all-gather.16.cloned.1.call-done.refs_4_), kind=kOutput, calls=%fused_computation.6 | convolution fusion | flops 17217617920 | bytes 41943040 | tf_op jit(solution)/shard_map/dot_general | solution.py:749
  368.3 20.7 %convolution_convert_fusion = bf16[2048,2048]{1,0:T(8,128)(2,1)} fusion(bf16[2048,2048]{1,0:T(8,128)(2,1)S(1)} %get-tuple-element.117.refs_1_, bf16[2048,2048]{1,0:T(8,128)(2,1)S(1)} %bitcast.139), kind=kOutput, calls=%fused_computation.14 | convolution fusion | flops 17184063488 | bytes 25165824 | tf_op jit(solution)/shard_map/dot_general | solution.py:757
  389.1 32.8 %fusion.6 = (bf16[2048,2048]{1,0:T(8,128)(2,1)}, bf16[2048,2048]{1,0:T(8,128)(2,1)}) fusion(bf16[2048,2048]{1,0:T(8,128)(2,1)} %get-tuple-element.64, bf16[2048,2048]{1,0:T(8,128)(2,1)} %get-tuple-element.118, bf16[2048,2048]{1,0:T(8,128)(2,1)} %bitcast.138, bf16[2048,2048]{1,0:T(8,128)(2,1)} %all-gather.18.cloned.1.call-done.refs_2_), kind=kOutput, calls=%fused_computation.12 | convolution fusion | flops 17246978048 | bytes 50331648 | tf_op jit(solution)/shard_map/dot_general | solution.py:753
  421.9 13.9 %fusion.19 = bf16[1024,2048]{1,0:T(8,128)(2,1)} fusion(bf16[2048,2048]{1,0:T(8,128)(2,1)} %all-gather.18.cloned.1.call-done.refs_2_, bf16[2048,2048]{1,0:T(8,128)(2,1)} %copy-done.20), kind=kOutput, calls=%fused_computation.45 | convolution fusion | flops 8592031744 | bytes 16777216 | tf_op jit(solution)/shard_map/dot_general | solution.py:749
  435.8 45.0 %net.19 = (f32[2,128,2048]{2,1,0:T(8,128)}, bf16[1024,2048]{1,0:T(8,128)(2,1)}, bf16[2048,2048]{1,0:T(8,128)(2,1)}) custom-call(bf16[4,2,128,2048]{3,2,1,0:T(8,128)(2,1)} %bitcast.122, bf16[2048,2048]{1,0:T(8,128)(2,1)} %copy-done.20, bf16[2048,2048]{1,0:T(8,128)(2,1)} %all-gather.18.cloned.1.call-done.refs_2_, bf16[2048,2048]{1,0:T(8,128)(2,1)} %bitcast.91, ...), custom_call_target="tpu_custom_call" | custom-call | bytes 12582912 | tf_op jit(solution)/shard_map/net/pallas_call | solution.py:674
  480.9 31.0 %net.20 = (f32[2,128,2048]{2,1,0:T(8,128)}, bf16[1024,2048]{1,0:T(8,128)(2,1)}) custom-call(bf16[4,2,128,2048]{3,2,1,0:T(8,128)(2,1)} %bitcast.119, bf16[2048,2048]{1,0:T(8,128)(2,1)} %get-tuple-element.109.refs_4_.refs_1_, bf16[2048,2048]{1,0:T(8,128)(2,1)} %all-gather.14.cloned.1.call-done.refs_2_, bf16[2048,2048]{1,0:T(8,128)(2,1)} %get-tuple-element.110.refs_3_.refs_2_, ...), custom_call_target="tpu_custom_call" | custom-call | bytes 12582912 | tf_op jit(solution)/shard_map/net/pallas_call | solution.py:674
  512.0 30.0 %net.21 = (f32[2,128,2048]{2,1,0:T(8,128)}, bf16[1024,2048]{1,0:T(8,128)(2,1)}) custom-call(bf16[4,2,128,2048]{3,2,1,0:T(8,128)(2,1)} %bitcast.121, bf16[2048,2048]{1,0:T(8,128)(2,1)} %get-tuple-element.109.refs_4_.refs_1_, bf16[2048,2048]{1,0:T(8,128)(2,1)} %all-gather.14.cloned.1.call-done.refs_2_, bf16[2048,2048]{1,0:T(8,128)(2,1)} %get-tuple-element.110.refs_3_.refs_2_, ...), custom_call_target="tpu_custom_call" | custom-call | bytes 12582912 | tf_op jit(solution)/shard_map/net/pallas_call | solution.py:674
  542.0 30.1 %net.22 = (f32[2,128,2048]{2,1,0:T(8,128)}, bf16[2048,2048]{1,0:T(8,128)(2,1)}) custom-call(bf16[4,2,128,2048]{3,2,1,0:T(8,128)(2,1)} %bitcast.120, bf16[2048,2048]{1,0:T(8,128)(2,1)} %bitcast.92, bf16[2048,2048]{1,0:T(8,128)(2,1)} %get-tuple-element.110.refs_3_.refs_2_), custom_call_target="tpu_custom_call" | custom-call | bytes 12582912 | tf_op jit(solution)/shard_map/net/pallas_call | solution.py:674
  583.8 5.9 convolution_convert_fusion.3
  589.7 25.9 %net.23 = (bf16[2,4,256,512]{3,2,1,0:T(8,128)(2,1)}, bf16[2048,2048]{1,0:T(8,128)(2,1)}) custom-call(bf16[2,256,2048]{2,1,0:T(8,128)(2,1)} %bitcast.128, bf16[512,2048]{1,0:T(8,128)(2,1)} %bitcast.100, bf16[512,2048]{1,0:T(8,128)(2,1)} %copy-done.19), custom_call_target="tpu_custom_call" | custom-call | bytes 12582912 | tf_op jit(solution)/shard_map/net/pallas_call | solution.py:674
  615.7 33.8 %attention_backward.1 = (bf16[2048,512]{1,0:T(8,128)(2,1)S(1)}, bf16[2048,512]{1,0:T(8,128)(2,1)S(1)}, bf16[2048,512]{1,0:T(8,128)(2,1)}, f32[4,8,128]{2,1,0:T(8,128)S(1)}) custom-call(f32[4]{0:T(128)S(1)} %add_divide_fusion.gate, s32[1]{0:T(128)} %bitcast.88.resets, s32[1]{0:T(128)S(6)} %copy.55.depth, ...), custom_call_target="tpu_custom_call" | custom-call | flops 8053063680 | bytes 12582912 | tf_op jit(solution)/shard_map/attention_backward/pallas_call | solution.py:266
  653.9 50.8 %net.24 = (bf16[8,64,2048]{2,1,0:T(8,128)(2,1)}, bf16[2048,1536]{1,0:T(8,128)(2,1)}, bf16[2048,2048]{1,0:T(8,128)(2,1)}) custom-call(bf16[8,4,64,2048]{3,2,1,0:T(8,128)(2,1)} %bitcast.116, bf16[2048,2048]{1,0:T(8,128)(2,1)} %bitcast.94, bf16[2048,1536]{1,0:T(8,128)(2,1)} %pad_maximum_fusion.refs_2_.refs_3_, ...), custom_call_target="tpu_custom_call" | custom-call | bytes 25165824 | tf_op jit(solution)/shard_map/net/pallas_call | solution.py:674
  704.8 98.4 %net.25 = (f32[2,256,2048]{2,1,0:T(8,128)}, bf16[1,64,2048]{2,1,0:T(8,128)(2,1)}, bf16[4,1,256,2048]{3,2,1,0:T(8,128)(2,1)}, bf16[4,1,256,2048]{3,2,1,0:T(8,128)(2,1)}) custom-call(bf16[2,4,256,2048]{3,2,1,0:T(8,128)(2,1)} %bitcast.117, bf16[8,1,64,2048]{3,2,1,0:T(8,128)(2,1)} %bitcast.131, bf16[1,256,2048]{2,1,0:T(8,128)(2,1)} %bitcast.134, ...), custom_call_target="tpu_custom_call" | custom-call | bytes 25165824 | tf_op jit(solution)/shard_map/net/pallas_call | solution.py:674
  803.2 7.3 move_blocks.3
  820.8 16.0 %net.26 = (f32[8,1,8,640]{3,2,1,0:T(8,128)S(1)}, bf16[4,1,64,2048]{3,2,1,0:T(8,128)(2,1)S(1)}) custom-call(f32[1,8,640]{2,1,0:T(8,128)S(1)} %reshape.186.refs_0_, bf16[1,64,2048]{2,1,0:T(8,128)(2,1)S(1)} %copy-done.7), custom_call_target="tpu_custom_call" | custom-call | bytes 3145728 | tf_op jit(solution)/shard_map/net/pallas_call | solution.py:674
  836.8 5.2 net.27
  842.1 8.1 spread_columns.3.refs_0_
  853.0 7.8 bitcast_convert_fusion
  862.3 6.0 fusion.9
  868.3 11.2 %all-gather.20.cloned.1.call-done = bf16[1024,1536]{1,0:T(8,128)(2,1)} async-done(((bf16[256,1536]{1,0:T(8,128)(2,1)}), bf16[1024,1536]{1,0:T(8,128)(2,1)}) %all-gather.20.cloned.1.call-update) | async-done | bytes 3145744 | tf_op jit(solution)/shard_map/all_gather | solution.py:963
  879.5 8.1 spread_columns.5
  887.6 6.5 spread_columns.4
  (164 shorter events, 61.6 us)
Async XLA Ops:
  7.2 5.4 copy-start
  7.2 72.1 %all-gather.12.cloned.1.call-start = ((), (), s32[]{:S(2)}) async-start(), calls=%async_computation.5 | async-start | bytes 2359296 | tf_op jit(solution)/shard_map/all_gather | solution.py:804
  13.3 131.7 %all-gather.10.cloned.1.call-start = ((), (), s32[]{:S(2)}) async-start(), calls=%async_computation.4 | async-start | bytes 7077888 | tf_op jit(solution)/shard_map/all_gather | solution.py:804
  17.5 255.1 %all-gather.14.cloned.1.call-start = ((), (), s32[]{:S(2)}) async-start(), calls=%async_computation.6 | async-start | bytes 9437184 | tf_op jit(solution)/shard_map/all_gather | solution.py:804
  69.3 3.4 copy-start.3
  79.2 259.3 %all-gather.16.cloned.1.call-start = ((), (), s32[]{:S(2)}) async-start(), calls=%async_computation.7 | async-start | bytes 9437184 | tf_op jit(solution)/shard_map/all_gather | solution.py:804
  87.2 53.8 %copy-start.34 = (f32[16]{0:T(128)S(1)}, f32[16]{0:T(128)}, u32[]{:S(2)}) copy-start(f32[16]{0:T(128)} %param.28) | copy-start | bytes 196
  136.8 3.4 copy-start.4
  140.2 248.9 %all-gather.18.cloned.1.call-start = ((), (), s32[]{:S(2)}) async-start(), calls=%async_computation.8 | async-start | bytes 9437184 | tf_op jit(solution)/shard_map/all_gather | solution.py:804
  183.5 432.2 %reduce-scatter.7.cloned.1.call-start = ((), (), s32[]{:S(2)}) async-start(), calls=%async_computation.10 | async-start | bytes 9437184 | tf_op jit(solution)/shard_map/reduce_scatter | solution.py:862
  183.7 25.7 %copy-start.14 = (bf16[1,2,256,2048]{3,2,1,0:T(8,128)(2,1)S(1)}, bf16[1,2,256,2048]{3,2,1,0:T(8,128)(2,1)}, u32[]{:S(2)}) copy-start(bf16[1,2,256,2048]{3,2,1,0:T(8,128)(2,1)} %param.20) | copy-start | bytes 6291460
  209.4 7.9 copy-start.5
  209.5 8.0 copy-start.22
  338.4 29.9 %copy-start.33 = (bf16[2,4,256,2048]{3,2,1,0:T(8,128)(2,1)S(1)}, bf16[2,4,256,2048]{3,2,1,0:T(8,128)(2,1)}, u32[]{:S(2)}) copy-start(bf16[2,4,256,2048]{3,2,1,0:T(8,128)(2,1)} %get-tuple-element.68) | copy-start | bytes 25165828
  389.0 264.8 %reduce-scatter.5.cloned.1.call-start = ((), (), s32[]{:S(2)}) async-start(), calls=%async_computation.9 | async-start | bytes 9437184 | tf_op jit(solution)/shard_map/reduce_scatter | solution.py:862
  480.9 223.9 %reduce-scatter.9.cloned.1.call-start = ((), (), s32[]{:S(2)}) async-start(), calls=%async_computation.11 | async-start | bytes 9437184 | tf_op jit(solution)/shard_map/reduce_scatter | solution.py:862
  572.2 238.4 %reduce-scatter.11.cloned.1.call-start = ((), (), s32[]{:S(2)}) async-start(), calls=%async_computation.12 | async-start | bytes 7077888 | tf_op jit(solution)/shard_map/reduce_scatter | solution.py:862
  577.9 4.4 slice-start
  583.8 5.9 copy-start.19
  704.7 163.6 %all-gather.22.cloned.1.call-start = ((), (), s32[]{:S(2)}) async-start(), calls=%async_computation.14 | async-start | bytes 5242880 | tf_op jit(solution)/shard_map/all_gather | solution.py:962
  810.5 69.0 %all-gather.20.cloned.1.call-start = ((), (), s32[]{:S(2)}) async-start(), calls=%async_computation.13 | async-start | bytes 3932160 | tf_op jit(solution)/shard_map/all_gather | solution.py:963
  811.3 5.2 copy-start.15
  811.3 5.2 copy-start.24
  811.3 5.2 copy-start.28
  816.1 4.6 copy-start.7
  842.1 8.7 copy-start.30
  842.1 18.7 %copy-start.18 = (bf16[1,2,256,2048]{3,2,1,0:T(8,128)(2,1)S(1)}, bf16[1,2,256,2048]{3,2,1,0:T(8,128)(2,1)}, u32[]{:S(2)}) copy-start(bf16[1,2,256,2048]{3,2,1,0:T(8,128)(2,1)} %param.21) | copy-start | bytes 6291460
  851.4 9.4 %copy-start.16 = (bf16[1,2,256,2048]{3,2,1,0:T(8,128)(2,1)S(1)}, bf16[1,2,256,2048]{3,2,1,0:T(8,128)(2,1)}, u32[]{:S(2)}) copy-start(bf16[1,2,256,2048]{3,2,1,0:T(8,128)(2,1)} %param.20) | copy-start | bytes 6291460
  853.0 7.8 copy-start.10
  853.0 7.8 copy-start.12
  853.0 9.3 %copy-start.13 = (f32[512,2048]{1,0:T(8,128)S(1)}, f32[512,2048]{1,0:T(8,128)}, u32[]{:S(2)}) copy-start(f32[512,2048]{1,0:T(8,128)} %move_blocks.3) | copy-start | bytes 12582916
  879.5 14.6 %copy-start.1 = (bf16[256,2048]{1,0:T(8,128)(2,1)S(1)}, bf16[256,2048]{1,0:T(8,128)(2,1)}, u32[]{:S(2)}) copy-start(bf16[256,2048]{1,0:T(8,128)(2,1)} %param.23) | copy-start | bytes 3145732
  (16 other events, 34.5 us)
Sparse Core Ops, SparseCore 0:
  13.4 36.1 all-gather.11
  51.7 66.5 all-gather.9
  120.4 87.2 all-gather.13
  209.1 87.2 all-gather.15
  298.3 87.2 all-gather.17
  389.2 88.9 reduce-scatter.6
  481.0 89.3 reduce-scatter.4
  572.7 88.4 reduce-scatter.8
  704.8 88.7 reduce-scatter.10
  810.7 38.6 all-gather.21
  850.9 28.5 all-gather.19

commit v8 on v7

--- a/solution.py
+++ b/solution.py
@@ -871,7 +871,7 @@
         grad_gate, grad_up = grad_gate.astype(bf16), grad_up.astype(bf16)
 
         def output_terms(s):
-            return Product([(hidden, w_d)], (1, 0), (512, 512), (s * seg, seg))
+            return Product([(hidden, w_d)], (1, 0), (1024, 512), (s * seg, seg))
 
         def h_two_terms(s):
             pairs = [(grad_gate, w_g), (grad_up, w_u)]

time: 909 us -> 906 us (level)
  transfers between devices with their start and end apart: 11 -> 11, of which waited for: 1 -> 1; matrix products, arithmetic and copies ran while one was open for 18% -> 19% of each run, Pallas kernels for 73% -> 73%
where the time goes in v8:
time: 906 us; the launch traced here: 899 us
  Pallas kernels  672 us (74%)
  matrix products  126 us (14%)
  other arithmetic  37.9 us (4%)
  local copies, waits for them, and re-layouts  32.4 us (4%)
  between operations  16.5 us (2%)
  waiting for transfers between devices  12.6 us (1%)
    pallas_call x14, Pallas kernels, run(): pl.pallas_call(kernel, in_specs=[anywhere] * len(ins), out_specs=[anywher...  572 us
    dot_general x4, matrix products, mm(): return jnp.dot(left, right, preferred_element_type=f32)  67 us
    dot_general x2, matrix products, mm_nt(): lax.dot_general(left, right, (((1,), (1,)), ((), ())), preferred_element_...  38.7 us
    pallas_call x1, Pallas kernels, attention_backward(): pl.pallas_call(functools.partial(backward_kernel, min(256, seg), segs), g...  33.8 us
    unnamed x96, local copies, waits for them, and re-layouts  25.5 us
    pallas_call x3, Pallas kernels, spread_columns(): pl.pallas_call(kernel, grid_spec=pltpu.PrefetchScalarGridSpec(num_scalar_...  22.7 us
    dot_general x1, matrix products, mm_tn(): lax.dot_general(left, right, (((0,), (0,)), ((), ())), preferred_element_...  20.7 us
    pallas_call x1, Pallas kernels, attention_forward(): pl.pallas_call(functools.partial(forward_kernel, min(256, seg), segs), gr...  19.8 us
  transfers between devices with their start and end apart: 11, of which 1 were waited for; matrix products, arithmetic and copies ran while one was open for 19% of the time, Pallas kernels for 73%

profile of v8, /device:TPU:0, one launch (start us, length us, event | category | flops | bytes accessed | tf_op | source)
XLA Modules:
  0.0 898.5 jit_solution(10858000831596126771)
XLA Ops:
  17.5 51.7 %net.14 = bf16[2,4,256,2048]{3,2,1,0:T(8,128)(2,1)S(1)} custom-call(bf16[2,256,2048]{2,1,0:T(8,128)(2,1)S(1)} %bitcast.102), custom_call_target="tpu_custom_call" | custom-call | bytes 25165824 | tf_op jit(solution)/shard_map/net/pallas_call | solution.py:674
  72.7 6.5 own_columns.3
  79.3 6.3 move_blocks.2
  87.2 49.6 %net.16 = bf16[8,4,64,2048]{3,2,1,0:T(8,128)(2,1)S(1)} custom-call(bf16[8,64,2048]{2,1,0:T(8,128)(2,1)S(1)} %bitcast.101), custom_call_target="tpu_custom_call" | custom-call | bytes 25165824 | tf_op jit(solution)/shard_map/net/pallas_call | solution.py:674
  145.0 18.6 %convolution_convert_fusion.2.q_ref.k_ref.v_ref = bf16[2048,1536]{1,0:T(8,128)(2,1)} fusion(bf16[2048,2048]{1,0:T(8,128)(2,1)} %bitcast.93, bf16[2048,1536]{1,0:T(8,128)(2,1)} %all-gather.10.cloned.1.call-done.refs_4_), kind=kOutput, calls=%fused_computation.16 | convolution fusion | flops 12888047616 | bytes 20971520 | tf_op jit(solution)/shard_map/dot_general | solution.py:749
  163.7 19.8 %attention_forward.1 = (bf16[2048,512]{1,0:T(8,128)(2,1)S(1)}, f32[4,2,1,1024]{3,2,1,0:T(1,128)S(1)}, f32[4,2,128,128]{3,2,1,0:T(8,128)S(1)}, f32[4,2,1,128]{3,2,1,0:T(1,128)S(1)}) custom-call(f32[4]{0:T(128)S(1)} %add_divide_fusion.gate, s32[1]{0:T(128)} %bitcast.87.resets, bf16[2048,1536]{1,0:T(8,128)(2,1)} %convolution_convert_fusion.2.q_ref.k_ref.v_ref, ...), custom_call_target="tpu_custom_call" | custom-call | flops 4026531840 | bytes 12582912 | tf_op jit(solution)/shard_map/attention_forward/pallas_call | solution.py:133
  183.8 25.7 %net.15 = bf16[2,256,2048]{2,1,0:T(8,128)(2,1)S(1)} custom-call(bf16[2,4,256,512]{3,2,1,0:T(8,128)(2,1)S(1)} %bitcast.104), custom_call_target="tpu_custom_call" | custom-call | bytes 12582912 | tf_op jit(solution)/shard_map/net/pallas_call | solution.py:674
  209.5 7.9 multiply_reduce_fusion.2
  219.6 49.8 %net.17 = bf16[2,4,256,2048]{3,2,1,0:T(8,128)(2,1)S(1)} custom-call(bf16[2,256,2048]{2,1,0:T(8,128)(2,1)S(1)} %bitcast.103), custom_call_target="tpu_custom_call" | custom-call | bytes 25165824 | tf_op jit(solution)/shard_map/net/pallas_call | solution.py:674
  272.6 65.8 %net.18 = (bf16[2,4,256,2048]{3,2,1,0:T(8,128)(2,1)}, bf16[2048,2048]{1,0:T(8,128)(2,1)}) custom-call(bf16[2,256,2048]{2,1,0:T(8,128)(2,1)} %bitcast.107, bf16[2048,2048]{1,0:T(8,128)(2,1)} %bitcast.89, bf16[2048,2048]{1,0:T(8,128)(2,1)} %all-gather.14.cloned.1.call-done.refs_2_), custom_call_target="tpu_custom_call" | custom-call | bytes 25165824 | tf_op jit(solution)/shard_map/net/pallas_call | solution.py:674
  338.5 26.5 %fusion = (bf16[2048,2048]{1,0:T(8,128)(2,1)S(1)}, bf16[2048,2048]{1,0:T(8,128)(2,1)}) fusion(bf16[2048,2048]{1,0:T(8,128)(2,1)} %get-tuple-element.64, bf16[2048,2048]{1,0:T(8,128)(2,1)} %bitcast.90, bf16[2048,2048]{1,0:T(8,128)(2,1)} %all-gather.16.cloned.1.call-done.refs_4_), kind=kOutput, calls=%fused_computation.6 | convolution fusion | flops 17217617920 | bytes 41943040 | tf_op jit(solution)/shard_map/dot_general | solution.py:749
  368.3 20.7 %convolution_convert_fusion = bf16[2048,2048]{1,0:T(8,128)(2,1)} fusion(bf16[2048,2048]{1,0:T(8,128)(2,1)S(1)} %get-tuple-element.117.refs_1_, bf16[2048,2048]{1,0:T(8,128)(2,1)S(1)} %bitcast.139), kind=kOutput, calls=%fused_computation.14 | convolution fusion | flops 17184063488 | bytes 25165824 | tf_op jit(solution)/shard_map/dot_general | solution.py:757
  389.1 32.8 %fusion.6 = (bf16[2048,2048]{1,0:T(8,128)(2,1)}, bf16[2048,2048]{1,0:T(8,128)(2,1)}) fusion(bf16[2048,2048]{1,0:T(8,128)(2,1)} %get-tuple-element.64, bf16[2048,2048]{1,0:T(8,128)(2,1)} %get-tuple-element.118, bf16[2048,2048]{1,0:T(8,128)(2,1)} %bitcast.138, bf16[2048,2048]{1,0:T(8,128)(2,1)} %all-gather.18.cloned.1.call-done.refs_2_), kind=kOutput, calls=%fused_computation.12 | convolution fusion | flops 17246978048 | bytes 50331648 | tf_op jit(solution)/shard_map/dot_general | solution.py:753
  421.9 13.9 %fusion.19 = bf16[1024,2048]{1,0:T(8,128)(2,1)} fusion(bf16[2048,2048]{1,0:T(8,128)(2,1)} %all-gather.18.cloned.1.call-done.refs_2_, bf16[2048,2048]{1,0:T(8,128)(2,1)} %copy-done.20), kind=kOutput, calls=%fused_computation.45 | convolution fusion | flops 8592031744 | bytes 16777216 | tf_op jit(solution)/shard_map/dot_general | solution.py:749
  435.8 42.5 %net.19 = (f32[2,128,2048]{2,1,0:T(8,128)}, bf16[1024,2048]{1,0:T(8,128)(2,1)}, bf16[2048,2048]{1,0:T(8,128)(2,1)}) custom-call(bf16[4,2,128,2048]{3,2,1,0:T(8,128)(2,1)} %bitcast.122, bf16[2048,2048]{1,0:T(8,128)(2,1)} %copy-done.20, bf16[2048,2048]{1,0:T(8,128)(2,1)} %all-gather.18.cloned.1.call-done.refs_2_, bf16[2048,2048]{1,0:T(8,128)(2,1)} %bitcast.91, ...), custom_call_target="tpu_custom_call" | custom-call | bytes 12582912 | tf_op jit(solution)/shard_map/net/pallas_call | solution.py:674
  478.4 30.8 %net.20 = (f32[2,128,2048]{2,1,0:T(8,128)}, bf16[1024,2048]{1,0:T(8,128)(2,1)}) custom-call(bf16[4,2,128,2048]{3,2,1,0:T(8,128)(2,1)} %bitcast.119, bf16[2048,2048]{1,0:T(8,128)(2,1)} %get-tuple-element.109.refs_4_.refs_1_, bf16[2048,2048]{1,0:T(8,128)(2,1)} %all-gather.14.cloned.1.call-done.refs_2_, bf16[2048,2048]{1,0:T(8,128)(2,1)} %get-tuple-element.110.refs_3_.refs_2_, ...), custom_call_target="tpu_custom_call" | custom-call | bytes 12582912 | tf_op jit(solution)/shard_map/net/pallas_call | solution.py:674
  509.2 30.3 %net.21 = (f32[2,128,2048]{2,1,0:T(8,128)}, bf16[1024,2048]{1,0:T(8,128)(2,1)}) custom-call(bf16[4,2,128,2048]{3,2,1,0:T(8,128)(2,1)} %bitcast.121, bf16[2048,2048]{1,0:T(8,128)(2,1)} %get-tuple-element.109.refs_4_.refs_1_, bf16[2048,2048]{1,0:T(8,128)(2,1)} %all-gather.14.cloned.1.call-done.refs_2_, bf16[2048,2048]{1,0:T(8,128)(2,1)} %get-tuple-element.110.refs_3_.refs_2_, ...), custom_call_target="tpu_custom_call" | custom-call | bytes 12582912 | tf_op jit(solution)/shard_map/net/pallas_call | solution.py:674
  539.5 29.8 %net.22 = (f32[2,128,2048]{2,1,0:T(8,128)}, bf16[2048,2048]{1,0:T(8,128)(2,1)}) custom-call(bf16[4,2,128,2048]{3,2,1,0:T(8,128)(2,1)} %bitcast.120, bf16[2048,2048]{1,0:T(8,128)(2,1)} %bitcast.92, bf16[2048,2048]{1,0:T(8,128)(2,1)} %get-tuple-element.110.refs_3_.refs_2_), custom_call_target="tpu_custom_call" | custom-call | bytes 12582912 | tf_op jit(solution)/shard_map/net/pallas_call | solution.py:674
  581.1 5.9 convolution_convert_fusion.3
  587.0 25.9 %net.23 = (bf16[2,4,256,512]{3,2,1,0:T(8,128)(2,1)}, bf16[2048,2048]{1,0:T(8,128)(2,1)}) custom-call(bf16[2,256,2048]{2,1,0:T(8,128)(2,1)} %bitcast.128, bf16[512,2048]{1,0:T(8,128)(2,1)} %bitcast.100, bf16[512,2048]{1,0:T(8,128)(2,1)} %copy-done.19), custom_call_target="tpu_custom_call" | custom-call | bytes 12582912 | tf_op jit(solution)/shard_map/net/pallas_call | solution.py:674
  612.9 33.8 %attention_backward.1 = (bf16[2048,512]{1,0:T(8,128)(2,1)S(1)}, bf16[2048,512]{1,0:T(8,128)(2,1)S(1)}, bf16[2048,512]{1,0:T(8,128)(2,1)}, f32[4,8,128]{2,1,0:T(8,128)S(1)}) custom-call(f32[4]{0:T(128)S(1)} %add_divide_fusion.gate, s32[1]{0:T(128)} %bitcast.88.resets, s32[1]{0:T(128)S(6)} %copy.55.depth, ...), custom_call_target="tpu_custom_call" | custom-call | flops 8053063680 | bytes 12582912 | tf_op jit(solution)/shard_map/attention_backward/pallas_call | solution.py:266
  651.1 51.0 %net.24 = (bf16[8,64,2048]{2,1,0:T(8,128)(2,1)}, bf16[2048,1536]{1,0:T(8,128)(2,1)}, bf16[2048,2048]{1,0:T(8,128)(2,1)}) custom-call(bf16[8,4,64,2048]{3,2,1,0:T(8,128)(2,1)} %bitcast.116, bf16[2048,2048]{1,0:T(8,128)(2,1)} %bitcast.94, bf16[2048,1536]{1,0:T(8,128)(2,1)} %pad_maximum_fusion.refs_2_.refs_3_, ...), custom_call_target="tpu_custom_call" | custom-call | bytes 25165824 | tf_op jit(solution)/shard_map/net/pallas_call | solution.py:674
  702.2 98.6 %net.25 = (f32[2,256,2048]{2,1,0:T(8,128)}, bf16[1,64,2048]{2,1,0:T(8,128)(2,1)}, bf16[4,1,256,2048]{3,2,1,0:T(8,128)(2,1)}, bf16[4,1,256,2048]{3,2,1,0:T(8,128)(2,1)}) custom-call(bf16[2,4,256,2048]{3,2,1,0:T(8,128)(2,1)} %bitcast.117, bf16[8,1,64,2048]{3,2,1,0:T(8,128)(2,1)} %bitcast.131, bf16[1,256,2048]{2,1,0:T(8,128)(2,1)} %bitcast.134, ...), custom_call_target="tpu_custom_call" | custom-call | bytes 25165824 | tf_op jit(solution)/shard_map/net/pallas_call | solution.py:674
  800.8 7.3 move_blocks.3
  818.3 15.6 %net.26 = (f32[8,1,8,640]{3,2,1,0:T(8,128)S(1)}, bf16[4,1,64,2048]{3,2,1,0:T(8,128)(2,1)S(1)}) custom-call(f32[1,8,640]{2,1,0:T(8,128)S(1)} %reshape.186.refs_0_, bf16[1,64,2048]{2,1,0:T(8,128)(2,1)S(1)} %copy-done.7), custom_call_target="tpu_custom_call" | custom-call | bytes 3145728 | tf_op jit(solution)/shard_map/net/pallas_call | solution.py:674
  834.0 5.2 net.27
  839.2 8.1 spread_columns.3.refs_0_
  850.1 7.8 bitcast_convert_fusion
  859.3 6.0 fusion.9
  865.4 11.6 %all-gather.20.cloned.1.call-done = bf16[1024,1536]{1,0:T(8,128)(2,1)} async-done(((bf16[256,1536]{1,0:T(8,128)(2,1)}), bf16[1024,1536]{1,0:T(8,128)(2,1)}) %all-gather.20.cloned.1.call-update) | async-done | bytes 3145744 | tf_op jit(solution)/shard_map/all_gather | solution.py:963
  877.0 8.1 spread_columns.5
  885.1 6.5 spread_columns.4
  (164 shorter events, 61.6 us)
Async XLA Ops:
  7.2 5.4 copy-start
  7.2 72.1 %all-gather.12.cloned.1.call-start = ((), (), s32[]{:S(2)}) async-start(), calls=%async_computation.5 | async-start | bytes 2359296 | tf_op jit(solution)/shard_map/all_gather | solution.py:804
  13.3 131.7 %all-gather.10.cloned.1.call-start = ((), (), s32[]{:S(2)}) async-start(), calls=%async_computation.4 | async-start | bytes 7077888 | tf_op jit(solution)/shard_map/all_gather | solution.py:804
  17.5 255.1 %all-gather.14.cloned.1.call-start = ((), (), s32[]{:S(2)}) async-start(), calls=%async_computation.6 | async-start | bytes 9437184 | tf_op jit(solution)/shard_map/all_gather | solution.py:804
  69.3 3.4 copy-start.3
  79.2 259.3 %all-gather.16.cloned.1.call-start = ((), (), s32[]{:S(2)}) async-start(), calls=%async_computation.7 | async-start | bytes 9437184 | tf_op jit(solution)/shard_map/all_gather | solution.py:804
  87.2 53.8 %copy-start.34 = (f32[16]{0:T(128)S(1)}, f32[16]{0:T(128)}, u32[]{:S(2)}) copy-start(f32[16]{0:T(128)} %param.28) | copy-start | bytes 196
  136.8 3.4 copy-start.4
  140.2 248.9 %all-gather.18.cloned.1.call-start = ((), (), s32[]{:S(2)}) async-start(), calls=%async_computation.8 | async-start | bytes 9437184 | tf_op jit(solution)/shard_map/all_gather | solution.py:804
  183.5 429.4 %reduce-scatter.7.cloned.1.call-start = ((), (), s32[]{:S(2)}) async-start(), calls=%async_computation.10 | async-start | bytes 9437184 | tf_op jit(solution)/shard_map/reduce_scatter | solution.py:862
  183.7 25.7 %copy-start.14 = (bf16[1,2,256,2048]{3,2,1,0:T(8,128)(2,1)S(1)}, bf16[1,2,256,2048]{3,2,1,0:T(8,128)(2,1)}, u32[]{:S(2)}) copy-start(bf16[1,2,256,2048]{3,2,1,0:T(8,128)(2,1)} %param.20) | copy-start | bytes 6291460
  209.4 7.9 copy-start.5
  209.5 8.0 copy-start.22
  338.4 29.9 %copy-start.33 = (bf16[2,4,256,2048]{3,2,1,0:T(8,128)(2,1)S(1)}, bf16[2,4,256,2048]{3,2,1,0:T(8,128)(2,1)}, u32[]{:S(2)}) copy-start(bf16[2,4,256,2048]{3,2,1,0:T(8,128)(2,1)} %get-tuple-element.68) | copy-start | bytes 25165828
  389.0 262.0 %reduce-scatter.5.cloned.1.call-start = ((), (), s32[]{:S(2)}) async-start(), calls=%async_computation.9 | async-start | bytes 9437184 | tf_op jit(solution)/shard_map/reduce_scatter | solution.py:862
  478.4 223.8 %reduce-scatter.9.cloned.1.call-start = ((), (), s32[]{:S(2)}) async-start(), calls=%async_computation.11 | async-start | bytes 9437184 | tf_op jit(solution)/shard_map/reduce_scatter | solution.py:862
  569.3 238.8 %reduce-scatter.11.cloned.1.call-start = ((), (), s32[]{:S(2)}) async-start(), calls=%async_computation.12 | async-start | bytes 7077888 | tf_op jit(solution)/shard_map/reduce_scatter | solution.py:862
  575.1 4.5 slice-start
  581.1 5.9 copy-start.19
  702.1 163.2 %all-gather.22.cloned.1.call-start = ((), (), s32[]{:S(2)}) async-start(), calls=%async_computation.14 | async-start | bytes 5242880 | tf_op jit(solution)/shard_map/all_gather | solution.py:962
  808.1 68.9 %all-gather.20.cloned.1.call-start = ((), (), s32[]{:S(2)}) async-start(), calls=%async_computation.13 | async-start | bytes 3932160 | tf_op jit(solution)/shard_map/all_gather | solution.py:963
  808.8 5.2 copy-start.15
  808.8 5.2 copy-start.24
  808.8 5.2 copy-start.28
  813.7 4.6 copy-start.7
  839.2 8.6 copy-start.30
  839.2 18.7 %copy-start.18 = (bf16[1,2,256,2048]{3,2,1,0:T(8,128)(2,1)S(1)}, bf16[1,2,256,2048]{3,2,1,0:T(8,128)(2,1)}, u32[]{:S(2)}) copy-start(bf16[1,2,256,2048]{3,2,1,0:T(8,128)(2,1)} %param.21) | copy-start | bytes 6291460
  848.5 9.4 %copy-start.16 = (bf16[1,2,256,2048]{3,2,1,0:T(8,128)(2,1)S(1)}, bf16[1,2,256,2048]{3,2,1,0:T(8,128)(2,1)}, u32[]{:S(2)}) copy-start(bf16[1,2,256,2048]{3,2,1,0:T(8,128)(2,1)} %param.20) | copy-start | bytes 6291460
  850.1 7.8 copy-start.10
  850.1 7.8 copy-start.12
  850.1 9.2 %copy-start.13 = (f32[512,2048]{1,0:T(8,128)S(1)}, f32[512,2048]{1,0:T(8,128)}, u32[]{:S(2)}) copy-start(f32[512,2048]{1,0:T(8,128)} %move_blocks.3) | copy-start | bytes 12582916
  877.0 14.6 %copy-start.1 = (bf16[256,2048]{1,0:T(8,128)(2,1)S(1)}, bf16[256,2048]{1,0:T(8,128)(2,1)}, u32[]{:S(2)}) copy-start(bf16[256,2048]{1,0:T(8,128)(2,1)} %param.23) | copy-start | bytes 3145732
  (16 other events, 34.6 us)
Sparse Core Ops, SparseCore 0:
  13.4 36.1 all-gather.11
  51.7 66.5 all-gather.9
  120.4 87.2 all-gather.13
  209.1 87.2 all-gather.15
  298.3 87.2 all-gather.17
  389.2 88.9 reduce-scatter.6
  480.5 88.1 reduce-scatter.4
  571.0 88.1 reduce-scatter.8
  702.2 88.5 reduce-scatter.10
  808.2 38.6 all-gather.21
  848.4 28.5 all-gather.19
